TPU v7x, 128 devices: a whole 4x4x4 slice. The times are simulated.
128 devices in a mesh: pipe: 2 (over z_hi), dp: 16 (over z_lo, y, core), tensor: 4 (over x).
Axes of the slice: x: 4, y: 4, z: 4 (z_hi: 2, z_lo: 2; z = z_hi * 2 + z_lo), core: 2. Of those that a mesh axis runs over, the one named last changes fastest.
Arguments:
- inputs: bfloat16 [2, 4096, 1024], P(None, ('dp', 'tensor')), may hold values from -6 to 6
- cotangent: bfloat16 [2, 4096, 1024], P(None, ('dp', 'tensor')), may hold values from -16 to 16
- doc_lengths: int32 [2, 16, 4], P(None, 'dp'), may hold values from 1 to 256, as said below
- routes: int32 [2, 2, 4096, 8], P('pipe', None, 'dp'), may hold values from 0 to 15, all different within a row; in each aligned block of 256 rows (0 to 255, 256 to 511, ..., all dimensions but the last counted through in order) at most 160 rows name the same one
- norm_attn: bfloat16 [2, 1024], P('pipe', ('dp', 'tensor')), may hold values from 0.5 to 1.5
- w_query: bfloat16 [2, 1024, 1024], P('pipe', 'dp', 'tensor'), may hold values from -0.1875 to 0.1875
- w_key: bfloat16 [2, 1024, 512], P('pipe', 'dp', 'tensor'), may hold values from -0.1875 to 0.1875
- w_value: bfloat16 [2, 1024, 512], P('pipe', 'dp', 'tensor'), may hold values from -0.1875 to 0.1875
- w_out: bfloat16 [2, 1024, 1024], P('pipe', 'tensor', 'dp'), may hold values from -0.75 to 0.75
- w_router: bfloat16 [2, 1024, 16], P('pipe', ('dp', 'tensor')), may hold values from -0.09375 to 0.09375
- norm_ffn: bfloat16 [2, 1024], P('pipe', ('dp', 'tensor')), may hold values from 0.5 to 1.5
- w_gate: bfloat16 [2, 16, 1024, 512], P('pipe', None, 'dp', 'tensor'), may hold values from -0.1875 to 0.1875
- w_up: bfloat16 [2, 16, 1024, 512], P('pipe', None, 'dp', 'tensor'), may hold values from -0.1875 to 0.1875
- w_down: bfloat16 [2, 16, 512, 1024], P('pipe', None, 'tensor', 'dp'), may hold values from -0.75 to 0.75
Outputs:
- section_out: bfloat16 [2, 2, 4096, 1024], P('pipe', None, ('dp', 'tensor'))
- input_grad: float32 [2, 2, 4096, 1024], P('pipe', None, ('dp', 'tensor'))
- grad_norm_attn: float32 [2, 1024], P('pipe', ('dp', 'tensor'))
- grad_query: float32 [2, 1024, 1024], P('pipe', 'dp', 'tensor')
- grad_key: float32 [2, 1024, 512], P('pipe', 'dp', 'tensor')
- grad_value: float32 [2, 1024, 512], P('pipe', 'dp', 'tensor')
- grad_out: float32 [2, 1024, 1024], P('pipe', 'tensor', 'dp')
- grad_router: float32 [2, 1024, 16], P('pipe', ('dp', 'tensor'))
- grad_norm_ffn: float32 [2, 1024], P('pipe', ('dp', 'tensor'))
- grad_gate: float32 [2, 16, 1024, 512], P('pipe', None, 'dp', 'tensor')
- grad_up: float32 [2, 16, 1024, 512], P('pipe', None, 'dp', 'tensor')
- grad_down: float32 [2, 16, 512, 1024], P('pipe', None, 'tensor', 'dp')
Inputs may be any that keep to these rules, and one draw needn't show every extreme that they name: `doc_lengths`: each row holds 4 lengths that sum to 256; one of these documents, at a place drawn from the seed, holds tokens of every index of tensor. `routes`: in each block of 256 consecutive rows (one section, one micro-batch, one pack) no expert is named more than 160 times, and in some blocks one expert is named exactly 160 times.
All inputs are finite; a program needn't handle non-finite values.
Results may differ from a plain program's by a relative error of at most 0.035.
Values may be sent and summed in bfloat16 or wider, within the bound.
No kernel may reach another device: no remote copies, remote signals or barrier semaphores. Data moves between devices by JAX's collectives and lax.ppermute only.
A program may use at most 192 MiB of HBM per device.

v0:
```python
import math

import jax
import jax.numpy as jnp
from jax import lax
from jax.experimental import pallas as pl
from jax.experimental.pallas import tpu as pltpu
from jax.sharding import PartitionSpec as P

HD = 64
E = 16
TOP = 8
EPSILON = 1e-06
MASKED = -1000000000.0
BF = jnp.bfloat16
F32 = jnp.float32
VMEM_LIMIT = 56 * 1024 * 1024
PER = 8
PER_GRAD = 4
LANES = 128


def params():
    return pltpu.CompilerParams(
        vmem_limit_bytes=VMEM_LIMIT, dimension_semantics=("arbitrary",)
    )


def dot(left, right):
    return jnp.dot(left, right, preferred_element_type=F32)


def dot_nt(left, right):
    return lax.dot_general(
        left, right, (((1,), (1,)), ((), ())), preferred_element_type=F32
    )


def dot_tn(left, right):
    return lax.dot_general(
        left, right, (((0,), (0,)), ((), ())), preferred_element_type=F32
    )


def column(rows, index):
    lanes = lax.broadcasted_iota(jnp.int32, rows.shape, 1)
    return jnp.sum(jnp.where(lanes == index, rows, 0.0), axis=1, keepdims=True)


def whole(shape):
    return pl.BlockSpec(shape, lambda i, s: (0,) * len(shape))


def rms_scale(values):
    return lax.rsqrt(jnp.mean(values * values, axis=-1, keepdims=True) + EPSILON)


def norm_back(values, scale_rows, gain, grad_normed):
    weighted = grad_normed * gain
    grad_values = scale_rows * weighted - values * scale_rows**3 * jnp.mean(
        weighted * values, axis=-1, keepdims=True
    )
    grad_gain = jnp.sum(grad_normed * values * scale_rows, axis=0, keepdims=True)
    return grad_values, grad_gain


def swap_halves(values):
    width = values.shape[1]
    lanes = lax.broadcasted_iota(jnp.int32, values.shape, 1)
    ahead = pltpu.roll(values, width - HD // 2, 1)
    behind = pltpu.roll(values, HD // 2, 1)
    return jnp.where(lanes % HD < HD // 2, ahead, behind)


def assemble(me, pieces, target):
    rows = pieces[0].shape[0]
    for shift in range(4):
        owner = lax.rem(me + 4 - shift, 4)
        target[own_rows(owner, rows), :] = pieces[shift][...]


def own_rows(me, rows):
    return pl.ds(pl.multiple_of(me * rows, rows), rows)


def anywhere(count):
    return [pl.BlockSpec(memory_space=pl.ANY)] * count


def fetches(core, sources, buffers, sems):
    dp = buffers.shape[1]
    half, quarter = dp // 2, dp // 4
    here, there = core * half, (1 - core) * half
    copies = [[pltpu.make_async_copy(sources[0], buffers.at[0], sems.at[0])]]
    number = 1
    for shift, starts in (
        (1, (here, there)),
        (2, (here, here + quarter, there, there + quarter)),
        (3, (here, there)),
    ):
        group = []
        for start in starts:
            source = sources[number]
            place = buffers.at[shift, pl.ds(start, source.shape[0])]
            group.append(pltpu.make_async_copy(source, place, sems.at[number]))
            number += 1
        copies.append(group)
    return copies


def group_weights(buffers, step):
    dp = buffers.shape[1]
    blocks = [
        buffers[step, :, 64 * j : 64 * (j + 1), :].reshape(dp * 64, LANES) for j in range(6)
    ]
    return jnp.concatenate(blocks[:4], axis=1), jnp.concatenate(blocks[4:], axis=1)


def smalls_kernel(sref, *refs):
    sources, (router_ref, gains_ref, stage, sems) = refs[:9], refs[9:]
    dp = stage.shape[0]
    half, quarter = dp // 2, dp // 4
    me = sref[0]
    here, there = sref[2] * half, (1 - sref[2]) * half
    places = (
        (0, 0), (1, here), (1, there),
        (2, here), (2, here + quarter), (2, there), (2, there + quarter), (3, here), (3, there),
    )
    copies = []
    for number, (shift, start) in enumerate(places):
        source = sources[number]
        owner = lax.rem(me + 4 - shift, 4)
        copies.append(
            pltpu.make_async_copy(
                source.at[:, pl.ds(384, 16)],
                stage.at[pl.ds(start, source.shape[0]), owner],
                sems.at[number],
            )
        )
    for copy in copies:
        copy.start()
    for copy in copies:
        copy.wait()
    rows = stage[...].reshape(dp * 64, LANES)
    router_ref[...] = rows
    turned = rows.astype(F32).T
    gains_ref[...] = turned[E : E + 8, :]


def smalls_of(scalars, w_attn):
    dp = w_attn[0].shape[0]
    width = dp * 64
    return pl.pallas_call(
        smalls_kernel,
        grid_spec=pltpu.PrefetchScalarGridSpec(
            num_scalar_prefetch=1,
            grid=(1,),
            in_specs=anywhere(9),
            out_specs=[whole((width, LANES)), whole((8, width))],
            scratch_shapes=[pltpu.VMEM((dp, 4, 16, LANES), BF), pltpu.SemaphoreType.DMA((9,))],
        ),
        out_shape=[
            jax.ShapeDtypeStruct((width, LANES), BF),
            jax.ShapeDtypeStruct((8, width), F32),
        ],
        compiler_params=params(),
        name="router_and_gains",
    )(scalars, *w_attn)


def attention_forward_kernel(n_after, sref, *refs):
    pieces, refs = refs[:4], refs[4:]
    sources, refs = refs[:9], refs[9 + n_after :]
    (
        gains_ref, cos_ref, sin_ref, bias_ref, picked_ref, router_ref,
        a_ref, xown_ref, qkv_ref, o_ref, lse_ref, hown_ref, b_ref, gates_ref,
        hidden, buffers, sems,
    ) = refs
    me = sref[0]
    group, width = b_ref.shape
    shard = xown_ref.shape[0]

    @pl.when(sref[1] > 0)
    def _():
        copies = fetches(sref[2], sources, buffers, sems)
        for copy in copies[0]:
            copy.start()
        assemble(me, pieces, b_ref)
        entering = b_ref[...].astype(F32)
        a_ref[...] = (entering * rms_scale(entering) * gains_ref[0:1, :]).astype(BF)
        xown_ref[...] = pieces[0][...]
        hidden[...] = entering
        cos = jnp.concatenate([cos_ref[...]] * 3, axis=1)
        sin = jnp.concatenate([sin_ref[...]] * 3, axis=1)
        bias = bias_ref[...]
        lanes = lax.broadcasted_iota(jnp.int32, (group, LANES), 1)
        lse_all = jnp.zeros((group, LANES), F32)
        for step in range(4):
            for copy in copies[step]:
                copy.wait()
            for copy in copies[step + 1] if step < 3 else []:
                copy.start()
            w_qkv, w_out = group_weights(buffers, step)
            qkv = dot(a_ref[...], w_qkv)
            qk = qkv[:, :384]
            turned = qk * cos + swap_halves(qk) * sin
            q = (turned[:, :256] * HD**-0.5).astype(BF)
            k = turned[:, 256:].astype(BF)
            v = qkv[:, 384:].astype(BF)
            qkv_ref[step, :, :256] = q
            qkv_ref[step, :, 256:384] = k
            qkv_ref[step, :, 384:] = v
            outs = []
            for head in range(4):
                kv = head // 2
                scores = dot_nt(
                    q[:, head * HD : (head + 1) * HD], k[:, kv * HD : (kv + 1) * HD]
                )
                scores = scores + bias
                peak = jnp.max(scores, axis=1, keepdims=True)
                soft = jnp.exp(scores - peak)
                total = jnp.sum(soft, axis=1, keepdims=True)
                lse_all = jnp.where(lanes == 4 * step + head, peak + jnp.log(total), lse_all)
                soft = (soft * (1.0 / total)).astype(BF)
                outs.append(dot(soft, v[:, kv * HD : (kv + 1) * HD]))
            mixed = jnp.concatenate(outs, axis=1).astype(BF)
            if step == 0:
                o_ref[...] = mixed
            hidden[...] += dot_nt(mixed, w_out)
        lse_ref[...] = lse_all
        rows = hidden[...]
        normed = (rows * rms_scale(rows) * gains_ref[1:2, :]).astype(BF)
        b_ref[...] = normed
        hown_ref[...] = hidden[own_rows(me, shard), :]
        logits = dot(normed, router_ref[...])[:, :E]
        picked = picked_ref[...]
        peak = jnp.max(jnp.where(picked > 0, logits, -1e30), axis=1, keepdims=True)
        powers = jnp.where(picked > 0, jnp.exp(jnp.minimum(logits - peak, 0.0)), 0.0)
        gates_ref[...] = powers / jnp.sum(powers, axis=1, keepdims=True)


def attention_forward(scalars, pieces, gains, tables, picked, w_attn, router, after):
    shard, width = pieces[0].shape
    group = 4 * shard
    dp = width // 64
    cos, sin, bias = tables
    smalls = [gains, cos, sin, bias, picked, router]
    per_step = lambda i, s: (i * s[1], 0, 0)
    outs = [
        ((group, width), BF, None),
        ((shard, width), BF, None),
        ((4, group, 512), BF, None),
        ((group, 256), BF, None),
        ((group, LANES), F32, None),
        ((shard, width), F32, None),
        ((group, width), BF, None),
        ((group, E), F32, None),
    ]
    return pl.pallas_call(
        lambda *refs: attention_forward_kernel(len(after), *refs),
        grid_spec=pltpu.PrefetchScalarGridSpec(
            num_scalar_prefetch=1,
            grid=(1,),
            in_specs=[whole(x.shape) for x in pieces]
            + anywhere(9 + len(after))
            + [whole(x.shape) for x in smalls],
            out_specs=[
                whole(shape) if block is None else pl.BlockSpec(block, per_step)
                for shape, _, block in outs
            ],
            scratch_shapes=[
                pltpu.VMEM((group, width), F32),
                pltpu.VMEM((4, dp, 400, LANES), BF),
                pltpu.SemaphoreType.DMA((9,)),
            ],
        ),
        out_shape=[jax.ShapeDtypeStruct(shape, kind) for shape, kind, _ in outs],
        compiler_params=params(),
        cost_estimate=pl.CostEstimate(
            flops=2 * group * width * 768 * 4 + 16 * 4 * group * group * HD,
            bytes_accessed=width * 768 * 8 + 6 * group * width * 2,
            transcendentals=16 * group * group,
        ),
        name="attention_forward",
    )(scalars, *pieces, *w_attn, *after, *smalls)


def experts_forward_kernel(n_after, sref, *refs):
    (b_ref, gate_ref, w_ref, *refs) = refs[n_after:]
    pieces, (gu_ref, total) = refs[:4], refs[4:]
    step = pl.program_id(0)
    width = b_ref.shape[1]
    ff = w_ref.shape[-1]

    @pl.when(sref[1] > 0)
    def _():
        b = b_ref[...]
        gates = gate_ref[...]
        acts, downs = [], []
        for j in range(PER):
            gate_up = jnp.concatenate(
                [w_ref[:, 0, j].reshape(width, ff), w_ref[:, 1, j].reshape(width, ff)], axis=1
            )
            both = dot(b, gate_up)
            gu_ref[j] = both.astype(BF)
            gate_pre, up_pre = both[:, :ff], both[:, ff:]
            act = gate_pre * jax.nn.sigmoid(gate_pre) * up_pre
            acts.append((act * column(gates, step * PER + j)).astype(BF))
            downs.append(w_ref[:, 2, j].reshape(width, ff))
        out = dot_nt(jnp.concatenate(acts, axis=1), jnp.concatenate(downs, axis=1))

        @pl.when(step == 0)
        def _():
            total[...] = out

        @pl.when(step > 0)
        def _():
            total[...] += out

        @pl.when(step == pl.num_programs(0) - 1)
        def _():
            rows = b_ref.shape[0] // 4
            for shift in range(4):
                place = own_rows(lax.rem(sref[0] + shift, 4), rows)
                pieces[shift][...] = total[place, :].astype(BF)


def experts_forward(scalars, b, gates, w, after):
    group, width = b.shape
    dp, _, experts, dr, ff = w.shape
    piece = (group // 4, width)
    return pl.pallas_call(
        lambda *refs: experts_forward_kernel(len(after), *refs),
        grid_spec=pltpu.PrefetchScalarGridSpec(
            num_scalar_prefetch=1,
            grid=(experts // PER,),
            in_specs=anywhere(len(after))
            + [
                whole((group, width)),
                whole((group, experts)),
                pl.BlockSpec((dp, 3, PER, dr, ff), lambda i, s: (0, 0, i * s[1], 0, 0)),
            ],
            out_specs=[whole(piece)] * 4
            + [pl.BlockSpec((PER, group, 2 * ff), lambda i, s: (i * s[1], 0, 0))],
            scratch_shapes=[pltpu.VMEM((group, width), F32)],
        ),
        out_shape=[jax.ShapeDtypeStruct(piece, BF)] * 4
        + [jax.ShapeDtypeStruct((experts, group, 2 * ff), BF)],
        compiler_params=params(),
        cost_estimate=pl.CostEstimate(
            flops=2 * group * width * ff * 3 * experts,
            bytes_accessed=w.size * 2 + experts * group * 2 * ff * 2,
            transcendentals=experts * group * ff,
        ),
        name="experts_forward",
    )(scalars, *after, b, gates, w)


def experts_backward_kernel(n_after, sref, *refs):
    (*refs,) = refs[n_after:]
    given, refs = refs[:4], refs[4:]
    gate_ref, gu_ref, w_ref, *refs = refs
    pieces, refs = refs[:4], refs[4:]
    grad_ref, dgu_ref, ga_ref, total, total_gate = refs
    step = pl.program_id(0)
    group, width = grad_ref.shape
    ff = w_ref.shape[-1]

    @pl.when(sref[1] > 0)
    def _():
        @pl.when(step == 0)
        def _():
            assemble(sref[0], given, grad_ref)

        grad = grad_ref[...]
        gates = gate_ref[...]
        down = jnp.concatenate(
            [w_ref[:, 2, j].reshape(width, ff) for j in range(PER)], axis=1
        )
        turned = dot(grad, down)
        lanes = lax.broadcasted_iota(jnp.int32, (group, LANES), 1)
        grad_gate = jnp.zeros((group, LANES), F32)
        out = None
        for j in range(PER):
            expert = step * PER + j
            back = turned[:, j * ff : (j + 1) * ff]
            both = gu_ref[j].astype(F32)
            gate_pre, up_pre = both[:, :ff], both[:, ff:]
            sigma = jax.nn.sigmoid(gate_pre)
            silu = gate_pre * sigma
            act = silu * up_pre
            gate = column(gates, expert)
            grad_gate = jnp.where(
                lanes == expert, jnp.sum(act * back, axis=1, keepdims=True), grad_gate
            )
            grad_act = gate * back
            grad_pre = grad_act * up_pre * sigma * (1.0 + gate_pre * (1.0 - sigma))
            grad_up = grad_act * silu
            grad_both = jnp.concatenate([grad_pre.astype(BF), grad_up.astype(BF)], axis=1)
            dgu_ref[j] = grad_both
            ga_ref[:, j * ff : (j + 1) * ff] = (gate * act).astype(BF)
            gate_up = jnp.concatenate(
                [w_ref[:, 0, j].reshape(width, ff), w_ref[:, 1, j].reshape(width, ff)], axis=1
            )
            part = dot_nt(grad_both, gate_up)
            out = part if out is None else out + part

        @pl.when(step == 0)
        def _():
            total[...] = out
            total_gate[...] = grad_gate

        @pl.when(step > 0)
        def _():
            total[...] += out
            total_gate[...] += grad_gate

        @pl.when(step == pl.num_programs(0) - 1)
        def _():
            rows = group // 4
            for shift in range(4):
                place = own_rows(lax.rem(sref[0] + shift, 4), rows)
                pieces[shift][:, :width] = total[place, :].astype(BF)
                pieces[shift][:, width:] = total_gate[place, :].astype(BF)


def experts_backward(scalars, given, gates, gu, w, after):
    dp, _, experts, dr, ff = w.shape
    group = gates.shape[0]
    width = dp * dr
    piece = (group // 4, width + LANES)
    return pl.pallas_call(
        lambda *refs: experts_backward_kernel(len(after), *refs),
        grid_spec=pltpu.PrefetchScalarGridSpec(
            num_scalar_prefetch=1,
            grid=(experts // PER,),
            in_specs=anywhere(len(after))
            + [whole(x.shape) for x in given]
            + [
                whole((group, experts)),
                pl.BlockSpec((PER, group, 2 * ff), lambda i, s: (i * s[1], 0, 0)),
                pl.BlockSpec((dp, 3, PER, dr, ff), lambda i, s: (0, 0, i * s[1], 0, 0)),
            ],
            out_specs=[whole(piece)] * 4
            + [
                whole((group, width)),
                pl.BlockSpec((PER, group, 2 * ff), lambda i, s: (i * s[1], 0, 0)),
                pl.BlockSpec((group, PER * ff), lambda i, s: (0, i * s[1])),
            ],
            scratch_shapes=[pltpu.VMEM((group, width), F32), pltpu.VMEM((group, LANES), F32)],
        ),
        out_shape=[jax.ShapeDtypeStruct(piece, BF)] * 4
        + [
            jax.ShapeDtypeStruct((group, width), BF),
            jax.ShapeDtypeStruct((experts, group, 2 * ff), BF),
            jax.ShapeDtypeStruct((group, experts * ff), BF),
        ],
        compiler_params=params(),
        cost_estimate=pl.CostEstimate(
            flops=2 * group * width * ff * 3 * experts,
            bytes_accessed=w.size * 2 + 5 * experts * group * ff * 2,
            transcendentals=experts * group * ff,
        ),
        name="experts_backward",
    )(scalars, *after, *given, gates, gu, w)


def middle_kernel(n_after, sref, *refs):
    refs = refs[n_after:]
    pieces, refs = refs[:4], refs[4:]
    grad_ref, hown_ref, gates_ref, b_ref, gains_ref, router_ref, dh_ref, do_ref, small_ref = refs
    rows, width = grad_ref.shape

    @pl.when(sref[1] > 0)
    def _():
        place = own_rows(sref[0], rows)
        joined = pieces[0][...].astype(F32)
        for shift in range(1, 4):
            joined = joined + pieces[shift][...].astype(F32)
        grad_normed = joined[:, :width]
        grad_gate = joined[:, width : width + E]
        gates = gates_ref[place, :]
        grad_logits = (
            gates * (grad_gate - jnp.sum(gates * grad_gate, axis=1, keepdims=True))
        ).astype(BF)
        normed = b_ref[place, :]
        grad_normed = grad_normed + dot_nt(grad_logits, router_ref[:, :E])
        hidden = hown_ref[...]
        part, grad_gain = norm_back(hidden, rms_scale(hidden), gains_ref[1:2, :], grad_normed)
        grad_hidden = grad_ref[...].astype(F32) + part
        dh_ref[...] = grad_hidden
        do_ref[...] = grad_hidden.astype(BF)
        small_ref[0:E, :] = dot_tn(grad_logits, normed)
        small_ref[E : E + 1, :] = grad_gain
        small_ref[E + 1 :, :] = jnp.zeros((small_ref.shape[0] - E - 1, width), F32)


def middle(scalars, pieces, grad_own, hown, gates, b, gains, router, after):
    rows, width = grad_own.shape
    operands = [*pieces, grad_own, hown, gates, b, gains, router]
    return pl.pallas_call(
        lambda *refs: middle_kernel(len(after), *refs),
        grid_spec=pltpu.PrefetchScalarGridSpec(
            num_scalar_prefetch=1,
            grid=(1,),
            in_specs=anywhere(len(after)) + [whole(x.shape) for x in operands],
            out_specs=[whole((rows, width)), whole((rows, width)), whole((24, width))],
        ),
        out_shape=[
            jax.ShapeDtypeStruct((rows, width), F32),
            jax.ShapeDtypeStruct((rows, width), BF),
            jax.ShapeDtypeStruct((24, width), F32),
        ],
        compiler_params=params(),
        cost_estimate=pl.CostEstimate(
            flops=rows * width * 64, bytes_accessed=rows * width * 24, transcendentals=rows
        ),
        name="norm_backward",
    )(scalars, *after, *operands)


def attention_backward_kernel(n_after, sref, *refs):
    pieces, refs = refs[:4], refs[4:]
    sources, refs = refs[:9], refs[9 + n_after :]
    (
        dh_ref, xown_ref, small_ref, gains_ref, cos_ref, sin_ref, bias_ref, qkv_ref, lse_ref,
        dx_ref, dxlow_ref, small_out_ref, full_ref, dqkv_ref,
        now, buffers, sems,
    ) = refs
    me = sref[0]
    shard = dh_ref.shape[0]

    @pl.when(sref[1] > 0)
    def _():
        copies = fetches(sref[2], sources, buffers, sems)
        for copy in copies[0]:
            copy.start()
        assemble(me, pieces, full_ref)
        bias = bias_ref[...]
        lse = lse_ref[...]
        cos = jnp.concatenate([cos_ref[...]] * 3, axis=1)
        sin = jnp.concatenate([sin_ref[...]] * 3, axis=1)
        total = jnp.zeros((shard, full_ref.shape[1]), F32)
        for step in range(4):
            for copy in copies[step]:
                copy.wait()
            for copy in copies[step + 1] if step < 3 else []:
                copy.start()
            w_qkv, w_out = group_weights(buffers, step)
            do = dot(full_ref[...], w_out).astype(BF)
            qkv = qkv_ref[step]
            q, k, v = qkv[:, :256], qkv[:, 256:384], qkv[:, 384:]
            q_turned = q.T
            do_turned = do.T
            dq, dk, dv = [], [], []
            for kv in range(2):
                k_one = k[:, kv * HD : (kv + 1) * HD]
                v_one = v[:, kv * HD : (kv + 1) * HD]
                dk_one = dv_one = None
                for head in (2 * kv, 2 * kv + 1):
                    part = slice(head * HD, (head + 1) * HD)
                    scores = dot_nt(q[:, part], k_one) + bias
                    soft = jnp.exp(scores - lse[:, 4 * step + head : 4 * step + head + 1])
                    grad_soft = dot_nt(do[:, part], v_one)
                    grad_scores = soft * (
                        grad_soft - jnp.sum(soft * grad_soft, axis=1, keepdims=True)
                    )
                    grad_scores = grad_scores.astype(BF)
                    dq.append(dot(grad_scores, k_one))
                    dk_part = dot(q_turned[part, :], grad_scores)
                    dv_part = dot(do_turned[part, :], soft.astype(BF))
                    dk_one = dk_part if dk_one is None else dk_one + dk_part
                    dv_one = dv_part if dv_one is None else dv_one + dv_part
                dk.append(dk_one)
                dv.append(dv_one)
            grad_k = jnp.concatenate(dk, axis=0).T
            grad_v = jnp.concatenate(dv, axis=0).T
            grad_qk = jnp.concatenate([jnp.concatenate(dq, axis=1) * HD**-0.5, grad_k], axis=1)
            grad_qk = (grad_qk * cos - swap_halves(grad_qk) * sin).astype(BF)
            now[step, :, :384] = grad_qk
            now[step, :, 384:] = grad_v.astype(BF)
            if step == 0:
                dqkv_ref[...] = now[0]
            total += dot_nt(now[step, own_rows(me, shard), :], w_qkv)

        entering = xown_ref[...].astype(F32)
        part, grad_gain = norm_back(entering, rms_scale(entering), gains_ref[0:1, :], total)
        grad_entering = dh_ref[...] + part
        dx_ref[...] = grad_entering
        dxlow_ref[...] = grad_entering.astype(BF)
        rows = lax.broadcasted_iota(jnp.int32, small_ref.shape, 0)
        small_out_ref[...] = jnp.where(rows == E + 1, grad_gain, small_ref[...])


def attention_backward(
    scalars, pieces, dh, xown, small, gains, tables, qkv, lse, w_attn, after
):
    shard, width = dh.shape
    group = 4 * shard
    dp = width // 64
    cos, sin, bias = tables
    smalls = [dh, xown, small, gains, cos, sin, bias]
    per_step = lambda i, s: (i * s[1], 0, 0)
    outs = [
        ((shard, width), F32),
        ((shard, width), BF),
        (small.shape, F32),
        ((group, width), BF),
        ((group, 512), BF),
    ]
    return pl.pallas_call(
        lambda *refs: attention_backward_kernel(len(after), *refs),
        grid_spec=pltpu.PrefetchScalarGridSpec(
            num_scalar_prefetch=1,
            grid=(1,),
            in_specs=[whole(x.shape) for x in pieces]
            + anywhere(9 + len(after))
            + [whole(x.shape) for x in smalls]
            + [whole(qkv.shape), whole(lse.shape)],
            out_specs=[whole(shape) for shape, _ in outs],
            scratch_shapes=[
                pltpu.VMEM((4, group, 512), BF),
                pltpu.VMEM((4, dp, 400, LANES), BF),
                pltpu.SemaphoreType.DMA((9,)),
            ],
        ),
        out_shape=[jax.ShapeDtypeStruct(shape, kind) for shape, kind in outs],
        compiler_params=params(),
        cost_estimate=pl.CostEstimate(
            flops=group * width * 1024 * 2 + 16 * 10 * group * group * HD,
            bytes_accessed=width * 768 * 8 + 6 * group * width * 2,
            transcendentals=16 * group * group,
        ),
        name="attention_backward",
    )(scalars, *pieces, *w_attn, *after, *smalls, qkv, lse)


def expert_weights_kernel(n_after, sref, *refs):
    refs = refs[n_after:]
    b, refs = refs[:4], refs[4:]
    g, refs = refs[:4], refs[4:]
    dgu, refs = refs[:4], refs[4:]
    ga, refs = refs[:4], refs[4:]
    out_ref, bt_ref, gt_ref = refs
    group = b[0].shape[0]
    dp, _, _, dr, ff = out_ref.shape
    first = sref[1] > 0

    def chosen(four, micro, *index):
        index = index or (Ellipsis,)
        return jnp.where(first, four[micro][index], four[2 + micro][index])

    @pl.when(pl.program_id(0) == 0)
    def _():
        for micro in range(2):
            place = slice(micro * group, (micro + 1) * group)
            bt_ref[:, place] = chosen(b, micro).T
            gt_ref[:, place] = chosen(g, micro).T

    bt = bt_ref[...]
    for j in range(PER_GRAD):
        rows = jnp.concatenate([chosen(dgu, 0, j), chosen(dgu, 1, j)], axis=0)
        grads = dot(bt, rows).astype(BF)
        out_ref[:, 0, j] = grads[:, :ff].reshape(dp, dr, ff)
        out_ref[:, 1, j] = grads[:, ff:].reshape(dp, dr, ff)
    rows = jnp.concatenate([chosen(ga, 0), chosen(ga, 1)], axis=0)
    grads = dot(gt_ref[...], rows).astype(BF)
    for j in range(PER_GRAD):
        out_ref[:, 2, j] = grads[:, j * ff : (j + 1) * ff].reshape(dp, dr, ff)


def expert_weights(scalars, rows_b, grads, dgus, gas, dp, after):
    group, width = rows_b[0].shape
    experts, _, ff2 = dgus[0].shape
    ff = ff2 // 2
    dr = width // dp
    square = whole((group, width))
    wide, flat = [], []
    for held in (lambda s: s[1], lambda s: 1 - s[1]):
        wide += [
            pl.BlockSpec((PER_GRAD, group, ff2), lambda i, s, held=held: (i * held(s), 0, 0))
        ] * 2
        flat += [pl.BlockSpec((group, PER_GRAD * ff), lambda i, s, held=held: (0, i * held(s)))] * 2
    return pl.pallas_call(
        lambda *refs: expert_weights_kernel(len(after), *refs),
        grid_spec=pltpu.PrefetchScalarGridSpec(
            num_scalar_prefetch=1,
            grid=(experts // PER_GRAD,),
            in_specs=anywhere(len(after)) + [square] * 8 + wide + flat,
            out_specs=pl.BlockSpec((dp, 3, PER_GRAD, dr, ff), lambda i, s: (0, 0, i, 0, 0)),
            scratch_shapes=[
                pltpu.VMEM((width, 2 * group), BF),
                pltpu.VMEM((width, 2 * group), BF),
            ],
        ),
        out_shape=jax.ShapeDtypeStruct((dp, 3, experts, dr, ff), BF),
        compiler_params=params(),
        cost_estimate=pl.CostEstimate(
            flops=4 * group * width * ff * 3 * experts,
            bytes_accessed=dp * 3 * experts * dr * ff * 2 + 6 * experts * group * ff * 2,
            transcendentals=0,
        ),
        name="expert_weight_grads",
    )(scalars, *after, *rows_b, *grads, *dgus, *gas)


def attention_weights_kernel(sref, *refs):
    a, o, f, d, small = (refs[4 * j : 4 * j + 4] for j in range(5))
    out_ref = refs[20]
    dp = out_ref.shape[0]
    first = sref[1] > 0

    def chosen(four, micro):
        return jnp.where(first, four[micro][...], four[2 + micro][...])

    sums = dot_tn(chosen(a, 0), chosen(d, 0)) + dot_tn(chosen(a, 1), chosen(d, 1))
    for j in range(4):
        out_ref[:, 64 * j : 64 * (j + 1), :] = (
            sums[:, LANES * j : LANES * (j + 1)].astype(BF).reshape(dp, 64, LANES)
        )
    sums = dot_tn(chosen(f, 0), chosen(o, 0)) + dot_tn(chosen(f, 1), chosen(o, 1))
    for j in range(2):
        out_ref[:, 64 * (4 + j) : 64 * (5 + j), :] = (
            sums[:, LANES * j : LANES * (j + 1)].astype(BF).reshape(dp, 64, LANES)
        )
    rows = chosen(small, 0) + chosen(small, 1)
    rows = jnp.concatenate(
        [rows, jnp.zeros((LANES - rows.shape[0], rows.shape[1]), F32)], axis=0
    )
    out_ref[:, 384:, :] = rows.T.astype(BF).reshape(dp, 64, LANES)


def attention_weights(scalars, a, o, f, d, small, dp):
    group, width = a[0].shape
    operands = [*a, *o, *f, *d, *small]
    return pl.pallas_call(
        attention_weights_kernel,
        grid_spec=pltpu.PrefetchScalarGridSpec(
            num_scalar_prefetch=1,
            grid=(1,),
            in_specs=[whole(x.shape) for x in operands],
            out_specs=whole((dp, 448, LANES)),
        ),
        out_shape=jax.ShapeDtypeStruct((dp, 448, LANES), BF),
        compiler_params=params(),
        cost_estimate=pl.CostEstimate(
            flops=4 * group * width * 768,
            bytes_accessed=group * width * 14 + width * 768 * 2,
            transcendentals=0,
        ),
        name="attention_weight_grads",
    )(scalars, *operands)


def moved(array, shift):
    return lax.ppermute(array, "tensor", [(i, (i + shift) % 4) for i in range(4)])


def swapped(array, dp):
    return lax.ppermute(array, "dp", [(i, i ^ 1) for i in range(dp)])


def to_owner(pieces):
    return [pieces[0]] + [moved(pieces[s], s) for s in range(1, 4)]


def to_all(rows):
    return [rows] + [moved(rows, s) for s in range(1, 4)]


def across(rows, up):
    start, end = (0, 4) if up else (4, 0)
    return [
        lax.ppermute(
            rows, ("pipe", "tensor"), [(start + i, end + (i + s) % 4) for i in range(4)]
        )
        for s in range(4)
    ]


def tables_of(lengths, group):
    ends = jnp.cumsum(lengths)
    starts = ends - lengths
    index = jnp.arange(group, dtype=jnp.int32)
    inside = index[:, None] >= starts[None, :]
    start = jnp.max(jnp.where(inside, starts[None, :], 0), axis=1)
    position = (index - start).astype(F32)
    half = HD // 2
    freq = jnp.exp(jnp.arange(half, dtype=F32) * (-2.0 * math.log(10000.0) / HD))
    angle = position[:, None] * freq[None, :]
    cos, sin = jnp.cos(angle), jnp.sin(angle)
    visible = (index[None, :] <= index[:, None]) & (index[None, :] >= start[:, None])
    bias = jnp.where(visible, 0.0, MASKED).astype(F32)
    return (
        jnp.concatenate([cos, cos, cos, cos], axis=1),
        jnp.concatenate([-sin, sin, -sin, sin], axis=1),
        bias,
    )


def per_device(
    inputs, cotangent, doc_lengths, routes, norm_attn, w_query, w_key, w_value, w_out,
    w_router, norm_ffn, w_gate, w_up, w_down,
):
    section = lax.axis_index("pipe")
    first_section = section == 0
    me = lax.axis_index("tensor")
    dp = lax.axis_size("dp")
    core = lax.axis_index("dp") % 2
    micro = inputs.shape[0]
    shard, width = inputs.shape[1:]
    group = shard * 4
    rows_dp = width // dp
    scalars = [
        jnp.stack([me, (section == s).astype(jnp.int32), core]).astype(jnp.int32)
        for s in range(2)
    ]

    out_turned = w_out[0].T
    small = jnp.concatenate([w_router[0], norm_attn[0][:, None], norm_ffn[0][:, None]], axis=1)
    small = jnp.pad(small, ((0, 0), (0, LANES - E - 2)))
    piece = jnp.concatenate(
        [
            w_query[0][:, :LANES], w_query[0][:, LANES:], w_key[0], w_value[0],
            out_turned[:, :LANES], out_turned[:, LANES:], small,
        ],
        axis=0,
    )
    w_own = jnp.broadcast_to(piece[None], (dp,) + piece.shape)
    w_own, inputs, cotangent = lax.optimization_barrier((w_own, inputs, cotangent))
    w_own = lax.all_to_all(w_own, "dp", 0, 0, tiled=True)
    pieces_w = jnp.stack([w_gate[0], w_up[0], w_down[0].transpose(0, 2, 1)])
    w_experts = lax.all_gather(pieces_w, "dp", axis=0)
    rows_in, rows_cot = to_all(inputs), to_all(cotangent)
    rows_in, rows_cot, w_own = lax.optimization_barrier((rows_in, rows_cot, w_own))
    half, quarter = dp // 2, dp // 4
    mine = lax.dynamic_slice_in_dim(w_own, core * half, half, 0)
    w_next, w_last = moved(mine, 1), moved(mine, 3)
    w_over = [moved(w_next[:quarter], 1), moved(w_last[quarter:], 3)]
    other = [swapped(x, dp) for x in (w_next, w_last, *w_over)]
    w_attn = [w_own, w_next, other[0], *w_over, other[2], other[3], w_last, other[1]]
    router, gains = smalls_of(scalars[0], w_attn)

    rows_in = [[part[m] for part in rows_in] for m in range(micro)]
    rows_cot = [[part[m] for part in rows_cot] for m in range(micro)]
    tables = [tables_of(doc_lengths[m, 0], group) for m in range(micro)]
    ids = jnp.arange(E, dtype=jnp.int32)
    picked = jnp.any(routes[0][..., None] == ids, axis=2).astype(F32)

    after = []
    saves = [[None] * micro, [None] * micro]
    firsts = [[None] * micro, [None] * micro]
    middles = [[None] * micro, [None] * micro]
    lasts = [[None] * micro, [None] * micro]

    def attend(s, m, pieces):
        nonlocal after
        out = attention_forward(
            scalars[s], pieces, gains, tables[m], picked[m], w_attn, router, after
        )
        saves[s][m] = list(out)
        after = [out[6]]

    def expert(s, m):
        nonlocal after
        b, gates = saves[s][m][6:8]
        *parts, gu = experts_forward(scalars[s], b, gates, w_experts, after)
        saves[s][m].append(gu)
        after = [gu]
        return parts

    def expert_back(s, m, pieces):
        nonlocal after
        gates, gu = saves[s][m][7:9]
        *parts, grad, dgu, ga = experts_backward(
            scalars[s], pieces, gates, gu, w_experts, after
        )
        after = [grad]
        firsts[s][m] = (to_owner(parts), grad, dgu, ga)

    def norm_between(s, m, own):
        nonlocal after
        kept = saves[s][m]
        dh, do, small = middle(
            scalars[s], firsts[s][m][0], own, kept[5], kept[7], kept[6], gains, router, after
        )
        middles[s][m] = (dh, to_all(do), small)
        after = [do]

    def attend_back(s, m):
        nonlocal after
        kept = saves[s][m]
        dh, rows, small = middles[s][m]
        dx, dx_low, small, full, dqkv = attention_backward(
            scalars[s], rows, dh, kept[1], small, gains, tables[m], kept[2], kept[4],
            w_attn, after,
        )
        lasts[s][m] = (small, full, dqkv, dx)
        after = [dx]
        return dx_low

    def layer_sum(parts, hown):
        return finish(to_owner(parts), hown)

    attend(0, 0, rows_in[0])
    first_out = layer_sum(expert(0, 0), saves[0][0][5])
    first_in = across(first_out, True)
    after = [first_out]
    attend(0, 1, rows_in[1])
    attend(1, 0, first_in)
    second_out = layer_sum(expert(0, 1), saves[0][1][5])
    second_in = across(second_out, True)
    late = [expert(1, 0)]
    expert_back(1, 0, rows_cot[0])
    attend(1, 1, second_in)
    late.append(expert(1, 1))
    norm_between(1, 0, cotangent[0])
    expert_back(1, 1, rows_cot[1])
    first_back = across(attend_back(1, 0), False)
    norm_between(1, 1, cotangent[1])
    second_back = across(attend_back(1, 1), False)
    expert_back(0, 0, first_back)
    norm_between(0, 0, first_back[0])
    expert_back(0, 1, second_back)
    joined = firsts[0] + firsts[1]
    grad_experts = expert_weights(
        scalars[0],
        [saves[s][m][6] for s in range(2) for m in range(micro)],
        [x[1] for x in joined],
        [x[2] for x in joined],
        [x[3] for x in joined],
        dp,
        after,
    )
    expert_sums = lax.psum_scatter(grad_experts, "dp", scatter_dimension=0, tiled=True)[0]
    after = [grad_experts]
    norm_between(0, 1, second_back[0])
    attend_back(0, 0)
    attend_back(0, 1)
    late, _ = lax.optimization_barrier((late, lasts[1][1][3]))
    outputs = [
        [first_out, second_out],
        [layer_sum(late[m], saves[1][m][5]) for m in range(micro)],
    ]
    grads_in = [[lasts[s][m][3] for m in range(micro)] for s in range(2)]

    joined = lasts[0] + lasts[1]
    grad_attn = attention_weights(
        scalars[0],
        [saves[s][m][0] for s in range(2) for m in range(micro)],
        [saves[s][m][3] for s in range(2) for m in range(micro)],
        [x[1] for x in joined],
        [x[2] for x in joined],
        [x[0] for x in joined],
        dp,
    )
    grad_attn = lax.all_to_all(grad_attn, "dp", 0, 0, tiled=True)
    attn_sums = jnp.sum(grad_attn.astype(F32), axis=0)
    small = attn_sums[384:].reshape(4, 16, LANES)
    small_own = None
    for shift in range(4):
        part = lax.dynamic_index_in_dim(small, (me + shift) % 4, 0, keepdims=False)
        part = moved(part, shift) if shift else part
        small_own = part if small_own is None else small_own + part
    expert_sums = expert_sums.astype(F32)
    blocks = [attn_sums[64 * j : 64 * (j + 1)] for j in range(6)]
    section_rows = jnp.stack(
        [jnp.where(first_section, outputs[0][m], outputs[1][m]) for m in range(micro)]
    )
    grad_in = jnp.stack(
        [jnp.where(first_section, grads_in[0][m], grads_in[1][m]) for m in range(micro)]
    )
    return (
        section_rows[None],
        grad_in[None],
        small_own[:, E + 1][None],
        jnp.concatenate(blocks[:2], axis=1)[None],
        blocks[2][None],
        blocks[3][None],
        jnp.concatenate(blocks[4:], axis=1).T[None],
        small_own[:, :E][None],
        small_own[:, E][None],
        expert_sums[0][None],
        expert_sums[1][None],
        expert_sums[2].transpose(0, 2, 1)[None],
    )


def finish(parts, hown):
    result = hown
    for part in parts:
        result = result + part.astype(F32)
    return result.astype(BF)


def solution(mesh):
    in_specs = (
        P(None, ("dp", "tensor"), None),
        P(None, ("dp", "tensor"), None),
        P(None, "dp", None),
        P("pipe", None, "dp", None),
        P("pipe", ("dp", "tensor")),
        P("pipe", "dp", "tensor"),
        P("pipe", "dp", "tensor"),
        P("pipe", "dp", "tensor"),
        P("pipe", "tensor", "dp"),
        P("pipe", ("dp", "tensor"), None),
        P("pipe", ("dp", "tensor")),
        P("pipe", None, "dp", "tensor"),
        P("pipe", None, "dp", "tensor"),
        P("pipe", None, "tensor", "dp"),
    )
    out_specs = (
        P("pipe", None, ("dp", "tensor"), None),
        P("pipe", None, ("dp", "tensor"), None),
        P("pipe", ("dp", "tensor")),
        P("pipe", "dp", "tensor"),
        P("pipe", "dp", "tensor"),
        P("pipe", "dp", "tensor"),
        P("pipe", "tensor", "dp"),
        P("pipe", ("dp", "tensor"), None),
        P("pipe", ("dp", "tensor")),
        P("pipe", None, "dp", "tensor"),
        P("pipe", None, "dp", "tensor"),
        P("pipe", None, "tensor", "dp"),
    )
    return jax.shard_map(
        per_device, mesh=mesh, in_specs=in_specs, out_specs=out_specs, check_vma=False
    )
```

profile of v0, /device:TPU:0, one launch (start us, length us, event | category | flops | bytes accessed | tf_op | source)
XLA Modules:
  0.0 461.6 jit_solution(14248712349299581764)
XLA Ops:
  18.5 5.9 %all-to-all-start = ((bf16[16,400,128]{2,1,0:T(8,128)(2,1)}), bf16[16,400,128]{2,1,0:T(8,128)(2,1)S(1)}, u32[]{:S(2)}, u32[]{:S(2)}) async-start(bf16[16,400,128]{2,1,0:T(8,128)(2,1)} %broadcast_in_dim.42), calls=%async_computation | async-start | bytes 3276800 | tf_op jit(solution)/shard_map/all_to_all | solution.py:831
  34.2 4.3 collective-permute-done.4
  40.5 21.9 %all-to-all-done.refs_0_.refs_5_ = bf16[16,400,128]{2,1,0:T(8,128)(2,1)S(1)} async-done(((bf16[16,400,128]{2,1,0:T(8,128)(2,1)}), bf16[16,400,128]{2,1,0:T(8,128)(2,1)S(1)}, u32[]{:S(2)}, u32[]{:S(2)}) %all-to-all-start) | async-done | bytes 1638432 | tf_op jit(solution)/shard_map/all_to_all | solution.py:831
  71.3 13.3 %collective-permute-done.6.refs_1_.refs_6_ = bf16[8,400,128]{2,1,0:T(8,128)(2,1)S(1)} collective-permute-done((bf16[8,400,128]{2,1,0:T(8,128)(2,1)S(1)}, bf16[8,400,128]{2,1,0:T(8,128)(2,1)S(1)}, u32[]{:S(2)}, u32[]{:S(2)}) %collective-permute-start.6) | collective-permute-done | bytes 819232 | tf_op jit(solution)/shard_map/ppermute | solution.py:756
  90.1 7.2 %collective-permute-done.8.refs_3_.refs_8_ = bf16[4,400,128]{2,1,0:T(8,128)(2,1)S(1)} collective-permute-done((bf16[4,400,128]{2,1,0:T(8,128)(2,1)S(1)}, bf16[4,400,128]{2,1,0:T(8,128)(2,1)S(1)}, u32[]{:S(2)}, u32[]{:S(2)}) %collective-permute-start.8) | collective-permute-done | bytes 409632 | tf_op jit(solution)/shard_map/ppermute | solution.py:756
  104.0 12.3 %attention_forward.4 = (bf16[256,1024]{1,0:T(8,128)(2,1)}, bf16[64,1024]{1,0:T(8,128)(2,1)}, bf16[4,256,512]{2,1,0:T(8,128)(2,1)}, bf16[256,256]{1,0:T(8,128)(2,...) custom-call(s32[3]{0:T(128)} %add_add_fusion.sref.refs_0_, ...), custom_call_target="tpu_custom_call" | custom-call | flops 1879048192 | bytes 9437184 | tf_op jit(solution)/shard_map/attention_forward/pallas_call | solution.py:259
  116.3 8.8 %experts_forward.4 = (bf16[64,1024]{1,0:T(8,128)(2,1)}, bf16[64,1024]{1,0:T(8,128)(2,1)}, bf16[64,1024]{1,0:T(8,128)(2,1)}, bf16[64,1024]{1,0:T(8,128)(2,1)}, bf16[16,256,256]{2,1,0:T(8,128)(2,1)}) custom-call(s32[3]{0:T(128)} %add_add_fusion.sref.refs_0_, bf16[256,1024]{1,0:T(8,128)(2,1)} %get-tuple-element.155.refs_1_.refs_2_.refs_9_, ...), custom_call_target="tpu_custom_call" | custom-call | flops 3221225472 | bytes 14680064 | tf_op jit(solution)/shard_map/experts_forward/pallas_call | solution.py:332
  143.6 12.5 %attention_forward.5 = (bf16[256,1024]{1,0:T(8,128)(2,1)}, bf16[64,1024]{1,0:T(8,128)(2,1)}, bf16[4,256,512]{2,1,0:T(8,128)(2,1)}, bf16[256,256]{1,0:T(8,128)(2,...) custom-call(s32[3]{0:T(128)} %add_add_fusion.sref.refs_0_, ...), custom_call_target="tpu_custom_call" | custom-call | flops 1879048192 | bytes 9437184 | tf_op jit(solution)/shard_map/attention_forward/pallas_call | solution.py:259
  160.8 8.6 %experts_forward.5 = (bf16[64,1024]{1,0:T(8,128)(2,1)}, bf16[64,1024]{1,0:T(8,128)(2,1)}, bf16[64,1024]{1,0:T(8,128)(2,1)}, bf16[64,1024]{1,0:T(8,128)(2,1)}, bf16[16,256,256]{2,1,0:T(8,128)(2,1)}) custom-call(s32[3]{0:T(128)} %add_add_fusion.sref.refs_0_, bf16[256,1024]{1,0:T(8,128)(2,1)} %get-tuple-element.163.refs_1_.refs_2_.refs_9_.refs_4_, ...), custom_call_target="tpu_custom_call" | custom-call | flops 3221225472 | bytes 14680064 | tf_op jit(solution)/shard_map/experts_forward/pallas_call | solution.py:332
  171.4 4.9 %experts_forward.6 = (bf16[64,1024]{1,0:T(8,128)(2,1)}, bf16[64,1024]{1,0:T(8,128)(2,1)}, bf16[64,1024]{1,0:T(8,128)(2,1)}, bf16[64,1024]{1,0:T(8,128)(2,1)}, bf16[16,256,256]{2,1,0:T(8,128)(2,1)}) custom-call(s32[3]{0:T(128)} %add_add_fusion.1.refs_0_, bf16[16,256,256]{2,1,0:T(8,128)(2,1)} %get-tuple-element.165.refs_1_.refs_7_, ...), custom_call_target="tpu_custom_call" | custom-call | flops 3221225472 | bytes 14680064 | tf_op jit(solution)/shard_map/experts_forward/pallas_call | solution.py:332
  179.4 6.5 %collective-permute-start.24 = (bf16[64,1024]{1,0:T(8,128)(2,1)S(1)}, bf16[64,1024]{1,0:T(8,128)(2,1)S(1)}, u32[]{:S(2)}, u32[]{:S(2)}) collective-permute-start(bf16[64,1024]{1,0:T(8,128)(2,1)S(1)} %add_convert_fusion.2), channel_id=1, source_target_pairs={{0,64},{1,65},{2,66},{3,67},{4,68},{5,69},{6,70},{7,71},{8,72},{9,... | collective-permute-start | bytes 393224 | tf_op jit(solution)/shard_map/ppermute | solution.py:774
  193.1 5.4 %experts_backward.4 = (bf16[64,1152]{1,0:T(8,128)(2,1)}, bf16[64,1152]{1,0:T(8,128)(2,1)}, bf16[64,1152]{1,0:T(8,128)(2,1)}, bf16[64,1152]{1,0:T(8,128)(2,1)}, b...) custom-call(s32[3]{0:T(128)} %add_add_fusion.1.refs_0_, ...), custom_call_target="tpu_custom_call" | custom-call | flops 3221225472 | bytes 17825792 | tf_op jit(solution)/shard_map/experts_backward/pallas_call | solution.py:432
  206.6 4.8 %experts_forward.7 = (bf16[64,1024]{1,0:T(8,128)(2,1)}, bf16[64,1024]{1,0:T(8,128)(2,1)}, bf16[64,1024]{1,0:T(8,128)(2,1)}, bf16[64,1024]{1,0:T(8,128)(2,1)}, bf16[16,256,256]{2,1,0:T(8,128)(2,1)}) custom-call(s32[3]{0:T(128)} %add_add_fusion.1.refs_0_, bf16[256,1024]{1,0:T(8,128)(2,1)} %get-tuple-element.182.refs_1_.refs_2_.refs_9_.refs_5_, ...), custom_call_target="tpu_custom_call" | custom-call | flops 3221225472 | bytes 14680064 | tf_op jit(solution)/shard_map/experts_forward/pallas_call | solution.py:332
  220.6 5.4 %experts_backward.5 = (bf16[64,1152]{1,0:T(8,128)(2,1)}, bf16[64,1152]{1,0:T(8,128)(2,1)}, bf16[64,1152]{1,0:T(8,128)(2,1)}, bf16[64,1152]{1,0:T(8,128)(2,1)}, b...) custom-call(s32[3]{0:T(128)} %add_add_fusion.1.refs_0_, ...), custom_call_target="tpu_custom_call" | custom-call | flops 3221225472 | bytes 17825792 | tf_op jit(solution)/shard_map/experts_backward/pallas_call | solution.py:432
  253.2 29.7 %collective-permute-done.46.refs_2_.refs_6_ = bf16[64,1024]{1,0:T(8,128)(2,1)S(1)} collective-permute-done((bf16[64,1024]{1,0:T(8,128)(2,1)S(1)}, bf16[64,1024]{1,0:T(8,128)(2,1)S(1)}, u32[]{:S(2)}, u32[]{:S(2)}) %collective-permute-start.46) | collective-permute-done | bytes 131104 | tf_op jit(solution)/shard_map/ppermute | solution.py:774
  286.4 10.6 %experts_backward.6 = (bf16[64,1152]{1,0:T(8,128)(2,1)}, bf16[64,1152]{1,0:T(8,128)(2,1)}, bf16[64,1152]{1,0:T(8,128)(2,1)}, bf16[64,1152]{1,0:T(8,128)(2,1)}, b...) custom-call(s32[3]{0:T(128)} %add_add_fusion.sref.refs_0_, ...), custom_call_target="tpu_custom_call" | custom-call | flops 3221225472 | bytes 17825792 | tf_op jit(solution)/shard_map/experts_backward/pallas_call | solution.py:432
  320.2 10.4 %experts_backward.7 = (bf16[64,1152]{1,0:T(8,128)(2,1)}, bf16[64,1152]{1,0:T(8,128)(2,1)}, bf16[64,1152]{1,0:T(8,128)(2,1)}, bf16[64,1152]{1,0:T(8,128)(2,1)}, b...) custom-call(s32[3]{0:T(128)} %add_add_fusion.sref.refs_0_, ...), custom_call_target="tpu_custom_call" | custom-call | flops 3221225472 | bytes 17825792 | tf_op jit(solution)/shard_map/experts_backward/pallas_call | solution.py:432
  330.6 14.4 %expert_weight_grads.1.refs_1_ = bf16[16,3,16,64,128]{4,3,2,1,0:T(8,128)(2,1)} custom-call(s32[3]{0:T(128)} %add_add_fusion.sref.refs_0_, bf16[256,1024]{1,0:T(8,128)(2,1)} %get-tuple-element.230.refs_1_.refs_7_, bf16[256,1024]{1,0:T(8,128)(2,1)} %get-tuple-element.155.refs_1_.refs_2_.refs_9_, ...), custom_call_target="tpu_custom_call" | custom-call | flops 6442450944 | bytes 18874368 | tf_op jit(solution)/shard_map/expert_weight_grads/pallas_call | solution.py:684
  367.2 15.5 %attention_backward.6 = (f32[64,1024]{1,0:T(8,128)}, bf16[64,1024]{1,0:T(8,128)(2,1)}, f32[24,1024]{1,0:T(8,128)}, bf16[256,1024]{1,0:T(8,128)(2,1)}, bf16[256,512]{1,0:T(8,128)(2,1)}) custom-call(s32[3]{0:T(128)} %add_add_fusion.sref.refs_0_, bf16[64,1024]{1,0:T(8,128)(2,1)} %get-tuple-element.228.refs_1_, bf16[64,1024]{1,0:T(8,128)(2,1)} %copy-done.37, ...), custom_call_target="tpu_custom_call" | custom-call | flops 1207959552 | bytes 9437184 | tf_op jit(solution)/shard_map/attention_backward/pallas_call | solution.py:611
  383.4 15.6 %attention_backward.7 = (f32[64,1024]{1,0:T(8,128)}, bf16[64,1024]{1,0:T(8,128)(2,1)}, f32[24,1024]{1,0:T(8,128)}, bf16[256,1024]{1,0:T(8,128)(2,1)}, bf16[256,512]{1,0:T(8,128)(2,1)}) custom-call(s32[3]{0:T(128)} %add_add_fusion.sref.refs_0_, bf16[64,1024]{1,0:T(8,128)(2,1)} %get-tuple-element.243.refs_14_.refs_1_, bf16[64,1024]{1,0:T(8,128)(2,1)} %copy-done.36, ...), custom_call_target="tpu_custom_call" | custom-call | flops 1207959552 | bytes 9437184 | tf_op jit(solution)/shard_map/attention_backward/pallas_call | solution.py:611
  399.0 6.1 %attention_weight_grads.1 = bf16[16,448,128]{2,1,0:T(8,128)(2,1)} custom-call(s32[3]{0:T(128)} %add_add_fusion.sref.refs_0_, bf16[256,1024]{1,0:T(8,128)(2,1)} %get-tuple-element.256.refs_0_, bf16[256,1024]{1,0:T(8,128)(2,1)} %get-tuple-element.257.refs_1_, bf16[256,1024]{1,0:T(8,128)(2,1)} %get-tuple-element.258.refs_2_, ...), custom_call_target="tpu_custom_call" | custom-call | flops 805306368 | bytes 5242880 | tf_op jit(solution)/shard_map/attention_weight_grads/pallas_call | solution.py:736
  405.1 5.2 %all-to-all-start.1 = ((bf16[16,448,128]{2,1,0:T(8,128)(2,1)}), bf16[16,448,128]{2,1,0:T(8,128)(2,1)S(1)}, u32[]{:S(2)}, u32[]{:S(2)}) async-start(bf16[16,448,128]{2,1,0:T(8,128)(2,1)} %attention_weight_grads.1), calls=%async_computation.1 | async-start | bytes 3670016 | tf_op jit(solution)/shard_map/all_to_all | solution.py:957
  417.6 4.1 collective-permute-start.40
  429.1 12.4 %all-to-all-done.1 = bf16[16,448,128]{2,1,0:T(8,128)(2,1)S(1)} async-done(((bf16[16,448,128]{2,1,0:T(8,128)(2,1)}), bf16[16,448,128]{2,1,0:T(8,128)(2,1)S(1)}, u32[]{:S(2)}, u32[]{:S(2)}) %all-to-all-start.1) | async-done | bytes 1835040 | tf_op jit(solution)/shard_map/all_to_all | solution.py:957
  (364 shorter events, 200.4 us)
Async XLA Ops:
  7.3 109.1 %all-gather.3.cloned.1.call-start = ((), (), s32[]{:S(2)}) async-start(), calls=%async_computation.4 | async-start | bytes 13369344 | tf_op jit(solution)/shard_map/all_gather | solution.py:833
  11.3 19.6 %collective-permute-start = (bf16[2,64,1024]{2,1,0:T(8,128)(2,1)S(1)}, bf16[2,64,1024]{2,1,0:T(8,128)(2,1)}, u32[]{:S(2)}, u32[]{:S(2)}) collective-permute-start(bf16[2,64,1024]{2,1,0:T(8,128)(2,1)S(1)} %copy-done.22), channel_id=1, source_target_pairs={{0,1},{1,2},{2,3},{3,0},{4,5},{5,6},{6,7},{7,4},{8,9},{9,10},{10,1... | collective-permute-start | bytes 786440 | tf_op jit(solution)/shard_map/ppermute | solution.py:756
  12.9 21.4 %collective-permute-start.1 = (bf16[2,64,1024]{2,1,0:T(8,128)(2,1)S(1)}, bf16[2,64,1024]{2,1,0:T(8,128)(2,1)}, u32[]{:S(2)}, u32[]{:S(2)}) collective-permute-start(bf16[2,64,1024]{2,1,0:T(8,128)(2,1)S(1)} %copy-done.22), channel_id=1, source_target_pairs={{0,2},{1,3},{2,0},{3,1},{4,6},{5,7},{6,4},{7,5},{8,10},{9,11},{10,... | collective-permute-start | bytes 786440 | tf_op jit(solution)/shard_map/ppermute | solution.py:756
  15.6 18.7 %collective-permute-start.2 = (bf16[2,64,1024]{2,1,0:T(8,128)(2,1)S(1)}, bf16[2,64,1024]{2,1,0:T(8,128)(2,1)S(1)}, u32[]{:S(2)}, u32[]{:S(2)}) collective-permute-start(bf16[2,64,1024]{2,1,0:T(8,128)(2,1)S(1)} %copy-done.22), channel_id=1, source_target_pairs={{0,3},{1,0},{2,1},{3,2},{4,7},{5,4},{6,5},{7,6},{8,11},{9,8},{10,9... | collective-permute-start | bytes 786440 | tf_op jit(solution)/shard_map/ppermute | solution.py:756
  17.0 17.2 %collective-permute-start.3 = (bf16[2,64,1024]{2,1,0:T(8,128)(2,1)S(1)}, bf16[2,64,1024]{2,1,0:T(8,128)(2,1)S(1)}, u32[]{:S(2)}, u32[]{:S(2)}) collective-permute-start(bf16[2,64,1024]{2,1,0:T(8,128)(2,1)S(1)} %copy-done.13), channel_id=1, source_target_pairs={{0,1},{1,2},{2,3},{3,0},{4,5},{5,6},{6,7},{7,4},{8,9},{9,10},{10,1... | collective-permute-start | bytes 786440 | tf_op jit(solution)/shard_map/ppermute | solution.py:756
  17.6 20.9 %collective-permute-start.4 = (bf16[2,64,1024]{2,1,0:T(8,128)(2,1)S(1)}, bf16[2,64,1024]{2,1,0:T(8,128)(2,1)S(1)}, u32[]{:S(2)}, u32[]{:S(2)}) collective-permute-start(bf16[2,64,1024]{2,1,0:T(8,128)(2,1)S(1)} %copy-done.13), channel_id=1, source_target_pairs={{0,2},{1,3},{2,0},{3,1},{4,6},{5,7},{6,4},{7,5},{8,10},{9,11},{10,... | collective-permute-start | bytes 786440 | tf_op jit(solution)/shard_map/ppermute | solution.py:756
  18.5 44.0 %all-to-all-start = ((bf16[16,400,128]{2,1,0:T(8,128)(2,1)}), bf16[16,400,128]{2,1,0:T(8,128)(2,1)S(1)}, u32[]{:S(2)}, u32[]{:S(2)}) async-start(bf16[16,400,128]{2,1,0:T(8,128)(2,1)} %broadcast_in_dim.42), calls=%async_computation | async-start | bytes 3276800 | tf_op jit(solution)/shard_map/all_to_all | solution.py:831
  24.4 427.6 %reduce-scatter.2.cloned.1.call-start = ((), (), s32[]{:S(2)}) async-start(), calls=%async_computation.3 | async-start | bytes 13369344 | tf_op jit(solution)/shard_map/reduce_scatter | solution.py:935
  62.5 22.2 %collective-permute-start.6 = (bf16[8,400,128]{2,1,0:T(8,128)(2,1)S(1)}, bf16[8,400,128]{2,1,0:T(8,128)(2,1)S(1)}, u32[]{:S(2)}, u32[]{:S(2)}) collective-permute-start(bf16[8,400,128]{2,1,0:T(8,128)(2,1)S(1)} %constant_dynamic-slice_fusion), channel_id=1, source_target_pairs={{0,1},{1,2},{2,3},{3,0},{4,5},{5,6},{6,7},{7,4},{8,9},{9,10},{10,1... | collective-permute-start | bytes 2457608 | tf_op jit(solution)/shard_map/ppermute | solution.py:756
  65.2 21.0 %collective-permute-start.9 = (bf16[8,400,128]{2,1,0:T(8,128)(2,1)S(1)}, bf16[8,400,128]{2,1,0:T(8,128)(2,1)S(1)}, u32[]{:S(2)}, u32[]{:S(2)}) collective-permute-start(bf16[8,400,128]{2,1,0:T(8,128)(2,1)S(1)} %constant_dynamic-slice_fusion), channel_id=1, source_target_pairs={{0,3},{1,0},{2,1},{3,2},{4,7},{5,4},{6,5},{7,6},{8,11},{9,8},{10,9... | collective-permute-start | bytes 2457608 | tf_op jit(solution)/shard_map/ppermute | solution.py:756
  138.3 17.7 %collective-permute-start.17 = (bf16[64,1024]{1,0:T(8,128)(2,1)S(1)}, bf16[64,1024]{1,0:T(8,128)(2,1)S(1)}, u32[]{:S(2)}, u32[]{:S(2)}) collective-permute-start(bf16[64,1024]{1,0:T(8,128)(2,1)S(1)} %add_convert_fusion.3.refs_14_), channel_id=1, source_target_pairs={{0,64},{1,65},{2,66},{3,67},{4,68},{5,69},{6,70},{7,71},{8,72},{9,... | collective-permute-start | bytes 393224 | tf_op jit(solution)/shard_map/ppermute | solution.py:774
  139.6 16.5 %collective-permute-start.18 = (bf16[64,1024]{1,0:T(8,128)(2,1)S(1)}, bf16[64,1024]{1,0:T(8,128)(2,1)S(1)}, u32[]{:S(2)}, u32[]{:S(2)}) collective-permute-start(bf16[64,1024]{1,0:T(8,128)(2,1)S(1)} %add_convert_fusion.3.refs_14_), channel_id=1, source_target_pairs={{0,65},{1,66},{2,67},{3,64},{4,69},{5,70},{6,71},{7,68},{8,73},{9,... | collective-permute-start | bytes 393224 | tf_op jit(solution)/shard_map/ppermute | solution.py:774
  140.9 15.2 %collective-permute-start.19 = (bf16[64,1024]{1,0:T(8,128)(2,1)S(1)}, bf16[64,1024]{1,0:T(8,128)(2,1)S(1)}, u32[]{:S(2)}, u32[]{:S(2)}) collective-permute-start(bf16[64,1024]{1,0:T(8,128)(2,1)S(1)} %add_convert_fusion.3.refs_14_), channel_id=1, source_target_pairs={{0,66},{1,67},{2,64},{3,65},{4,70},{5,71},{6,68},{7,69},{8,74},{9,... | collective-permute-start | bytes 393224 | tf_op jit(solution)/shard_map/ppermute | solution.py:774
  179.4 19.2 %collective-permute-start.24 = (bf16[64,1024]{1,0:T(8,128)(2,1)S(1)}, bf16[64,1024]{1,0:T(8,128)(2,1)S(1)}, u32[]{:S(2)}, u32[]{:S(2)}) collective-permute-start(bf16[64,1024]{1,0:T(8,128)(2,1)S(1)} %add_convert_fusion.2), channel_id=1, source_target_pairs={{0,64},{1,65},{2,66},{3,67},{4,68},{5,69},{6,70},{7,71},{8,72},{9,... | collective-permute-start | bytes 393224 | tf_op jit(solution)/shard_map/ppermute | solution.py:774
  185.9 14.7 %collective-permute-start.25 = (bf16[64,1024]{1,0:T(8,128)(2,1)S(1)}, bf16[64,1024]{1,0:T(8,128)(2,1)S(1)}, u32[]{:S(2)}, u32[]{:S(2)}) collective-permute-start(bf16[64,1024]{1,0:T(8,128)(2,1)S(1)} %add_convert_fusion.2), channel_id=1, source_target_pairs={{0,65},{1,66},{2,67},{3,64},{4,69},{5,70},{6,71},{7,68},{8,73},{9,... | collective-permute-start | bytes 393224 | tf_op jit(solution)/shard_map/ppermute | solution.py:774
  243.3 39.6 %collective-permute-start.46 = (bf16[64,1024]{1,0:T(8,128)(2,1)S(1)}, bf16[64,1024]{1,0:T(8,128)(2,1)S(1)}, u32[]{:S(2)}, u32[]{:S(2)}) collective-permute-start(bf16[64,1024]{1,0:T(8,128)(2,1)S(1)} %copy-done.77), channel_id=1, source_target_pairs={{64,0},{65,1},{66,2},{67,3},{68,4},{69,5},{70,6},{71,7},{72,8},{73... | collective-permute-start | bytes 393224 | tf_op jit(solution)/shard_map/ppermute | solution.py:774
  244.6 38.3 %collective-permute-start.47 = (bf16[64,1024]{1,0:T(8,128)(2,1)S(1)}, bf16[64,1024]{1,0:T(8,128)(2,1)S(1)}, u32[]{:S(2)}, u32[]{:S(2)}) collective-permute-start(bf16[64,1024]{1,0:T(8,128)(2,1)S(1)} %copy-done.77), channel_id=1, source_target_pairs={{64,1},{65,2},{66,3},{67,0},{68,5},{69,6},{70,7},{71,4},{72,9},{73... | collective-permute-start | bytes 393224 | tf_op jit(solution)/shard_map/ppermute | solution.py:774
  245.9 39.8 %collective-permute-start.48 = (bf16[64,1024]{1,0:T(8,128)(2,1)S(1)}, bf16[64,1024]{1,0:T(8,128)(2,1)S(1)}, u32[]{:S(2)}, u32[]{:S(2)}) collective-permute-start(bf16[64,1024]{1,0:T(8,128)(2,1)S(1)} %copy-done.77), channel_id=1, source_target_pairs={{64,2},{65,3},{66,0},{67,1},{68,6},{69,7},{70,4},{71,5},{72,10},{7... | collective-permute-start | bytes 393224 | tf_op jit(solution)/shard_map/ppermute | solution.py:774
  247.5 38.2 %collective-permute-start.49 = (bf16[64,1024]{1,0:T(8,128)(2,1)S(1)}, bf16[64,1024]{1,0:T(8,128)(2,1)S(1)}, u32[]{:S(2)}, u32[]{:S(2)}) collective-permute-start(bf16[64,1024]{1,0:T(8,128)(2,1)S(1)} %copy-done.77), channel_id=1, source_target_pairs={{64,3},{65,0},{66,1},{67,2},{68,7},{69,4},{70,5},{71,6},{72,11},{7... | collective-permute-start | bytes 393224 | tf_op jit(solution)/shard_map/ppermute | solution.py:774
  352.1 14.4 %collective-permute-start.53 = (bf16[64,1024]{1,0:T(8,128)(2,1)S(1)}, bf16[64,1024]{1,0:T(8,128)(2,1)S(1)}, u32[]{:S(2)}, u32[]{:S(2)}) collective-permute-start(bf16[64,1024]{1,0:T(8,128)(2,1)S(1)} %copy-done.19), channel_id=1, source_target_pairs={{0,1},{1,2},{2,3},{3,0},{4,5},{5,6},{6,7},{7,4},{8,9},{9,10},{10,1... | collective-permute-start | bytes 393224 | tf_op jit(solution)/shard_map/ppermute | solution.py:756
  361.6 21.0 %collective-permute-start.63 = (bf16[64,1024]{1,0:T(8,128)(2,1)}, bf16[64,1024]{1,0:T(8,128)(2,1)S(1)}, u32[]{:S(2)}, u32[]{:S(2)}) collective-permute-start(bf16[64,1024]{1,0:T(8,128)(2,1)} %get-tuple-element.243.refs_14_.refs_1_), channel_id=1, source_target_pairs={{0,1},{1,2},{2,3},{3,0},{4,5},{5,6},{6,7},{7,4},{8,9},{9,10},{10,1... | collective-permute-start | bytes 393224 | tf_op jit(solution)/shard_map/ppermute | solution.py:756
  363.6 19.1 %collective-permute-start.64 = (bf16[64,1024]{1,0:T(8,128)(2,1)}, bf16[64,1024]{1,0:T(8,128)(2,1)S(1)}, u32[]{:S(2)}, u32[]{:S(2)}) collective-permute-start(bf16[64,1024]{1,0:T(8,128)(2,1)} %get-tuple-element.243.refs_14_.refs_1_), channel_id=1, source_target_pairs={{0,2},{1,3},{2,0},{3,1},{4,6},{5,7},{6,4},{7,5},{8,10},{9,11},{10,... | collective-permute-start | bytes 393224 | tf_op jit(solution)/shard_map/ppermute | solution.py:756
  366.4 16.2 %collective-permute-start.65 = (bf16[64,1024]{1,0:T(8,128)(2,1)}, bf16[64,1024]{1,0:T(8,128)(2,1)S(1)}, u32[]{:S(2)}, u32[]{:S(2)}) collective-permute-start(bf16[64,1024]{1,0:T(8,128)(2,1)} %get-tuple-element.243.refs_14_.refs_1_), channel_id=1, source_target_pairs={{0,3},{1,0},{2,1},{3,2},{4,7},{5,4},{6,5},{7,6},{8,11},{9,8},{10,9... | collective-permute-start | bytes 393224 | tf_op jit(solution)/shard_map/ppermute | solution.py:756
  405.1 36.5 %all-to-all-start.1 = ((bf16[16,448,128]{2,1,0:T(8,128)(2,1)}), bf16[16,448,128]{2,1,0:T(8,128)(2,1)S(1)}, u32[]{:S(2)}, u32[]{:S(2)}) async-start(bf16[16,448,128]{2,1,0:T(8,128)(2,1)} %attention_weight_grads.1), calls=%async_computation.1 | async-start | bytes 3670016 | tf_op jit(solution)/shard_map/all_to_all | solution.py:957
  (127 other events, 874.9 us)
Sparse Core Ops, SparseCore 0:
  9.8 91.9 all-gather.2
  345.2 104.3 reduce-scatter.1
where the time goes:
time: 470 us; the launch traced here: 462 us
  Pallas kernels  166 us (35%)
  waiting for transfers between devices  123 us (26%)
  starting transfers between devices  115 us (24%)
  local copies, waits for them, and re-layouts  25.9 us (6%)
  other arithmetic  16.2 us (3%)
  between operations  15.3 us (3%)
    ppermute x49, starting transfers between devices, moved(): lax.ppermute(array, 'tensor', [(i, (i + shift) % 4) for i in range(4)])  73.7 us
    ppermute x49, waiting for transfers between devices, moved(): lax.ppermute(array, 'tensor', [(i, (i + shift) % 4) for i in range(4)])  49.3 us
    ppermute x16, waiting for transfers between devices, across(): lax.ppermute(rows, ('pipe', 'tensor'), [(start + i, end + (i + s) % 4) fo...  38.8 us
    pallas_call x4, Pallas kernels, attention_backward(): pl.pallas_call(lambda *refs: attention_backward_kernel(len(after), *refs)...  38.4 us
    pallas_call x4, Pallas kernels, attention_forward(): pl.pallas_call(lambda *refs: attention_forward_kernel(len(after), *refs),...  32.6 us
    pallas_call x4, Pallas kernels, experts_backward(): pl.pallas_call(lambda *refs: experts_backward_kernel(len(after), *refs),...  31.8 us
    ppermute x16, starting transfers between devices, across(): lax.ppermute(rows, ('pipe', 'tensor'), [(start + i, end + (i + s) % 4) fo...  29.2 us
    pallas_call x4, Pallas kernels, experts_forward(): pl.pallas_call(lambda *refs: experts_forward_kernel(len(after), *refs), g...  27 us
  transfers between devices with their start and end apart: 73, of which 28 were waited for; matrix products, arithmetic and copies ran while one was open for 6% of the time, Pallas kernels for 22%

commit v1 on v0

--- a/solution.py
+++ b/solution.py
@@ -15,7 +15,8 @@
 BF = jnp.bfloat16
 F32 = jnp.float32
 VMEM_LIMIT = 56 * 1024 * 1024
-PER = 8
+PER = 4
+PER_BACK = 8
 PER_GRAD = 4
 LANES = 128
 
@@ -171,72 +172,77 @@
 def attention_forward_kernel(n_after, sref, *refs):
     pieces, refs = refs[:4], refs[4:]
     sources, refs = refs[:9], refs[9 + n_after :]
-    (
-        gains_ref, cos_ref, sin_ref, bias_ref, picked_ref, router_ref,
-        a_ref, xown_ref, qkv_ref, o_ref, lse_ref, hown_ref, b_ref, gates_ref,
-        hidden, buffers, sems,
-    ) = refs
+
+    @pl.when(sref[1] > 0)
+    def _():
+        attention_part(sref, pieces, sources, *refs)
+
+
+def attention_part(
+    sref, pieces, sources,
+    gains_ref, cos_ref, sin_ref, bias_ref, picked_ref, router_ref,
+    a_ref, xown_ref, qkv_ref, o_ref, lse_ref, hown_ref, b_ref, gates_ref,
+    hidden, buffers, sems,
+):
     me = sref[0]
     group, width = b_ref.shape
     shard = xown_ref.shape[0]
 
-    @pl.when(sref[1] > 0)
-    def _():
-        copies = fetches(sref[2], sources, buffers, sems)
-        for copy in copies[0]:
+    copies = fetches(sref[2], sources, buffers, sems)
+    for copy in copies[0]:
+        copy.start()
+    assemble(me, pieces, b_ref)
+    entering = b_ref[...].astype(F32)
+    a_ref[...] = (entering * rms_scale(entering) * gains_ref[0:1, :]).astype(BF)
+    xown_ref[...] = pieces[0][...]
+    hidden[...] = entering
+    cos = jnp.concatenate([cos_ref[...]] * 3, axis=1)
+    sin = jnp.concatenate([sin_ref[...]] * 3, axis=1)
+    bias = bias_ref[...]
+    lanes = lax.broadcasted_iota(jnp.int32, (group, LANES), 1)
+    lse_all = jnp.zeros((group, LANES), F32)
+    for step in range(4):
+        for copy in copies[step]:
+            copy.wait()
+        for copy in copies[step + 1] if step < 3 else []:
             copy.start()
-        assemble(me, pieces, b_ref)
-        entering = b_ref[...].astype(F32)
-        a_ref[...] = (entering * rms_scale(entering) * gains_ref[0:1, :]).astype(BF)
-        xown_ref[...] = pieces[0][...]
-        hidden[...] = entering
-        cos = jnp.concatenate([cos_ref[...]] * 3, axis=1)
-        sin = jnp.concatenate([sin_ref[...]] * 3, axis=1)
-        bias = bias_ref[...]
-        lanes = lax.broadcasted_iota(jnp.int32, (group, LANES), 1)
-        lse_all = jnp.zeros((group, LANES), F32)
-        for step in range(4):
-            for copy in copies[step]:
-                copy.wait()
-            for copy in copies[step + 1] if step < 3 else []:
-                copy.start()
-            w_qkv, w_out = group_weights(buffers, step)
-            qkv = dot(a_ref[...], w_qkv)
-            qk = qkv[:, :384]
-            turned = qk * cos + swap_halves(qk) * sin
-            q = (turned[:, :256] * HD**-0.5).astype(BF)
-            k = turned[:, 256:].astype(BF)
-            v = qkv[:, 384:].astype(BF)
-            qkv_ref[step, :, :256] = q
-            qkv_ref[step, :, 256:384] = k
-            qkv_ref[step, :, 384:] = v
-            outs = []
-            for head in range(4):
-                kv = head // 2
-                scores = dot_nt(
-                    q[:, head * HD : (head + 1) * HD], k[:, kv * HD : (kv + 1) * HD]
-                )
-                scores = scores + bias
-                peak = jnp.max(scores, axis=1, keepdims=True)
-                soft = jnp.exp(scores - peak)
-                total = jnp.sum(soft, axis=1, keepdims=True)
-                lse_all = jnp.where(lanes == 4 * step + head, peak + jnp.log(total), lse_all)
-                soft = (soft * (1.0 / total)).astype(BF)
-                outs.append(dot(soft, v[:, kv * HD : (kv + 1) * HD]))
-            mixed = jnp.concatenate(outs, axis=1).astype(BF)
-            if step == 0:
-                o_ref[...] = mixed
-            hidden[...] += dot_nt(mixed, w_out)
-        lse_ref[...] = lse_all
-        rows = hidden[...]
-        normed = (rows * rms_scale(rows) * gains_ref[1:2, :]).astype(BF)
-        b_ref[...] = normed
-        hown_ref[...] = hidden[own_rows(me, shard), :]
-        logits = dot(normed, router_ref[...])[:, :E]
-        picked = picked_ref[...]
-        peak = jnp.max(jnp.where(picked > 0, logits, -1e30), axis=1, keepdims=True)
-        powers = jnp.where(picked > 0, jnp.exp(jnp.minimum(logits - peak, 0.0)), 0.0)
-        gates_ref[...] = powers / jnp.sum(powers, axis=1, keepdims=True)
+        w_qkv, w_out = group_weights(buffers, step)
+        qkv = dot(a_ref[...], w_qkv)
+        qk = qkv[:, :384]
+        turned = qk * cos + swap_halves(qk) * sin
+        q = (turned[:, :256] * HD**-0.5).astype(BF)
+        k = turned[:, 256:].astype(BF)
+        v = qkv[:, 384:].astype(BF)
+        qkv_ref[step, :, :256] = q
+        qkv_ref[step, :, 256:384] = k
+        qkv_ref[step, :, 384:] = v
+        outs = []
+        for head in range(4):
+            kv = head // 2
+            scores = dot_nt(
+                q[:, head * HD : (head + 1) * HD], k[:, kv * HD : (kv + 1) * HD]
+            )
+            scores = scores + bias
+            peak = jnp.max(scores, axis=1, keepdims=True)
+            soft = jnp.exp(scores - peak)
+            total = jnp.sum(soft, axis=1, keepdims=True)
+            lse_all = jnp.where(lanes == 4 * step + head, peak + jnp.log(total), lse_all)
+            soft = (soft * (1.0 / total)).astype(BF)
+            outs.append(dot(soft, v[:, kv * HD : (kv + 1) * HD]))
+        mixed = jnp.concatenate(outs, axis=1).astype(BF)
+        if step == 0:
+            o_ref[...] = mixed
+        hidden[...] += dot_nt(mixed, w_out)
+    lse_ref[...] = lse_all
+    rows = hidden[...]
+    normed = (rows * rms_scale(rows) * gains_ref[1:2, :]).astype(BF)
+    b_ref[...] = normed
+    hown_ref[...] = hidden[own_rows(me, shard), :]
+    logits = dot(normed, router_ref[...])[:, :E]
+    picked = picked_ref[...]
+    peak = jnp.max(jnp.where(picked > 0, logits, -1e30), axis=1, keepdims=True)
+    powers = jnp.where(picked > 0, jnp.exp(jnp.minimum(logits - peak, 0.0)), 0.0)
+    gates_ref[...] = powers / jnp.sum(powers, axis=1, keepdims=True)
 
 
 def attention_forward(scalars, pieces, gains, tables, picked, w_attn, router, after):
@@ -285,44 +291,69 @@
     )(scalars, *pieces, *w_attn, *after, *smalls)
 
 
+def chunk(number):
+    return pl.ds(PER * number, PER)
+
+
 def experts_forward_kernel(n_after, sref, *refs):
-    (b_ref, gate_ref, w_ref, *refs) = refs[n_after:]
-    pieces, (gu_ref, total) = refs[:4], refs[4:]
-    step = pl.program_id(0)
-    width = b_ref.shape[1]
-    ff = w_ref.shape[-1]
+    w_ref, b_ref, gate_ref, *refs = refs[n_after:]
+    pieces, (gu_ref, total, held, gu_held, sems) = refs[:4], refs[4:]
 
     @pl.when(sref[1] > 0)
     def _():
-        b = b_ref[...]
-        gates = gate_ref[...]
+        come, leave = experts_copies(w_ref, gu_ref, held, gu_held, sems)
+        come[0].start()
+        come[1].start()
+        experts_part(sref, come, leave, b_ref, gate_ref, pieces, total, held, gu_held)
+
+
+def experts_copies(w_ref, gu_ref, held, gu_held, sems):
+    chunks = w_ref.shape[2] // PER
+    come = [
+        pltpu.make_async_copy(
+            w_ref.at[:, :, chunk(c)], held.at[:, :, chunk(c)], sems.at[c]
+        )
+        for c in range(chunks)
+    ]
+    leave = [
+        pltpu.make_async_copy(gu_held.at[chunk(c)], gu_ref.at[chunk(c)], sems.at[chunks + c])
+        for c in range(chunks)
+    ]
+    return come, leave
+
+
+def experts_part(sref, come, leave, b_ref, gate_ref, pieces, total, held, gu_held):
+    group, width = b_ref.shape
+    ff = held.shape[-1]
+    chunks = len(come)
+    gates = gate_ref[...]
+    for c in range(chunks):
+        come[c].wait()
+        if c + 2 < chunks:
+            come[c + 2].start()
         acts, downs = [], []
-        for j in range(PER):
+        for e in range(PER * c, PER * (c + 1)):
             gate_up = jnp.concatenate(
-                [w_ref[:, 0, j].reshape(width, ff), w_ref[:, 1, j].reshape(width, ff)], axis=1
+                [held[:, 0, e].reshape(width, ff), held[:, 1, e].reshape(width, ff)], axis=1
             )
-            both = dot(b, gate_up)
-            gu_ref[j] = both.astype(BF)
+            both = dot(b_ref[...], gate_up)
+            gu_held[e] = both.astype(BF)
             gate_pre, up_pre = both[:, :ff], both[:, ff:]
             act = gate_pre * jax.nn.sigmoid(gate_pre) * up_pre
-            acts.append((act * column(gates, step * PER + j)).astype(BF))
-            downs.append(w_ref[:, 2, j].reshape(width, ff))
+            acts.append((act * gates[:, e : e + 1]).astype(BF))
+            downs.append(held[:, 2, e].reshape(width, ff))
+        leave[c].start()
         out = dot_nt(jnp.concatenate(acts, axis=1), jnp.concatenate(downs, axis=1))
-
-        @pl.when(step == 0)
-        def _():
+        if c == 0:
             total[...] = out
-
-        @pl.when(step > 0)
-        def _():
+        else:
             total[...] += out
-
-        @pl.when(step == pl.num_programs(0) - 1)
-        def _():
-            rows = b_ref.shape[0] // 4
-            for shift in range(4):
-                place = own_rows(lax.rem(sref[0] + shift, 4), rows)
-                pieces[shift][...] = total[place, :].astype(BF)
+    rows = group // 4
+    for shift in range(4):
+        place = own_rows(lax.rem(sref[0] + shift, 4), rows)
+        pieces[shift][...] = total[place, :].astype(BF)
+    for c in range(chunks):
+        leave[c].wait()
 
 
 def experts_forward(scalars, b, gates, w, after):
@@ -333,16 +364,15 @@
         lambda *refs: experts_forward_kernel(len(after), *refs),
         grid_spec=pltpu.PrefetchScalarGridSpec(
             num_scalar_prefetch=1,
-            grid=(experts // PER,),
-            in_specs=anywhere(len(after))
-            + [
-                whole((group, width)),
-                whole((group, experts)),
-                pl.BlockSpec((dp, 3, PER, dr, ff), lambda i, s: (0, 0, i * s[1], 0, 0)),
+            grid=(1,),
+            in_specs=anywhere(len(after) + 1) + [whole((group, width)), whole((group, experts))],
+            out_specs=[whole(piece)] * 4 + anywhere(1),
+            scratch_shapes=[
+                pltpu.VMEM((group, width), F32),
+                pltpu.VMEM(w.shape, BF),
+                pltpu.VMEM((experts, group, 2 * ff), BF),
+                pltpu.SemaphoreType.DMA((2 * experts // PER,)),
             ],
-            out_specs=[whole(piece)] * 4
-            + [pl.BlockSpec((PER, group, 2 * ff), lambda i, s: (i * s[1], 0, 0))],
-            scratch_shapes=[pltpu.VMEM((group, width), F32)],
         ),
         out_shape=[jax.ShapeDtypeStruct(piece, BF)] * 4
         + [jax.ShapeDtypeStruct((experts, group, 2 * ff), BF)],
@@ -353,7 +383,72 @@
             transcendentals=experts * group * ff,
         ),
         name="experts_forward",
-    )(scalars, *after, b, gates, w)
+    )(scalars, *after, w, b, gates)
+
+
+def layer_forward_kernel(n_after, sref, *refs):
+    pieces, refs = refs[:4], refs[4:]
+    sources, refs = refs[:9], refs[9:]
+    w_ref, refs = refs[0], refs[1 + n_after :]
+    smalls, refs = refs[:6], refs[6:]
+    kept, refs = refs[:8], refs[8:]
+    parts, refs = refs[:4], refs[4:]
+    gu_ref, total, buffers, held, gu_held, sems, expert_sems = refs
+
+    @pl.when(sref[1] > 0)
+    def _():
+        come, leave = experts_copies(w_ref, gu_ref, held, gu_held, expert_sems)
+        come[0].start()
+        come[1].start()
+        attention_part(sref, pieces, sources, *smalls, *kept, total, buffers, sems)
+        experts_part(sref, come, leave, kept[6], kept[7], parts, total, held, gu_held)
+
+
+def layer_forward(scalars, pieces, gains, tables, picked, w_attn, router, w, after):
+    shard, width = pieces[0].shape
+    group = 4 * shard
+    dp, _, experts, dr, ff = w.shape
+    smalls = [gains, *tables, picked, router]
+    outs = [
+        ((group, width), BF),
+        ((shard, width), BF),
+        ((4, group, 512), BF),
+        ((group, 256), BF),
+        ((group, LANES), F32),
+        ((shard, width), F32),
+        ((group, width), BF),
+        ((group, E), F32),
+    ] + [((shard, width), BF)] * 4
+    gu_shape = (experts, group, 2 * ff)
+    out = pl.pallas_call(
+        lambda *refs: layer_forward_kernel(len(after), *refs),
+        grid_spec=pltpu.PrefetchScalarGridSpec(
+            num_scalar_prefetch=1,
+            grid=(1,),
+            in_specs=[whole(x.shape) for x in pieces]
+            + anywhere(10 + len(after))
+            + [whole(x.shape) for x in smalls],
+            out_specs=[whole(shape) for shape, _ in outs] + anywhere(1),
+            scratch_shapes=[
+                pltpu.VMEM((group, width), F32),
+                pltpu.VMEM((4, dp, 400, LANES), BF),
+                pltpu.VMEM(w.shape, BF),
+                pltpu.VMEM(gu_shape, BF),
+                pltpu.SemaphoreType.DMA((9,)),
+                pltpu.SemaphoreType.DMA((2 * experts // PER,)),
+            ],
+        ),
+        out_shape=[jax.ShapeDtypeStruct(shape, kind) for shape, kind in outs]
+        + [jax.ShapeDtypeStruct(gu_shape, BF)],
+        compiler_params=params(),
+        cost_estimate=pl.CostEstimate(
+            flops=2 * group * width * (768 * 4 + ff * 3 * experts) + 64 * group * group * HD,
+            bytes_accessed=width * 768 * 8 + w.size * 2 + 8 * group * width * 2,
+            transcendentals=16 * group * group + experts * group * ff,
+        ),
+        name="layer_forward",
+    )(scalars, *pieces, *w_attn, w, *after, *smalls)
+    return list(out[:8]), list(out[8:12]), out[12]
 
 
 def experts_backward_kernel(n_after, sref, *refs):
@@ -375,14 +470,14 @@
         grad = grad_ref[...]
         gates = gate_ref[...]
         down = jnp.concatenate(
-            [w_ref[:, 2, j].reshape(width, ff) for j in range(PER)], axis=1
+            [w_ref[:, 2, j].reshape(width, ff) for j in range(PER_BACK)], axis=1
         )
         turned = dot(grad, down)
         lanes = lax.broadcasted_iota(jnp.int32, (group, LANES), 1)
         grad_gate = jnp.zeros((group, LANES), F32)
         out = None
-        for j in range(PER):
-            expert = step * PER + j
+        for j in range(PER_BACK):
+            expert = step * PER_BACK + j
             back = turned[:, j * ff : (j + 1) * ff]
             both = gu_ref[j].astype(F32)
             gate_pre, up_pre = both[:, :ff], both[:, ff:]
@@ -433,19 +528,19 @@
         lambda *refs: experts_backward_kernel(len(after), *refs),
         grid_spec=pltpu.PrefetchScalarGridSpec(
             num_scalar_prefetch=1,
-            grid=(experts // PER,),
+            grid=(experts // PER_BACK,),
             in_specs=anywhere(len(after))
             + [whole(x.shape) for x in given]
             + [
                 whole((group, experts)),
-                pl.BlockSpec((PER, group, 2 * ff), lambda i, s: (i * s[1], 0, 0)),
-                pl.BlockSpec((dp, 3, PER, dr, ff), lambda i, s: (0, 0, i * s[1], 0, 0)),
+                pl.BlockSpec((PER_BACK, group, 2 * ff), lambda i, s: (i * s[1], 0, 0)),
+                pl.BlockSpec((dp, 3, PER_BACK, dr, ff), lambda i, s: (0, 0, i * s[1], 0, 0)),
             ],
             out_specs=[whole(piece)] * 4
             + [
                 whole((group, width)),
-                pl.BlockSpec((PER, group, 2 * ff), lambda i, s: (i * s[1], 0, 0)),
-                pl.BlockSpec((group, PER * ff), lambda i, s: (0, i * s[1])),
+                pl.BlockSpec((PER_BACK, group, 2 * ff), lambda i, s: (i * s[1], 0, 0)),
+                pl.BlockSpec((group, PER_BACK * ff), lambda i, s: (0, i * s[1])),
             ],
             scratch_shapes=[pltpu.VMEM((group, width), F32), pltpu.VMEM((group, LANES), F32)],
         ),
@@ -827,23 +922,24 @@
         axis=0,
     )
     w_own = jnp.broadcast_to(piece[None], (dp,) + piece.shape)
-    w_own, inputs, cotangent = lax.optimization_barrier((w_own, inputs, cotangent))
     w_own = lax.all_to_all(w_own, "dp", 0, 0, tiled=True)
     pieces_w = jnp.stack([w_gate[0], w_up[0], w_down[0].transpose(0, 2, 1)])
     w_experts = lax.all_gather(pieces_w, "dp", axis=0)
+    tables = [tables_of(doc_lengths[m, 0], group) for m in range(micro)]
+    tables, inputs, cotangent = lax.optimization_barrier((tables, inputs, cotangent))
     rows_in, rows_cot = to_all(inputs), to_all(cotangent)
     rows_in, rows_cot, w_own = lax.optimization_barrier((rows_in, rows_cot, w_own))
+    rows_in = [[part[m] for part in rows_in] for m in range(micro)]
+    rows_cot = [[part[m] for part in rows_cot] for m in range(micro)]
     half, quarter = dp // 2, dp // 4
     mine = lax.dynamic_slice_in_dim(w_own, core * half, half, 0)
     w_next, w_last = moved(mine, 1), moved(mine, 3)
     w_over = [moved(w_next[:quarter], 1), moved(w_last[quarter:], 3)]
     other = [swapped(x, dp) for x in (w_next, w_last, *w_over)]
     w_attn = [w_own, w_next, other[0], *w_over, other[2], other[3], w_last, other[1]]
+    w_attn, rows_in, rows_cot = lax.optimization_barrier((w_attn, rows_in, rows_cot))
     router, gains = smalls_of(scalars[0], w_attn)
 
-    rows_in = [[part[m] for part in rows_in] for m in range(micro)]
-    rows_cot = [[part[m] for part in rows_cot] for m in range(micro)]
-    tables = [tables_of(doc_lengths[m, 0], group) for m in range(micro)]
     ids = jnp.arange(E, dtype=jnp.int32)
     picked = jnp.any(routes[0][..., None] == ids, axis=2).astype(F32)
 
@@ -866,6 +962,15 @@
         b, gates = saves[s][m][6:8]
         *parts, gu = experts_forward(scalars[s], b, gates, w_experts, after)
         saves[s][m].append(gu)
+        after = [gu]
+        return parts
+
+    def layer(s, m, pieces):
+        nonlocal after
+        kept, parts, gu = layer_forward(
+            scalars[s], pieces, gains, tables[m], picked[m], w_attn, router, w_experts, after
+        )
+        saves[s][m] = [*kept, gu]
         after = [gu]
         return parts
 
@@ -907,19 +1012,17 @@
     first_in = across(first_out, True)
     after = [first_out]
     attend(0, 1, rows_in[1])
-    attend(1, 0, first_in)
+    late = [layer(1, 0, first_in)]
     second_out = layer_sum(expert(0, 1), saves[0][1][5])
     second_in = across(second_out, True)
-    late = [expert(1, 0)]
     expert_back(1, 0, rows_cot[0])
-    attend(1, 1, second_in)
-    late.append(expert(1, 1))
+    late.append(layer(1, 1, second_in))
     norm_between(1, 0, cotangent[0])
     expert_back(1, 1, rows_cot[1])
     first_back = across(attend_back(1, 0), False)
     norm_between(1, 1, cotangent[1])
+    expert_back(0, 0, first_back)
     second_back = across(attend_back(1, 1), False)
-    expert_back(0, 0, first_back)
     norm_between(0, 0, first_back[0])
     expert_back(0, 1, second_back)
     joined = firsts[0] + firsts[1]

time: 470 us -> 460 us (0.979)
  starting transfers between devices: 115 us -> 101 us
    all_to_all x1, waiting for transfers between devices: 21.9 us -> 0.01 us  [per_device(): w_own = lax.all_to_all(w_own, 'dp', 0, 0, tiled=True)]
    ppermute x49, waiting for transfers between devices: 49.3 us -> 66.8 us  [moved(): lax.ppermute(array, 'tensor', [(i, (i + shift) % 4) for i in range(4)])]
    pallas_call x0 -> x2, Pallas kernels: none -> 8.42 us  [layer_forward(): pl.pallas_call(lambda *refs: layer_forward_kernel(len(after), *refs), gri...]
    ppermute x16, starting transfers between devices: 29.2 us -> 20.9 us  [across(): lax.ppermute(rows, ('pipe', 'tensor'), [(start + i, end + (i + s) % 4) fo...]
    pallas_call x4 -> x2, Pallas kernels: 27 us -> 18.8 us  [experts_forward(): pl.pallas_call(lambda *refs: experts_forward_kernel(len(after), *refs), g...]
    ppermute x49, starting transfers between devices: 73.7 us -> 66.4 us  [moved(): lax.ppermute(array, 'tensor', [(i, (i + shift) % 4) for i in range(4)])]
    ppermute x16, waiting for transfers between devices: 38.8 us -> 44.5 us  [across(): lax.ppermute(rows, ('pipe', 'tensor'), [(start + i, end + (i + s) % 4) fo...]
    pallas_call x4 -> x2, Pallas kernels: 32.6 us -> 36.9 us  [attention_forward(): pl.pallas_call(lambda *refs: attention_forward_kernel(len(after), *refs),...]
  transfers between devices with their start and end apart: 73 -> 73, of which waited for: 28 -> 25; matrix products, arithmetic and copies ran while one was open for 6% -> 5% of each run, Pallas kernels for 22% -> 26%
where the time goes in v1:
time: 460 us; the launch traced here: 452 us
  Pallas kernels  170 us (37%)
  waiting for transfers between devices  124 us (27%)
  starting transfers between devices  101 us (22%)
  local copies, waits for them, and re-layouts  24.7 us (5%)
  other arithmetic  16.9 us (4%)
  between operations  15.6 us (3%)
    ppermute x49, waiting for transfers between devices, moved(): lax.ppermute(array, 'tensor', [(i, (i + shift) % 4) for i in range(4)])  66.8 us
    ppermute x49, starting transfers between devices, moved(): lax.ppermute(array, 'tensor', [(i, (i + shift) % 4) for i in range(4)])  66.4 us
    ppermute x16, waiting for transfers between devices, across(): lax.ppermute(rows, ('pipe', 'tensor'), [(start + i, end + (i + s) % 4) fo...  44.5 us
    pallas_call x4, Pallas kernels, attention_backward(): pl.pallas_call(lambda *refs: attention_backward_kernel(len(after), *refs)...  38.4 us
    pallas_call x2, Pallas kernels, attention_forward(): pl.pallas_call(lambda *refs: attention_forward_kernel(len(after), *refs),...  36.9 us
    pallas_call x4, Pallas kernels, experts_backward(): pl.pallas_call(lambda *refs: experts_backward_kernel(len(after), *refs),...  31.7 us
    ppermute x16, starting transfers between devices, across(): lax.ppermute(rows, ('pipe', 'tensor'), [(start + i, end + (i + s) % 4) fo...  20.9 us
    pallas_call x2, Pallas kernels, experts_forward(): pl.pallas_call(lambda *refs: experts_forward_kernel(len(after), *refs), g...  18.8 us
  transfers between devices with their start and end apart: 73, of which 25 were waited for; matrix products, arithmetic and copies ran while one was open for 5% of the time, Pallas kernels for 26%

profile of v1, /device:TPU:0, one launch (start us, length us, event | category | flops | bytes accessed | tf_op | source)
XLA Modules:
  0.0 451.7 jit_solution(14087577638125450450)
XLA Ops:
  11.2 6.0 %all-to-all-start = ((bf16[16,400,128]{2,1,0:T(8,128)(2,1)}), bf16[16,400,128]{2,1,0:T(8,128)(2,1)S(1)}, u32[]{:S(2)}, u32[]{:S(2)}) async-start(bf16[16,400,128]{2,1,0:T(8,128)(2,1)} %broadcast_in_dim.76), calls=%async_computation | async-start | bytes 3276800 | tf_op jit(solution)/shard_map/all_to_all | solution.py:925
  40.7 4.1 collective-permute-done.3
  44.8 6.6 %collective-permute-done.4 = bf16[2,64,1024]{2,1,0:T(8,128)(2,1)S(1)} collective-permute-done((bf16[2,64,1024]{2,1,0:T(8,128)(2,1)S(1)}, bf16[2,64,1024]{2,1,0:T(8,128)(2,1)S(1)}, u32[]{:S(2)}, u32[]{:S(2)}) %collective-permute-start.4) | collective-permute-done | bytes 262176 | tf_op jit(solution)/shard_map/ppermute | solution.py:851
  58.7 14.7 %collective-permute-done.6.refs_1_.refs_6_ = bf16[8,400,128]{2,1,0:T(8,128)(2,1)S(1)} collective-permute-done((bf16[8,400,128]{2,1,0:T(8,128)(2,1)S(1)}, bf16[8,400,128]{2,1,0:T(8,128)(2,1)S(1)}, u32[]{:S(2)}, u32[]{:S(2)}) %collective-permute-start.6) | collective-permute-done | bytes 819232 | tf_op jit(solution)/shard_map/ppermute | solution.py:851
  78.9 7.5 %collective-permute-done.8.refs_3_.refs_8_ = bf16[4,400,128]{2,1,0:T(8,128)(2,1)S(1)} collective-permute-done((bf16[4,400,128]{2,1,0:T(8,128)(2,1)S(1)}, bf16[4,400,128]{2,1,0:T(8,128)(2,1)S(1)}, u32[]{:S(2)}, u32[]{:S(2)}) %collective-permute-start.8) | collective-permute-done | bytes 409632 | tf_op jit(solution)/shard_map/ppermute | solution.py:851
  93.3 12.4 %attention_forward.2 = (bf16[256,1024]{1,0:T(8,128)(2,1)}, bf16[64,1024]{1,0:T(8,128)(2,1)}, bf16[4,256,512]{2,1,0:T(8,128)(2,1)}, bf16[256,256]{1,0:T(8,128)(2,...) custom-call(s32[3]{0:T(128)} %add_add_fusion.sref.refs_0_, ...), custom_call_target="tpu_custom_call" | custom-call | flops 1879048192 | bytes 9437184 | tf_op jit(solution)/shard_map/attention_forward/pallas_call | solution.py:265
  105.7 9.4 %experts_forward.2 = (bf16[64,1024]{1,0:T(8,128)(2,1)}, bf16[64,1024]{1,0:T(8,128)(2,1)}, bf16[64,1024]{1,0:T(8,128)(2,1)}, bf16[64,1024]{1,0:T(8,128)(2,1)}, bf16[16,256,256]{2,1,0:T(8,128)(2,1)}) custom-call(s32[3]{0:T(128)} %add_add_fusion.sref.refs_0_, bf16[256,1024]{1,0:T(8,128)(2,1)} %get-tuple-element.204.refs_1_.refs_3_.refs_9_.refs_2_, ...), custom_call_target="tpu_custom_call" | custom-call | flops 3221225472 | bytes 14680064 | tf_op jit(solution)/shard_map/experts_forward/pallas_call | solution.py:363
  119.5 5.0 %collective-permute-done.16 = bf16[64,1024]{1,0:T(8,128)(2,1)S(1)} collective-permute-done((bf16[64,1024]{1,0:T(8,128)(2,1)}, bf16[64,1024]{1,0:T(8,128)(2,1)S(1)}, u32[]{:S(2)}, u32[]{:S(2)}) %collective-permute-start.16) | collective-permute-done | bytes 131104 | tf_op jit(solution)/shard_map/ppermute | solution.py:851
  134.0 24.5 %attention_forward.3 = (bf16[256,1024]{1,0:T(8,128)(2,1)}, bf16[64,1024]{1,0:T(8,128)(2,1)}, bf16[4,256,512]{2,1,0:T(8,128)(2,1)}, bf16[256,256]{1,0:T(8,128)(2,...) custom-call(s32[3]{0:T(128)} %add_add_fusion.sref.refs_0_, ...), custom_call_target="tpu_custom_call" | custom-call | flops 1879048192 | bytes 9437184 | tf_op jit(solution)/shard_map/attention_forward/pallas_call | solution.py:265
  163.4 9.4 %experts_forward.3 = (bf16[64,1024]{1,0:T(8,128)(2,1)}, bf16[64,1024]{1,0:T(8,128)(2,1)}, bf16[64,1024]{1,0:T(8,128)(2,1)}, bf16[64,1024]{1,0:T(8,128)(2,1)}, bf16[16,256,256]{2,1,0:T(8,128)(2,1)}) custom-call(s32[3]{0:T(128)} %add_add_fusion.sref.refs_0_, bf16[16,256,256]{2,1,0:T(8,128)(2,1)} %get-tuple-element.224.refs_1_.refs_7_, ...), custom_call_target="tpu_custom_call" | custom-call | flops 3221225472 | bytes 14680064 | tf_op jit(solution)/shard_map/experts_forward/pallas_call | solution.py:363
  189.2 5.5 %experts_backward.4 = (bf16[64,1152]{1,0:T(8,128)(2,1)}, bf16[64,1152]{1,0:T(8,128)(2,1)}, bf16[64,1152]{1,0:T(8,128)(2,1)}, bf16[64,1152]{1,0:T(8,128)(2,1)}, b...) custom-call(s32[3]{0:T(128)} %add_add_fusion.1.refs_0_, ...), custom_call_target="tpu_custom_call" | custom-call | flops 3221225472 | bytes 17825792 | tf_op jit(solution)/shard_map/experts_backward/pallas_call | solution.py:527
  198.7 4.4 layer_forward.3
  212.7 5.4 %experts_backward.5 = (bf16[64,1152]{1,0:T(8,128)(2,1)}, bf16[64,1152]{1,0:T(8,128)(2,1)}, bf16[64,1152]{1,0:T(8,128)(2,1)}, bf16[64,1152]{1,0:T(8,128)(2,1)}, b...) custom-call(s32[3]{0:T(128)} %add_add_fusion.1.refs_0_, ...), custom_call_target="tpu_custom_call" | custom-call | flops 3221225472 | bytes 17825792 | tf_op jit(solution)/shard_map/experts_backward/pallas_call | solution.py:527
  236.6 35.5 %collective-permute-done.40.refs_2_.refs_6_ = bf16[64,1024]{1,0:T(8,128)(2,1)S(1)} collective-permute-done((bf16[64,1024]{1,0:T(8,128)(2,1)}, bf16[64,1024]{1,0:T(8,128)(2,1)S(1)}, u32[]{:S(2)}, u32[]{:S(2)}) %collective-permute-start.40) | collective-permute-done | bytes 131104 | tf_op jit(solution)/shard_map/ppermute | solution.py:869
  275.9 10.5 %experts_backward.6 = (bf16[64,1152]{1,0:T(8,128)(2,1)}, bf16[64,1152]{1,0:T(8,128)(2,1)}, bf16[64,1152]{1,0:T(8,128)(2,1)}, bf16[64,1152]{1,0:T(8,128)(2,1)}, b...) custom-call(s32[3]{0:T(128)} %add_add_fusion.sref.refs_0_, ...), custom_call_target="tpu_custom_call" | custom-call | flops 3221225472 | bytes 17825792 | tf_op jit(solution)/shard_map/experts_backward/pallas_call | solution.py:527
  303.9 7.4 %collective-permute-done.56.refs_2_.refs_6_ = bf16[64,1024]{1,0:T(8,128)(2,1)S(1)} collective-permute-done((bf16[64,1024]{1,0:T(8,128)(2,1)}, bf16[64,1024]{1,0:T(8,128)(2,1)S(1)}, u32[]{:S(2)}, u32[]{:S(2)}) %collective-permute-start.56) | collective-permute-done | bytes 131104 | tf_op jit(solution)/shard_map/ppermute | solution.py:869
  312.1 10.4 %experts_backward.7 = (bf16[64,1152]{1,0:T(8,128)(2,1)}, bf16[64,1152]{1,0:T(8,128)(2,1)}, bf16[64,1152]{1,0:T(8,128)(2,1)}, bf16[64,1152]{1,0:T(8,128)(2,1)}, b...) custom-call(s32[3]{0:T(128)} %add_add_fusion.sref.refs_0_, ...), custom_call_target="tpu_custom_call" | custom-call | flops 3221225472 | bytes 17825792 | tf_op jit(solution)/shard_map/experts_backward/pallas_call | solution.py:527
  322.5 14.4 %expert_weight_grads.1.refs_1_ = bf16[16,3,16,64,128]{4,3,2,1,0:T(8,128)(2,1)} custom-call(s32[3]{0:T(128)} %add_add_fusion.sref.refs_0_, bf16[256,1024]{1,0:T(8,128)(2,1)} %get-tuple-element.290.refs_1_.refs_7_, bf16[256,1024]{1,0:T(8,128)(2,1)} %get-tuple-element.204.refs_1_.refs_3_.refs_9_.refs_2_, ...), custom_call_target="tpu_custom_call" | custom-call | flops 6442450944 | bytes 18874368 | tf_op jit(solution)/shard_map/expert_weight_grads/pallas_call | solution.py:779
  355.6 15.5 %attention_backward.6 = (f32[64,1024]{1,0:T(8,128)}, bf16[64,1024]{1,0:T(8,128)(2,1)}, f32[24,1024]{1,0:T(8,128)}, bf16[256,1024]{1,0:T(8,128)(2,1)}, bf16[256,512]{1,0:T(8,128)(2,1)}) custom-call(s32[3]{0:T(128)} %add_add_fusion.sref.refs_0_, bf16[64,1024]{1,0:T(8,128)(2,1)} %get-tuple-element.288.refs_1_, bf16[64,1024]{1,0:T(8,128)(2,1)} %copy-done.37, ...), custom_call_target="tpu_custom_call" | custom-call | flops 1207959552 | bytes 9437184 | tf_op jit(solution)/shard_map/attention_backward/pallas_call | solution.py:706
  371.8 15.7 %attention_backward.7 = (f32[64,1024]{1,0:T(8,128)}, bf16[64,1024]{1,0:T(8,128)(2,1)}, f32[24,1024]{1,0:T(8,128)}, bf16[256,1024]{1,0:T(8,128)(2,1)}, bf16[256,512]{1,0:T(8,128)(2,1)}) custom-call(s32[3]{0:T(128)} %add_add_fusion.sref.refs_0_, bf16[64,1024]{1,0:T(8,128)(2,1)} %get-tuple-element.303.refs_14_.refs_1_, bf16[64,1024]{1,0:T(8,128)(2,1)} %copy-done.36, ...), custom_call_target="tpu_custom_call" | custom-call | flops 1207959552 | bytes 9437184 | tf_op jit(solution)/shard_map/attention_backward/pallas_call | solution.py:706
  387.5 6.1 %attention_weight_grads.1 = bf16[16,448,128]{2,1,0:T(8,128)(2,1)} custom-call(s32[3]{0:T(128)} %add_add_fusion.sref.refs_0_, bf16[256,1024]{1,0:T(8,128)(2,1)} %get-tuple-element.316.refs_0_, bf16[256,1024]{1,0:T(8,128)(2,1)} %get-tuple-element.317.refs_1_, bf16[256,1024]{1,0:T(8,128)(2,1)} %get-tuple-element.318.refs_2_, ...), custom_call_target="tpu_custom_call" | custom-call | flops 805306368 | bytes 5242880 | tf_op jit(solution)/shard_map/attention_weight_grads/pallas_call | solution.py:831
  393.6 6.1 %all-to-all-start.1 = ((bf16[16,448,128]{2,1,0:T(8,128)(2,1)}), bf16[16,448,128]{2,1,0:T(8,128)(2,1)S(1)}, u32[]{:S(2)}, u32[]{:S(2)}) async-start(bf16[16,448,128]{2,1,0:T(8,128)(2,1)} %attention_weight_grads.1), calls=%async_computation.1 | async-start | bytes 3670016 | tf_op jit(solution)/shard_map/all_to_all | solution.py:1060
  407.0 4.1 collective-permute-start.44
  418.5 12.7 %all-to-all-done.1 = bf16[16,448,128]{2,1,0:T(8,128)(2,1)S(1)} async-done(((bf16[16,448,128]{2,1,0:T(8,128)(2,1)}), bf16[16,448,128]{2,1,0:T(8,128)(2,1)S(1)}, u32[]{:S(2)}, u32[]{:S(2)}) %all-to-all-start.1) | async-done | bytes 1835040 | tf_op jit(solution)/shard_map/all_to_all | solution.py:1060
  (356 shorter events, 182.9 us)
Async XLA Ops:
  7.3 98.4 %all-gather.3.cloned.1.call-start = ((), (), s32[]{:S(2)}) async-start(), calls=%async_computation.4 | async-start | bytes 13369344 | tf_op jit(solution)/shard_map/all_gather | solution.py:927
  11.2 40.3 %all-to-all-start = ((bf16[16,400,128]{2,1,0:T(8,128)(2,1)}), bf16[16,400,128]{2,1,0:T(8,128)(2,1)S(1)}, u32[]{:S(2)}, u32[]{:S(2)}) async-start(bf16[16,400,128]{2,1,0:T(8,128)(2,1)} %broadcast_in_dim.76), calls=%async_computation | async-start | bytes 3276800 | tf_op jit(solution)/shard_map/all_to_all | solution.py:925
  17.2 424.7 %reduce-scatter.2.cloned.1.call-start = ((), (), s32[]{:S(2)}) async-start(), calls=%async_computation.3 | async-start | bytes 13369344 | tf_op jit(solution)/shard_map/reduce_scatter | solution.py:1038
  30.0 21.5 %collective-permute-start.4 = (bf16[2,64,1024]{2,1,0:T(8,128)(2,1)S(1)}, bf16[2,64,1024]{2,1,0:T(8,128)(2,1)S(1)}, u32[]{:S(2)}, u32[]{:S(2)}) collective-permute-start(bf16[2,64,1024]{2,1,0:T(8,128)(2,1)S(1)} %copy-done.13), channel_id=1, source_target_pairs={{0,2},{1,3},{2,0},{3,1},{4,6},{5,7},{6,4},{7,5},{8,10},{9,11},{10,... | collective-permute-start | bytes 786440 | tf_op jit(solution)/shard_map/ppermute | solution.py:851
  34.1 17.4 %collective-permute-start.5 = (bf16[2,64,1024]{2,1,0:T(8,128)(2,1)S(1)}, bf16[2,64,1024]{2,1,0:T(8,128)(2,1)}, u32[]{:S(2)}, u32[]{:S(2)}) collective-permute-start(bf16[2,64,1024]{2,1,0:T(8,128)(2,1)S(1)} %copy-done.13), channel_id=1, source_target_pairs={{0,3},{1,0},{2,1},{3,2},{4,7},{5,4},{6,5},{7,6},{8,11},{9,8},{10,9... | collective-permute-start | bytes 786440 | tf_op jit(solution)/shard_map/ppermute | solution.py:851
  51.6 21.9 %collective-permute-start.6 = (bf16[8,400,128]{2,1,0:T(8,128)(2,1)S(1)}, bf16[8,400,128]{2,1,0:T(8,128)(2,1)S(1)}, u32[]{:S(2)}, u32[]{:S(2)}) collective-permute-start(bf16[8,400,128]{2,1,0:T(8,128)(2,1)S(1)} %constant_dynamic-slice_fusion), channel_id=1, source_target_pairs={{0,1},{1,2},{2,3},{3,0},{4,5},{5,6},{6,7},{7,4},{8,9},{9,10},{10,1... | collective-permute-start | bytes 2457608 | tf_op jit(solution)/shard_map/ppermute | solution.py:851
  53.1 20.8 %collective-permute-start.9 = (bf16[8,400,128]{2,1,0:T(8,128)(2,1)S(1)}, bf16[8,400,128]{2,1,0:T(8,128)(2,1)S(1)}, u32[]{:S(2)}, u32[]{:S(2)}) collective-permute-start(bf16[8,400,128]{2,1,0:T(8,128)(2,1)S(1)} %constant_dynamic-slice_fusion), channel_id=1, source_target_pairs={{0,3},{1,0},{2,1},{3,2},{4,7},{5,4},{6,5},{7,6},{8,11},{9,8},{10,9... | collective-permute-start | bytes 2457608 | tf_op jit(solution)/shard_map/ppermute | solution.py:851
  128.7 29.8 %collective-permute-start.17 = (bf16[64,1024]{1,0:T(8,128)(2,1)S(1)}, bf16[64,1024]{1,0:T(8,128)(2,1)S(1)}, u32[]{:S(2)}, u32[]{:S(2)}) collective-permute-start(bf16[64,1024]{1,0:T(8,128)(2,1)S(1)} %add_convert_fusion.3.refs_14_), channel_id=1, source_target_pairs={{0,64},{1,65},{2,66},{3,67},{4,68},{5,69},{6,70},{7,71},{8,72},{9,... | collective-permute-start | bytes 393224 | tf_op jit(solution)/shard_map/ppermute | solution.py:869
  130.1 28.5 %collective-permute-start.18 = (bf16[64,1024]{1,0:T(8,128)(2,1)S(1)}, bf16[64,1024]{1,0:T(8,128)(2,1)S(1)}, u32[]{:S(2)}, u32[]{:S(2)}) collective-permute-start(bf16[64,1024]{1,0:T(8,128)(2,1)S(1)} %add_convert_fusion.3.refs_14_), channel_id=1, source_target_pairs={{0,65},{1,66},{2,67},{3,64},{4,69},{5,70},{6,71},{7,68},{8,73},{9,... | collective-permute-start | bytes 393224 | tf_op jit(solution)/shard_map/ppermute | solution.py:869
  131.4 27.2 %collective-permute-start.19 = (bf16[64,1024]{1,0:T(8,128)(2,1)S(1)}, bf16[64,1024]{1,0:T(8,128)(2,1)S(1)}, u32[]{:S(2)}, u32[]{:S(2)}) collective-permute-start(bf16[64,1024]{1,0:T(8,128)(2,1)S(1)} %add_convert_fusion.3.refs_14_), channel_id=1, source_target_pairs={{0,66},{1,67},{2,64},{3,65},{4,70},{5,71},{6,68},{7,69},{8,74},{9,... | collective-permute-start | bytes 393224 | tf_op jit(solution)/shard_map/ppermute | solution.py:869
  132.7 25.9 %collective-permute-start.20 = (bf16[64,1024]{1,0:T(8,128)(2,1)S(1)}, bf16[64,1024]{1,0:T(8,128)(2,1)S(1)}, u32[]{:S(2)}, u32[]{:S(2)}) collective-permute-start(bf16[64,1024]{1,0:T(8,128)(2,1)S(1)} %add_convert_fusion.3.refs_14_), channel_id=1, source_target_pairs={{0,67},{1,64},{2,65},{3,66},{4,71},{5,68},{6,69},{7,70},{8,75},{9,... | collective-permute-start | bytes 393224 | tf_op jit(solution)/shard_map/ppermute | solution.py:869
  227.3 44.7 %collective-permute-start.40 = (bf16[64,1024]{1,0:T(8,128)(2,1)}, bf16[64,1024]{1,0:T(8,128)(2,1)S(1)}, u32[]{:S(2)}, u32[]{:S(2)}) collective-permute-start(bf16[64,1024]{1,0:T(8,128)(2,1)} %get-tuple-element.267), channel_id=1, source_target_pairs={{64,0},{65,1},{66,2},{67,3},{68,4},{69,5},{70,6},{71,7},{72,8},{73... | collective-permute-start | bytes 393224 | tf_op jit(solution)/shard_map/ppermute | solution.py:869
  228.6 45.4 %collective-permute-start.41 = (bf16[64,1024]{1,0:T(8,128)(2,1)}, bf16[64,1024]{1,0:T(8,128)(2,1)S(1)}, u32[]{:S(2)}, u32[]{:S(2)}) collective-permute-start(bf16[64,1024]{1,0:T(8,128)(2,1)} %get-tuple-element.267), channel_id=1, source_target_pairs={{64,1},{65,2},{66,3},{67,0},{68,5},{69,6},{70,7},{71,4},{72,9},{73... | collective-permute-start | bytes 393224 | tf_op jit(solution)/shard_map/ppermute | solution.py:869
  229.9 45.3 %collective-permute-start.42 = (bf16[64,1024]{1,0:T(8,128)(2,1)}, bf16[64,1024]{1,0:T(8,128)(2,1)S(1)}, u32[]{:S(2)}, u32[]{:S(2)}) collective-permute-start(bf16[64,1024]{1,0:T(8,128)(2,1)} %get-tuple-element.267), channel_id=1, source_target_pairs={{64,2},{65,3},{66,0},{67,1},{68,6},{69,7},{70,4},{71,5},{72,10},{7... | collective-permute-start | bytes 393224 | tf_op jit(solution)/shard_map/ppermute | solution.py:869
  231.3 44.0 %collective-permute-start.43 = (bf16[64,1024]{1,0:T(8,128)(2,1)}, bf16[64,1024]{1,0:T(8,128)(2,1)S(1)}, u32[]{:S(2)}, u32[]{:S(2)}) collective-permute-start(bf16[64,1024]{1,0:T(8,128)(2,1)} %get-tuple-element.267), channel_id=1, source_target_pairs={{64,3},{65,0},{66,1},{67,2},{68,7},{69,4},{70,5},{71,6},{72,11},{7... | collective-permute-start | bytes 393224 | tf_op jit(solution)/shard_map/ppermute | solution.py:869
  236.2 52.6 %collective-permute-start.37 = (bf16[64,1024]{1,0:T(8,128)(2,1)}, bf16[64,1024]{1,0:T(8,128)(2,1)S(1)}, u32[]{:S(2)}, u32[]{:S(2)}) collective-permute-start(bf16[64,1024]{1,0:T(8,128)(2,1)} %get-tuple-element.266.refs_1_), channel_id=1, source_target_pairs={{0,1},{1,2},{2,3},{3,0},{4,5},{5,6},{6,7},{7,4},{8,9},{9,10},{10,1... | collective-permute-start | bytes 393224 | tf_op jit(solution)/shard_map/ppermute | solution.py:851
  272.1 18.0 %collective-permute-start.38 = (bf16[64,1024]{1,0:T(8,128)(2,1)}, bf16[64,1024]{1,0:T(8,128)(2,1)S(1)}, u32[]{:S(2)}, u32[]{:S(2)}) collective-permute-start(bf16[64,1024]{1,0:T(8,128)(2,1)} %get-tuple-element.266.refs_1_), channel_id=1, source_target_pairs={{0,2},{1,3},{2,0},{3,1},{4,6},{5,7},{6,4},{7,5},{8,10},{9,11},{10,... | collective-permute-start | bytes 393224 | tf_op jit(solution)/shard_map/ppermute | solution.py:851
  274.0 16.0 %collective-permute-start.39 = (bf16[64,1024]{1,0:T(8,128)(2,1)}, bf16[64,1024]{1,0:T(8,128)(2,1)S(1)}, u32[]{:S(2)}, u32[]{:S(2)}) collective-permute-start(bf16[64,1024]{1,0:T(8,128)(2,1)} %get-tuple-element.266.refs_1_), channel_id=1, source_target_pairs={{0,3},{1,0},{2,1},{3,2},{4,7},{5,4},{6,5},{7,6},{8,11},{9,8},{10,9... | collective-permute-start | bytes 393224 | tf_op jit(solution)/shard_map/ppermute | solution.py:851
  294.4 16.9 %collective-permute-start.56 = (bf16[64,1024]{1,0:T(8,128)(2,1)}, bf16[64,1024]{1,0:T(8,128)(2,1)S(1)}, u32[]{:S(2)}, u32[]{:S(2)}) collective-permute-start(bf16[64,1024]{1,0:T(8,128)(2,1)} %get-tuple-element.289), channel_id=1, source_target_pairs={{64,0},{65,1},{66,2},{67,3},{68,4},{69,5},{70,6},{71,7},{72,8},{73... | collective-permute-start | bytes 393224 | tf_op jit(solution)/shard_map/ppermute | solution.py:869
  295.7 15.6 %collective-permute-start.57 = (bf16[64,1024]{1,0:T(8,128)(2,1)}, bf16[64,1024]{1,0:T(8,128)(2,1)S(1)}, u32[]{:S(2)}, u32[]{:S(2)}) collective-permute-start(bf16[64,1024]{1,0:T(8,128)(2,1)} %get-tuple-element.289), channel_id=1, source_target_pairs={{64,1},{65,2},{66,3},{67,0},{68,5},{69,6},{70,7},{71,4},{72,9},{73... | collective-permute-start | bytes 393224 | tf_op jit(solution)/shard_map/ppermute | solution.py:869
  350.6 20.4 %collective-permute-start.63 = (bf16[64,1024]{1,0:T(8,128)(2,1)}, bf16[64,1024]{1,0:T(8,128)(2,1)S(1)}, u32[]{:S(2)}, u32[]{:S(2)}) collective-permute-start(bf16[64,1024]{1,0:T(8,128)(2,1)} %get-tuple-element.303.refs_14_.refs_1_), channel_id=1, source_target_pairs={{0,1},{1,2},{2,3},{3,0},{4,5},{5,6},{6,7},{7,4},{8,9},{9,10},{10,1... | collective-permute-start | bytes 393224 | tf_op jit(solution)/shard_map/ppermute | solution.py:851
  351.8 19.3 %collective-permute-start.64 = (bf16[64,1024]{1,0:T(8,128)(2,1)}, bf16[64,1024]{1,0:T(8,128)(2,1)S(1)}, u32[]{:S(2)}, u32[]{:S(2)}) collective-permute-start(bf16[64,1024]{1,0:T(8,128)(2,1)} %get-tuple-element.303.refs_14_.refs_1_), channel_id=1, source_target_pairs={{0,2},{1,3},{2,0},{3,1},{4,6},{5,7},{6,4},{7,5},{8,10},{9,11},{10,... | collective-permute-start | bytes 393224 | tf_op jit(solution)/shard_map/ppermute | solution.py:851
  354.7 16.4 %collective-permute-start.65 = (bf16[64,1024]{1,0:T(8,128)(2,1)}, bf16[64,1024]{1,0:T(8,128)(2,1)S(1)}, u32[]{:S(2)}, u32[]{:S(2)}) collective-permute-start(bf16[64,1024]{1,0:T(8,128)(2,1)} %get-tuple-element.303.refs_14_.refs_1_), channel_id=1, source_target_pairs={{0,3},{1,0},{2,1},{3,2},{4,7},{5,4},{6,5},{7,6},{8,11},{9,8},{10,9... | collective-permute-start | bytes 393224 | tf_op jit(solution)/shard_map/ppermute | solution.py:851
  393.6 37.7 %all-to-all-start.1 = ((bf16[16,448,128]{2,1,0:T(8,128)(2,1)}), bf16[16,448,128]{2,1,0:T(8,128)(2,1)S(1)}, u32[]{:S(2)}, u32[]{:S(2)}) async-start(bf16[16,448,128]{2,1,0:T(8,128)(2,1)} %attention_weight_grads.1), calls=%async_computation.1 | async-start | bytes 3670016 | tf_op jit(solution)/shard_map/all_to_all | solution.py:1060
  (124 other events, 868.8 us)
Sparse Core Ops, SparseCore 0:
  9.8 88.8 all-gather.2
  337.0 103.6 reduce-scatter.1

commit v2 on v1

--- a/solution.py
+++ b/solution.py
@@ -16,7 +16,7 @@
 F32 = jnp.float32
 VMEM_LIMIT = 56 * 1024 * 1024
 PER = 4
-PER_BACK = 8
+PER_STEP = 8
 PER_GRAD = 4
 LANES = 128
 
@@ -172,11 +172,130 @@
 def attention_forward_kernel(n_after, sref, *refs):
     pieces, refs = refs[:4], refs[4:]
     sources, refs = refs[:9], refs[9 + n_after :]
+    (
+        gains_ref, cos_ref, sin_ref, bias_ref, picked_ref, router_ref,
+        a_ref, xown_ref, qkv_ref, o_ref, lse_ref, hown_ref, b_ref, gates_ref,
+        hidden, buffers, sems,
+    ) = refs
+    step = pl.program_id(0)
+    me = sref[0]
+    group, width = b_ref.shape
+    shard = xown_ref.shape[0]
 
     @pl.when(sref[1] > 0)
     def _():
-        attention_part(sref, pieces, sources, *refs)
-
+        copies = fetches(sref[2], sources, buffers, sems)
+
+        @pl.when(step == 0)
+        def _():
+            for part in copies:
+                for copy in part:
+                    copy.start()
+            assemble(me, pieces, b_ref)
+            entering = b_ref[...].astype(F32)
+            a_ref[...] = (entering * rms_scale(entering) * gains_ref[0:1, :]).astype(BF)
+            xown_ref[...] = pieces[0][...]
+            hidden[...] = entering
+
+        for shift, part in enumerate(copies):
+
+            @pl.when(step == shift)
+            def _(part=part):
+                for copy in part:
+                    copy.wait()
+
+        w_qkv, w_out = group_weights(buffers, step)
+        qkv = dot(a_ref[...], w_qkv)
+        qk = qkv[:, :384]
+        cos = jnp.concatenate([cos_ref[...]] * 3, axis=1)
+        sin = jnp.concatenate([sin_ref[...]] * 3, axis=1)
+        turned = qk * cos + swap_halves(qk) * sin
+        q = (turned[:, :256] * HD**-0.5).astype(BF)
+        k = turned[:, 256:].astype(BF)
+        v = qkv[:, 384:].astype(BF)
+        qkv_ref[0, :, :256] = q
+        qkv_ref[0, :, 256:384] = k
+        qkv_ref[0, :, 384:] = v
+        bias = bias_ref[...]
+        lanes = lax.broadcasted_iota(jnp.int32, (group, LANES), 1)
+        lse_all = jnp.where(step == 0, 0.0, lse_ref[...])
+        outs = []
+        for head in range(4):
+            kv = head // 2
+            scores = dot_nt(q[:, head * HD : (head + 1) * HD], k[:, kv * HD : (kv + 1) * HD])
+            scores = scores + bias
+            peak = jnp.max(scores, axis=1, keepdims=True)
+            soft = jnp.exp(scores - peak)
+            total = jnp.sum(soft, axis=1, keepdims=True)
+            lse_all = jnp.where(lanes == 4 * step + head, peak + jnp.log(total), lse_all)
+            soft = (soft * (1.0 / total)).astype(BF)
+            outs.append(dot(soft, v[:, kv * HD : (kv + 1) * HD]))
+        mixed = jnp.concatenate(outs, axis=1).astype(BF)
+
+        @pl.when(step == 0)
+        def _():
+            o_ref[...] = mixed
+
+        lse_ref[...] = lse_all
+        hidden[...] += dot_nt(mixed, w_out)
+
+        @pl.when(step == pl.num_programs(0) - 1)
+        def _():
+            rows = hidden[...]
+            normed = (rows * rms_scale(rows) * gains_ref[1:2, :]).astype(BF)
+            b_ref[...] = normed
+            hown_ref[...] = hidden[own_rows(me, shard), :]
+            logits = dot(normed, router_ref[...])[:, :E]
+            picked = picked_ref[...]
+            peak = jnp.max(jnp.where(picked > 0, logits, -1e30), axis=1, keepdims=True)
+            powers = jnp.where(picked > 0, jnp.exp(jnp.minimum(logits - peak, 0.0)), 0.0)
+            gates_ref[...] = powers / jnp.sum(powers, axis=1, keepdims=True)
+
+
+def attention_forward(scalars, pieces, gains, tables, picked, w_attn, router, after):
+    shard, width = pieces[0].shape
+    group = 4 * shard
+    dp = width // 64
+    cos, sin, bias = tables
+    smalls = [gains, cos, sin, bias, picked, router]
+    per_step = lambda i, s: (i * s[1], 0, 0)
+    outs = [
+        ((group, width), BF, None),
+        ((shard, width), BF, None),
+        ((4, group, 512), BF, (1, group, 512)),
+        ((group, 256), BF, None),
+        ((group, LANES), F32, None),
+        ((shard, width), F32, None),
+        ((group, width), BF, None),
+        ((group, E), F32, None),
+    ]
+    return pl.pallas_call(
+        lambda *refs: attention_forward_kernel(len(after), *refs),
+        grid_spec=pltpu.PrefetchScalarGridSpec(
+            num_scalar_prefetch=1,
+            grid=(4,),
+            in_specs=[whole(x.shape) for x in pieces]
+            + anywhere(9 + len(after))
+            + [whole(x.shape) for x in smalls],
+            out_specs=[
+                whole(shape) if block is None else pl.BlockSpec(block, per_step)
+                for shape, _, block in outs
+            ],
+            scratch_shapes=[
+                pltpu.VMEM((group, width), F32),
+                pltpu.VMEM((4, dp, 400, LANES), BF),
+                pltpu.SemaphoreType.DMA((9,)),
+            ],
+        ),
+        out_shape=[jax.ShapeDtypeStruct(shape, kind) for shape, kind, _ in outs],
+        compiler_params=params(),
+        cost_estimate=pl.CostEstimate(
+            flops=2 * group * width * 768 * 4 + 16 * 4 * group * group * HD,
+            bytes_accessed=width * 768 * 8 + 6 * group * width * 2,
+            transcendentals=16 * group * group,
+        ),
+        name="attention_forward",
+    )(scalars, *pieces, *w_attn, *after, *smalls)
 
 def attention_part(
     sref, pieces, sources,
@@ -245,66 +364,79 @@
     gates_ref[...] = powers / jnp.sum(powers, axis=1, keepdims=True)
 
 
-def attention_forward(scalars, pieces, gains, tables, picked, w_attn, router, after):
-    shard, width = pieces[0].shape
-    group = 4 * shard
-    dp = width // 64
-    cos, sin, bias = tables
-    smalls = [gains, cos, sin, bias, picked, router]
-    per_step = lambda i, s: (i * s[1], 0, 0)
-    outs = [
-        ((group, width), BF, None),
-        ((shard, width), BF, None),
-        ((4, group, 512), BF, None),
-        ((group, 256), BF, None),
-        ((group, LANES), F32, None),
-        ((shard, width), F32, None),
-        ((group, width), BF, None),
-        ((group, E), F32, None),
-    ]
+def chunk(number):
+    return pl.ds(PER * number, PER)
+
+
+def experts_forward_kernel(n_after, sref, *refs):
+    (b_ref, gate_ref, w_ref, *refs) = refs[n_after:]
+    pieces, (gu_ref, total) = refs[:4], refs[4:]
+    step = pl.program_id(0)
+    width = b_ref.shape[1]
+    ff = w_ref.shape[-1]
+
+    @pl.when(sref[1] > 0)
+    def _():
+        b = b_ref[...]
+        gates = gate_ref[...]
+        acts, downs = [], []
+        for j in range(PER_STEP):
+            gate_up = jnp.concatenate(
+                [w_ref[:, 0, j].reshape(width, ff), w_ref[:, 1, j].reshape(width, ff)], axis=1
+            )
+            both = dot(b, gate_up)
+            gu_ref[j] = both.astype(BF)
+            gate_pre, up_pre = both[:, :ff], both[:, ff:]
+            act = gate_pre * jax.nn.sigmoid(gate_pre) * up_pre
+            acts.append((act * column(gates, step * PER_STEP + j)).astype(BF))
+            downs.append(w_ref[:, 2, j].reshape(width, ff))
+        out = dot_nt(jnp.concatenate(acts, axis=1), jnp.concatenate(downs, axis=1))
+
+        @pl.when(step == 0)
+        def _():
+            total[...] = out
+
+        @pl.when(step > 0)
+        def _():
+            total[...] += out
+
+        @pl.when(step == pl.num_programs(0) - 1)
+        def _():
+            rows = b_ref.shape[0] // 4
+            for shift in range(4):
+                place = own_rows(lax.rem(sref[0] + shift, 4), rows)
+                pieces[shift][...] = total[place, :].astype(BF)
+
+
+def experts_forward(scalars, b, gates, w, after):
+    group, width = b.shape
+    dp, _, experts, dr, ff = w.shape
+    piece = (group // 4, width)
     return pl.pallas_call(
-        lambda *refs: attention_forward_kernel(len(after), *refs),
+        lambda *refs: experts_forward_kernel(len(after), *refs),
         grid_spec=pltpu.PrefetchScalarGridSpec(
             num_scalar_prefetch=1,
-            grid=(1,),
-            in_specs=[whole(x.shape) for x in pieces]
-            + anywhere(9 + len(after))
-            + [whole(x.shape) for x in smalls],
-            out_specs=[
-                whole(shape) if block is None else pl.BlockSpec(block, per_step)
-                for shape, _, block in outs
+            grid=(experts // PER_STEP,),
+            in_specs=anywhere(len(after))
+            + [
+                whole((group, width)),
+                whole((group, experts)),
+                pl.BlockSpec((dp, 3, PER_STEP, dr, ff), lambda i, s: (0, 0, i * s[1], 0, 0)),
             ],
-            scratch_shapes=[
-                pltpu.VMEM((group, width), F32),
-                pltpu.VMEM((4, dp, 400, LANES), BF),
-                pltpu.SemaphoreType.DMA((9,)),
-            ],
-        ),
-        out_shape=[jax.ShapeDtypeStruct(shape, kind) for shape, kind, _ in outs],
+            out_specs=[whole(piece)] * 4
+            + [pl.BlockSpec((PER_STEP, group, 2 * ff), lambda i, s: (i * s[1], 0, 0))],
+            scratch_shapes=[pltpu.VMEM((group, width), F32)],
+        ),
+        out_shape=[jax.ShapeDtypeStruct(piece, BF)] * 4
+        + [jax.ShapeDtypeStruct((experts, group, 2 * ff), BF)],
         compiler_params=params(),
         cost_estimate=pl.CostEstimate(
-            flops=2 * group * width * 768 * 4 + 16 * 4 * group * group * HD,
-            bytes_accessed=width * 768 * 8 + 6 * group * width * 2,
-            transcendentals=16 * group * group,
-        ),
-        name="attention_forward",
-    )(scalars, *pieces, *w_attn, *after, *smalls)
-
-
-def chunk(number):
-    return pl.ds(PER * number, PER)
-
-
-def experts_forward_kernel(n_after, sref, *refs):
-    w_ref, b_ref, gate_ref, *refs = refs[n_after:]
-    pieces, (gu_ref, total, held, gu_held, sems) = refs[:4], refs[4:]
-
-    @pl.when(sref[1] > 0)
-    def _():
-        come, leave = experts_copies(w_ref, gu_ref, held, gu_held, sems)
-        come[0].start()
-        come[1].start()
-        experts_part(sref, come, leave, b_ref, gate_ref, pieces, total, held, gu_held)
+            flops=2 * group * width * ff * 3 * experts,
+            bytes_accessed=w.size * 2 + experts * group * 2 * ff * 2,
+            transcendentals=experts * group * ff,
+        ),
+        name="experts_forward",
+    )(scalars, *after, b, gates, w)
 
 
 def experts_copies(w_ref, gu_ref, held, gu_held, sems):
@@ -354,36 +486,6 @@
         pieces[shift][...] = total[place, :].astype(BF)
     for c in range(chunks):
         leave[c].wait()
-
-
-def experts_forward(scalars, b, gates, w, after):
-    group, width = b.shape
-    dp, _, experts, dr, ff = w.shape
-    piece = (group // 4, width)
-    return pl.pallas_call(
-        lambda *refs: experts_forward_kernel(len(after), *refs),
-        grid_spec=pltpu.PrefetchScalarGridSpec(
-            num_scalar_prefetch=1,
-            grid=(1,),
-            in_specs=anywhere(len(after) + 1) + [whole((group, width)), whole((group, experts))],
-            out_specs=[whole(piece)] * 4 + anywhere(1),
-            scratch_shapes=[
-                pltpu.VMEM((group, width), F32),
-                pltpu.VMEM(w.shape, BF),
-                pltpu.VMEM((experts, group, 2 * ff), BF),
-                pltpu.SemaphoreType.DMA((2 * experts // PER,)),
-            ],
-        ),
-        out_shape=[jax.ShapeDtypeStruct(piece, BF)] * 4
-        + [jax.ShapeDtypeStruct((experts, group, 2 * ff), BF)],
-        compiler_params=params(),
-        cost_estimate=pl.CostEstimate(
-            flops=2 * group * width * ff * 3 * experts,
-            bytes_accessed=w.size * 2 + experts * group * 2 * ff * 2,
-            transcendentals=experts * group * ff,
-        ),
-        name="experts_forward",
-    )(scalars, *after, w, b, gates)
 
 
 def layer_forward_kernel(n_after, sref, *refs):
@@ -470,14 +572,14 @@
         grad = grad_ref[...]
         gates = gate_ref[...]
         down = jnp.concatenate(
-            [w_ref[:, 2, j].reshape(width, ff) for j in range(PER_BACK)], axis=1
+            [w_ref[:, 2, j].reshape(width, ff) for j in range(PER_STEP)], axis=1
         )
         turned = dot(grad, down)
         lanes = lax.broadcasted_iota(jnp.int32, (group, LANES), 1)
         grad_gate = jnp.zeros((group, LANES), F32)
         out = None
-        for j in range(PER_BACK):
-            expert = step * PER_BACK + j
+        for j in range(PER_STEP):
+            expert = step * PER_STEP + j
             back = turned[:, j * ff : (j + 1) * ff]
             both = gu_ref[j].astype(F32)
             gate_pre, up_pre = both[:, :ff], both[:, ff:]
@@ -528,19 +630,19 @@
         lambda *refs: experts_backward_kernel(len(after), *refs),
         grid_spec=pltpu.PrefetchScalarGridSpec(
             num_scalar_prefetch=1,
-            grid=(experts // PER_BACK,),
+            grid=(experts // PER_STEP,),
             in_specs=anywhere(len(after))
             + [whole(x.shape) for x in given]
             + [
                 whole((group, experts)),
-                pl.BlockSpec((PER_BACK, group, 2 * ff), lambda i, s: (i * s[1], 0, 0)),
-                pl.BlockSpec((dp, 3, PER_BACK, dr, ff), lambda i, s: (0, 0, i * s[1], 0, 0)),
+                pl.BlockSpec((PER_STEP, group, 2 * ff), lambda i, s: (i * s[1], 0, 0)),
+                pl.BlockSpec((dp, 3, PER_STEP, dr, ff), lambda i, s: (0, 0, i * s[1], 0, 0)),
             ],
             out_specs=[whole(piece)] * 4
             + [
                 whole((group, width)),
-                pl.BlockSpec((PER_BACK, group, 2 * ff), lambda i, s: (i * s[1], 0, 0)),
-                pl.BlockSpec((group, PER_BACK * ff), lambda i, s: (0, i * s[1])),
+                pl.BlockSpec((PER_STEP, group, 2 * ff), lambda i, s: (i * s[1], 0, 0)),
+                pl.BlockSpec((group, PER_STEP * ff), lambda i, s: (0, i * s[1])),
             ],
             scratch_shapes=[pltpu.VMEM((group, width), F32), pltpu.VMEM((group, LANES), F32)],
         ),

time: 460 us -> 457 us (level)
  starting transfers between devices: 101 us -> 115 us
  Pallas kernels: 170 us -> 158 us
    pallas_call x2, Pallas kernels: 36.9 us -> 26.2 us  [attention_forward(): pl.pallas_call(lambda *refs: attention_forward_kernel(len(after), *refs),...]
    ppermute x16, starting transfers between devices: 20.9 us -> 30.9 us  [across(): lax.ppermute(rows, ('pipe', 'tensor'), [(start + i, end + (i + s) % 4) fo...]
  transfers between devices with their start and end apart: 73 -> 73, of which waited for: 25 -> 23; matrix products, arithmetic and copies ran while one was open for 5% -> 5% of each run, Pallas kernels for 26% -> 24%
where the time goes in v2:
time: 457 us; the launch traced here: 449 us
  Pallas kernels  158 us (35%)
  waiting for transfers between devices  120 us (26%)
  starting transfers between devices  115 us (25%)
  local copies, waits for them, and re-layouts  24.7 us (5%)
  other arithmetic  16.9 us (4%)
  between operations  15.4 us (3%)
    ppermute x49, starting transfers between devices, moved(): lax.ppermute(array, 'tensor', [(i, (i + shift) % 4) for i in range(4)])  70.6 us
    ppermute x49, waiting for transfers between devices, moved(): lax.ppermute(array, 'tensor', [(i, (i + shift) % 4) for i in range(4)])  63.6 us
    ppermute x16, waiting for transfers between devices, across(): lax.ppermute(rows, ('pipe', 'tensor'), [(start + i, end + (i + s) % 4) fo...  43 us
    pallas_call x4, Pallas kernels, attention_backward(): pl.pallas_call(lambda *refs: attention_backward_kernel(len(after), *refs)...  38.3 us
    pallas_call x4, Pallas kernels, experts_backward(): pl.pallas_call(lambda *refs: experts_backward_kernel(len(after), *refs),...  31.7 us
    ppermute x16, starting transfers between devices, across(): lax.ppermute(rows, ('pipe', 'tensor'), [(start + i, end + (i + s) % 4) fo...  30.9 us
    pallas_call x2, Pallas kernels, attention_forward(): pl.pallas_call(lambda *refs: attention_forward_kernel(len(after), *refs),...  26.2 us
    pallas_call x2, Pallas kernels, experts_forward(): pl.pallas_call(lambda *refs: experts_forward_kernel(len(after), *refs), g...  17.5 us
  transfers between devices with their start and end apart: 73, of which 23 were waited for; matrix products, arithmetic and copies ran while one was open for 5% of the time, Pallas kernels for 24%

profile of v2, /device:TPU:0, one launch (start us, length us, event | category | flops | bytes accessed | tf_op | source)
XLA Modules:
  0.0 449.5 jit_solution(13421140677800765487)
XLA Ops:
  11.2 6.0 %all-to-all-start = ((bf16[16,400,128]{2,1,0:T(8,128)(2,1)}), bf16[16,400,128]{2,1,0:T(8,128)(2,1)S(1)}, u32[]{:S(2)}, u32[]{:S(2)}) async-start(bf16[16,400,128]{2,1,0:T(8,128)(2,1)} %broadcast_in_dim.76), calls=%async_computation | async-start | bytes 3276800 | tf_op jit(solution)/shard_map/all_to_all | solution.py:1027
  44.8 6.6 %collective-permute-done.4 = bf16[2,64,1024]{2,1,0:T(8,128)(2,1)S(1)} collective-permute-done((bf16[2,64,1024]{2,1,0:T(8,128)(2,1)S(1)}, bf16[2,64,1024]{2,1,0:T(8,128)(2,1)S(1)}, u32[]{:S(2)}, u32[]{:S(2)}) %collective-permute-start.4) | collective-permute-done | bytes 262176 | tf_op jit(solution)/shard_map/ppermute | solution.py:953
  58.7 14.7 %collective-permute-done.6.refs_1_.refs_6_ = bf16[8,400,128]{2,1,0:T(8,128)(2,1)S(1)} collective-permute-done((bf16[8,400,128]{2,1,0:T(8,128)(2,1)S(1)}, bf16[8,400,128]{2,1,0:T(8,128)(2,1)S(1)}, u32[]{:S(2)}, u32[]{:S(2)}) %collective-permute-start.6) | collective-permute-done | bytes 819232 | tf_op jit(solution)/shard_map/ppermute | solution.py:953
  78.9 7.5 %collective-permute-done.8.refs_3_.refs_8_ = bf16[4,400,128]{2,1,0:T(8,128)(2,1)S(1)} collective-permute-done((bf16[4,400,128]{2,1,0:T(8,128)(2,1)S(1)}, bf16[4,400,128]{2,1,0:T(8,128)(2,1)S(1)}, u32[]{:S(2)}, u32[]{:S(2)}) %collective-permute-start.8) | collective-permute-done | bytes 409632 | tf_op jit(solution)/shard_map/ppermute | solution.py:953
  93.5 13.1 %attention_forward.2 = (bf16[256,1024]{1,0:T(8,128)(2,1)}, bf16[64,1024]{1,0:T(8,128)(2,1)}, bf16[4,256,512]{2,1,0:T(8,128)(2,1)}, bf16[256,256]{1,0:T(8,128)(2,...) custom-call(s32[3]{0:T(128)} %add_add_fusion.sref.refs_0_, ...), custom_call_target="tpu_custom_call" | custom-call | flops 1879048192 | bytes 9437184 | tf_op jit(solution)/shard_map/attention_forward/pallas_call | solution.py:272
  106.6 8.8 %experts_forward.2 = (bf16[64,1024]{1,0:T(8,128)(2,1)}, bf16[64,1024]{1,0:T(8,128)(2,1)}, bf16[64,1024]{1,0:T(8,128)(2,1)}, bf16[64,1024]{1,0:T(8,128)(2,1)}, bf16[16,256,256]{2,1,0:T(8,128)(2,1)}) custom-call(s32[3]{0:T(128)} %add_add_fusion.sref.refs_0_, bf16[256,1024]{1,0:T(8,128)(2,1)} %get-tuple-element.204.refs_1_.refs_2_.refs_9_, ...), custom_call_target="tpu_custom_call" | custom-call | flops 3221225472 | bytes 14680064 | tf_op jit(solution)/shard_map/experts_forward/pallas_call | solution.py:415
  119.6 5.1 %collective-permute-done.16 = bf16[64,1024]{1,0:T(8,128)(2,1)S(1)} collective-permute-done((bf16[64,1024]{1,0:T(8,128)(2,1)}, bf16[64,1024]{1,0:T(8,128)(2,1)S(1)}, u32[]{:S(2)}, u32[]{:S(2)}) %collective-permute-start.16) | collective-permute-done | bytes 131104 | tf_op jit(solution)/shard_map/ppermute | solution.py:953
  134.2 13.1 %attention_forward.3 = (bf16[256,1024]{1,0:T(8,128)(2,1)}, bf16[64,1024]{1,0:T(8,128)(2,1)}, bf16[4,256,512]{2,1,0:T(8,128)(2,1)}, bf16[256,256]{1,0:T(8,128)(2,...) custom-call(s32[3]{0:T(128)} %add_add_fusion.sref.refs_0_, ...), custom_call_target="tpu_custom_call" | custom-call | flops 1879048192 | bytes 9437184 | tf_op jit(solution)/shard_map/attention_forward/pallas_call | solution.py:272
  148.1 4.4 layer_forward.2
  152.6 8.7 %experts_forward.3 = (bf16[64,1024]{1,0:T(8,128)(2,1)}, bf16[64,1024]{1,0:T(8,128)(2,1)}, bf16[64,1024]{1,0:T(8,128)(2,1)}, bf16[64,1024]{1,0:T(8,128)(2,1)}, bf16[16,256,256]{2,1,0:T(8,128)(2,1)}) custom-call(s32[3]{0:T(128)} %add_add_fusion.sref.refs_0_, bf16[16,256,256]{2,1,0:T(8,128)(2,1)} %get-tuple-element.224.refs_1_.refs_7_, ...), custom_call_target="tpu_custom_call" | custom-call | flops 3221225472 | bytes 14680064 | tf_op jit(solution)/shard_map/experts_forward/pallas_call | solution.py:415
  172.2 10.0 %collective-permute-start.24 = (bf16[64,1024]{1,0:T(8,128)(2,1)S(1)}, bf16[64,1024]{1,0:T(8,128)(2,1)S(1)}, u32[]{:S(2)}, u32[]{:S(2)}) collective-permute-start(bf16[64,1024]{1,0:T(8,128)(2,1)S(1)} %add_convert_fusion.2), channel_id=1, source_target_pairs={{0,64},{1,65},{2,66},{3,67},{4,68},{5,69},{6,70},{7,71},{8,72},{9,... | collective-permute-start | bytes 393224 | tf_op jit(solution)/shard_map/ppermute | solution.py:971
  187.2 5.5 %experts_backward.4 = (bf16[64,1152]{1,0:T(8,128)(2,1)}, bf16[64,1152]{1,0:T(8,128)(2,1)}, bf16[64,1152]{1,0:T(8,128)(2,1)}, bf16[64,1152]{1,0:T(8,128)(2,1)}, b...) custom-call(s32[3]{0:T(128)} %add_add_fusion.1.refs_0_, ...), custom_call_target="tpu_custom_call" | custom-call | flops 3221225472 | bytes 17825792 | tf_op jit(solution)/shard_map/experts_backward/pallas_call | solution.py:629
  210.7 5.4 %experts_backward.5 = (bf16[64,1152]{1,0:T(8,128)(2,1)}, bf16[64,1152]{1,0:T(8,128)(2,1)}, bf16[64,1152]{1,0:T(8,128)(2,1)}, bf16[64,1152]{1,0:T(8,128)(2,1)}, b...) custom-call(s32[3]{0:T(128)} %add_add_fusion.1.refs_0_, ...), custom_call_target="tpu_custom_call" | custom-call | flops 3221225472 | bytes 17825792 | tf_op jit(solution)/shard_map/experts_backward/pallas_call | solution.py:629
  234.2 35.4 %collective-permute-done.40.refs_2_.refs_6_ = bf16[64,1024]{1,0:T(8,128)(2,1)S(1)} collective-permute-done((bf16[64,1024]{1,0:T(8,128)(2,1)}, bf16[64,1024]{1,0:T(8,128)(2,1)S(1)}, u32[]{:S(2)}, u32[]{:S(2)}) %collective-permute-start.40) | collective-permute-done | bytes 131104 | tf_op jit(solution)/shard_map/ppermute | solution.py:971
  273.9 10.5 %experts_backward.6 = (bf16[64,1152]{1,0:T(8,128)(2,1)}, bf16[64,1152]{1,0:T(8,128)(2,1)}, bf16[64,1152]{1,0:T(8,128)(2,1)}, bf16[64,1152]{1,0:T(8,128)(2,1)}, b...) custom-call(s32[3]{0:T(128)} %add_add_fusion.sref.refs_0_, ...), custom_call_target="tpu_custom_call" | custom-call | flops 3221225472 | bytes 17825792 | tf_op jit(solution)/shard_map/experts_backward/pallas_call | solution.py:629
  301.7 4.3 collective-permute-done.56.refs_2_.refs_6_
  310.0 10.4 %experts_backward.7 = (bf16[64,1152]{1,0:T(8,128)(2,1)}, bf16[64,1152]{1,0:T(8,128)(2,1)}, bf16[64,1152]{1,0:T(8,128)(2,1)}, bf16[64,1152]{1,0:T(8,128)(2,1)}, b...) custom-call(s32[3]{0:T(128)} %add_add_fusion.sref.refs_0_, ...), custom_call_target="tpu_custom_call" | custom-call | flops 3221225472 | bytes 17825792 | tf_op jit(solution)/shard_map/experts_backward/pallas_call | solution.py:629
  320.4 14.4 %expert_weight_grads.1.refs_1_ = bf16[16,3,16,64,128]{4,3,2,1,0:T(8,128)(2,1)} custom-call(s32[3]{0:T(128)} %add_add_fusion.sref.refs_0_, bf16[256,1024]{1,0:T(8,128)(2,1)} %get-tuple-element.290.refs_1_.refs_7_, bf16[256,1024]{1,0:T(8,128)(2,1)} %get-tuple-element.204.refs_1_.refs_2_.refs_9_, ...), custom_call_target="tpu_custom_call" | custom-call | flops 6442450944 | bytes 18874368 | tf_op jit(solution)/shard_map/expert_weight_grads/pallas_call | solution.py:881
  353.5 15.5 %attention_backward.6 = (f32[64,1024]{1,0:T(8,128)}, bf16[64,1024]{1,0:T(8,128)(2,1)}, f32[24,1024]{1,0:T(8,128)}, bf16[256,1024]{1,0:T(8,128)(2,1)}, bf16[256,512]{1,0:T(8,128)(2,1)}) custom-call(s32[3]{0:T(128)} %add_add_fusion.sref.refs_0_, bf16[64,1024]{1,0:T(8,128)(2,1)} %get-tuple-element.288.refs_1_, bf16[64,1024]{1,0:T(8,128)(2,1)} %copy-done.37, ...), custom_call_target="tpu_custom_call" | custom-call | flops 1207959552 | bytes 9437184 | tf_op jit(solution)/shard_map/attention_backward/pallas_call | solution.py:808
  369.7 15.6 %attention_backward.7 = (f32[64,1024]{1,0:T(8,128)}, bf16[64,1024]{1,0:T(8,128)(2,1)}, f32[24,1024]{1,0:T(8,128)}, bf16[256,1024]{1,0:T(8,128)(2,1)}, bf16[256,512]{1,0:T(8,128)(2,1)}) custom-call(s32[3]{0:T(128)} %add_add_fusion.sref.refs_0_, bf16[64,1024]{1,0:T(8,128)(2,1)} %get-tuple-element.303.refs_14_.refs_1_, bf16[64,1024]{1,0:T(8,128)(2,1)} %copy-done.36, ...), custom_call_target="tpu_custom_call" | custom-call | flops 1207959552 | bytes 9437184 | tf_op jit(solution)/shard_map/attention_backward/pallas_call | solution.py:808
  385.3 6.1 %attention_weight_grads.1 = bf16[16,448,128]{2,1,0:T(8,128)(2,1)} custom-call(s32[3]{0:T(128)} %add_add_fusion.sref.refs_0_, bf16[256,1024]{1,0:T(8,128)(2,1)} %get-tuple-element.316.refs_0_, bf16[256,1024]{1,0:T(8,128)(2,1)} %get-tuple-element.317.refs_1_, bf16[256,1024]{1,0:T(8,128)(2,1)} %get-tuple-element.318.refs_2_, ...), custom_call_target="tpu_custom_call" | custom-call | flops 805306368 | bytes 5242880 | tf_op jit(solution)/shard_map/attention_weight_grads/pallas_call | solution.py:933
  391.4 5.9 %all-to-all-start.1 = ((bf16[16,448,128]{2,1,0:T(8,128)(2,1)}), bf16[16,448,128]{2,1,0:T(8,128)(2,1)S(1)}, u32[]{:S(2)}, u32[]{:S(2)}) async-start(bf16[16,448,128]{2,1,0:T(8,128)(2,1)} %attention_weight_grads.1), calls=%async_computation.1 | async-start | bytes 3670016 | tf_op jit(solution)/shard_map/all_to_all | solution.py:1162
  404.7 4.1 collective-permute-start.44
  416.0 13.4 %all-to-all-done.1 = bf16[16,448,128]{2,1,0:T(8,128)(2,1)S(1)} async-done(((bf16[16,448,128]{2,1,0:T(8,128)(2,1)}), bf16[16,448,128]{2,1,0:T(8,128)(2,1)S(1)}, u32[]{:S(2)}, u32[]{:S(2)}) %all-to-all-start.1) | async-done | bytes 1835040 | tf_op jit(solution)/shard_map/all_to_all | solution.py:1162
  (356 shorter events, 189.5 us)
Async XLA Ops:
  7.3 99.4 %all-gather.3.cloned.1.call-start = ((), (), s32[]{:S(2)}) async-start(), calls=%async_computation.4 | async-start | bytes 13369344 | tf_op jit(solution)/shard_map/all_gather | solution.py:1029
  11.2 40.3 %all-to-all-start = ((bf16[16,400,128]{2,1,0:T(8,128)(2,1)}), bf16[16,400,128]{2,1,0:T(8,128)(2,1)S(1)}, u32[]{:S(2)}, u32[]{:S(2)}) async-start(bf16[16,400,128]{2,1,0:T(8,128)(2,1)} %broadcast_in_dim.76), calls=%async_computation | async-start | bytes 3276800 | tf_op jit(solution)/shard_map/all_to_all | solution.py:1027
  17.2 422.7 %reduce-scatter.2.cloned.1.call-start = ((), (), s32[]{:S(2)}) async-start(), calls=%async_computation.3 | async-start | bytes 13369344 | tf_op jit(solution)/shard_map/reduce_scatter | solution.py:1140
  25.2 15.5 %collective-permute-start.1 = (bf16[2,64,1024]{2,1,0:T(8,128)(2,1)S(1)}, bf16[2,64,1024]{2,1,0:T(8,128)(2,1)S(1)}, u32[]{:S(2)}, u32[]{:S(2)}) collective-permute-start(bf16[2,64,1024]{2,1,0:T(8,128)(2,1)S(1)} %copy-done.22), channel_id=1, source_target_pairs={{0,2},{1,3},{2,0},{3,1},{4,6},{5,7},{6,4},{7,5},{8,10},{9,11},{10,... | collective-permute-start | bytes 786440 | tf_op jit(solution)/shard_map/ppermute | solution.py:953
  29.4 15.4 %collective-permute-start.3 = (bf16[2,64,1024]{2,1,0:T(8,128)(2,1)S(1)}, bf16[2,64,1024]{2,1,0:T(8,128)(2,1)S(1)}, u32[]{:S(2)}, u32[]{:S(2)}) collective-permute-start(bf16[2,64,1024]{2,1,0:T(8,128)(2,1)S(1)} %copy-done.13), channel_id=1, source_target_pairs={{0,1},{1,2},{2,3},{3,0},{4,5},{5,6},{6,7},{7,4},{8,9},{9,10},{10,1... | collective-permute-start | bytes 786440 | tf_op jit(solution)/shard_map/ppermute | solution.py:953
  30.0 21.5 %collective-permute-start.4 = (bf16[2,64,1024]{2,1,0:T(8,128)(2,1)S(1)}, bf16[2,64,1024]{2,1,0:T(8,128)(2,1)S(1)}, u32[]{:S(2)}, u32[]{:S(2)}) collective-permute-start(bf16[2,64,1024]{2,1,0:T(8,128)(2,1)S(1)} %copy-done.13), channel_id=1, source_target_pairs={{0,2},{1,3},{2,0},{3,1},{4,6},{5,7},{6,4},{7,5},{8,10},{9,11},{10,... | collective-permute-start | bytes 786440 | tf_op jit(solution)/shard_map/ppermute | solution.py:953
  34.1 17.4 %collective-permute-start.5 = (bf16[2,64,1024]{2,1,0:T(8,128)(2,1)S(1)}, bf16[2,64,1024]{2,1,0:T(8,128)(2,1)}, u32[]{:S(2)}, u32[]{:S(2)}) collective-permute-start(bf16[2,64,1024]{2,1,0:T(8,128)(2,1)S(1)} %copy-done.13), channel_id=1, source_target_pairs={{0,3},{1,0},{2,1},{3,2},{4,7},{5,4},{6,5},{7,6},{8,11},{9,8},{10,9... | collective-permute-start | bytes 786440 | tf_op jit(solution)/shard_map/ppermute | solution.py:953
  51.6 21.9 %collective-permute-start.6 = (bf16[8,400,128]{2,1,0:T(8,128)(2,1)S(1)}, bf16[8,400,128]{2,1,0:T(8,128)(2,1)S(1)}, u32[]{:S(2)}, u32[]{:S(2)}) collective-permute-start(bf16[8,400,128]{2,1,0:T(8,128)(2,1)S(1)} %constant_dynamic-slice_fusion), channel_id=1, source_target_pairs={{0,1},{1,2},{2,3},{3,0},{4,5},{5,6},{6,7},{7,4},{8,9},{9,10},{10,1... | collective-permute-start | bytes 2457608 | tf_op jit(solution)/shard_map/ppermute | solution.py:953
  53.1 20.8 %collective-permute-start.9 = (bf16[8,400,128]{2,1,0:T(8,128)(2,1)S(1)}, bf16[8,400,128]{2,1,0:T(8,128)(2,1)S(1)}, u32[]{:S(2)}, u32[]{:S(2)}) collective-permute-start(bf16[8,400,128]{2,1,0:T(8,128)(2,1)S(1)} %constant_dynamic-slice_fusion), channel_id=1, source_target_pairs={{0,3},{1,0},{2,1},{3,2},{4,7},{5,4},{6,5},{7,6},{8,11},{9,8},{10,9... | collective-permute-start | bytes 2457608 | tf_op jit(solution)/shard_map/ppermute | solution.py:953
  129.0 18.4 %collective-permute-start.17 = (bf16[64,1024]{1,0:T(8,128)(2,1)S(1)}, bf16[64,1024]{1,0:T(8,128)(2,1)S(1)}, u32[]{:S(2)}, u32[]{:S(2)}) collective-permute-start(bf16[64,1024]{1,0:T(8,128)(2,1)S(1)} %add_convert_fusion.3.refs_14_), channel_id=1, source_target_pairs={{0,64},{1,65},{2,66},{3,67},{4,68},{5,69},{6,70},{7,71},{8,72},{9,... | collective-permute-start | bytes 393224 | tf_op jit(solution)/shard_map/ppermute | solution.py:971
  130.3 17.1 %collective-permute-start.18 = (bf16[64,1024]{1,0:T(8,128)(2,1)S(1)}, bf16[64,1024]{1,0:T(8,128)(2,1)S(1)}, u32[]{:S(2)}, u32[]{:S(2)}) collective-permute-start(bf16[64,1024]{1,0:T(8,128)(2,1)S(1)} %add_convert_fusion.3.refs_14_), channel_id=1, source_target_pairs={{0,65},{1,66},{2,67},{3,64},{4,69},{5,70},{6,71},{7,68},{8,73},{9,... | collective-permute-start | bytes 393224 | tf_op jit(solution)/shard_map/ppermute | solution.py:971
  131.6 15.8 %collective-permute-start.19 = (bf16[64,1024]{1,0:T(8,128)(2,1)S(1)}, bf16[64,1024]{1,0:T(8,128)(2,1)S(1)}, u32[]{:S(2)}, u32[]{:S(2)}) collective-permute-start(bf16[64,1024]{1,0:T(8,128)(2,1)S(1)} %add_convert_fusion.3.refs_14_), channel_id=1, source_target_pairs={{0,66},{1,67},{2,64},{3,65},{4,70},{5,71},{6,68},{7,69},{8,74},{9,... | collective-permute-start | bytes 393224 | tf_op jit(solution)/shard_map/ppermute | solution.py:971
  172.2 21.0 %collective-permute-start.24 = (bf16[64,1024]{1,0:T(8,128)(2,1)S(1)}, bf16[64,1024]{1,0:T(8,128)(2,1)S(1)}, u32[]{:S(2)}, u32[]{:S(2)}) collective-permute-start(bf16[64,1024]{1,0:T(8,128)(2,1)S(1)} %add_convert_fusion.2), channel_id=1, source_target_pairs={{0,64},{1,65},{2,66},{3,67},{4,68},{5,69},{6,70},{7,71},{8,72},{9,... | collective-permute-start | bytes 393224 | tf_op jit(solution)/shard_map/ppermute | solution.py:971
  225.2 44.5 %collective-permute-start.40 = (bf16[64,1024]{1,0:T(8,128)(2,1)}, bf16[64,1024]{1,0:T(8,128)(2,1)S(1)}, u32[]{:S(2)}, u32[]{:S(2)}) collective-permute-start(bf16[64,1024]{1,0:T(8,128)(2,1)} %get-tuple-element.267), channel_id=1, source_target_pairs={{64,0},{65,1},{66,2},{67,3},{68,4},{69,5},{70,6},{71,7},{72,8},{73... | collective-permute-start | bytes 393224 | tf_op jit(solution)/shard_map/ppermute | solution.py:971
  226.5 45.2 %collective-permute-start.41 = (bf16[64,1024]{1,0:T(8,128)(2,1)}, bf16[64,1024]{1,0:T(8,128)(2,1)S(1)}, u32[]{:S(2)}, u32[]{:S(2)}) collective-permute-start(bf16[64,1024]{1,0:T(8,128)(2,1)} %get-tuple-element.267), channel_id=1, source_target_pairs={{64,1},{65,2},{66,3},{67,0},{68,5},{69,6},{70,7},{71,4},{72,9},{73... | collective-permute-start | bytes 393224 | tf_op jit(solution)/shard_map/ppermute | solution.py:971
  227.8 45.5 %collective-permute-start.42 = (bf16[64,1024]{1,0:T(8,128)(2,1)}, bf16[64,1024]{1,0:T(8,128)(2,1)S(1)}, u32[]{:S(2)}, u32[]{:S(2)}) collective-permute-start(bf16[64,1024]{1,0:T(8,128)(2,1)} %get-tuple-element.267), channel_id=1, source_target_pairs={{64,2},{65,3},{66,0},{67,1},{68,6},{69,7},{70,4},{71,5},{72,10},{7... | collective-permute-start | bytes 393224 | tf_op jit(solution)/shard_map/ppermute | solution.py:971
  229.1 44.1 %collective-permute-start.43 = (bf16[64,1024]{1,0:T(8,128)(2,1)}, bf16[64,1024]{1,0:T(8,128)(2,1)S(1)}, u32[]{:S(2)}, u32[]{:S(2)}) collective-permute-start(bf16[64,1024]{1,0:T(8,128)(2,1)} %get-tuple-element.267), channel_id=1, source_target_pairs={{64,3},{65,0},{66,1},{67,2},{68,7},{69,4},{70,5},{71,6},{72,11},{7... | collective-permute-start | bytes 393224 | tf_op jit(solution)/shard_map/ppermute | solution.py:971
  234.0 52.3 %collective-permute-start.37 = (bf16[64,1024]{1,0:T(8,128)(2,1)}, bf16[64,1024]{1,0:T(8,128)(2,1)S(1)}, u32[]{:S(2)}, u32[]{:S(2)}) collective-permute-start(bf16[64,1024]{1,0:T(8,128)(2,1)} %get-tuple-element.266.refs_1_), channel_id=1, source_target_pairs={{0,1},{1,2},{2,3},{3,0},{4,5},{5,6},{6,7},{7,4},{8,9},{9,10},{10,1... | collective-permute-start | bytes 393224 | tf_op jit(solution)/shard_map/ppermute | solution.py:953
  269.6 18.1 %collective-permute-start.38 = (bf16[64,1024]{1,0:T(8,128)(2,1)}, bf16[64,1024]{1,0:T(8,128)(2,1)S(1)}, u32[]{:S(2)}, u32[]{:S(2)}) collective-permute-start(bf16[64,1024]{1,0:T(8,128)(2,1)} %get-tuple-element.266.refs_1_), channel_id=1, source_target_pairs={{0,2},{1,3},{2,0},{3,1},{4,6},{5,7},{6,4},{7,5},{8,10},{9,11},{10,... | collective-permute-start | bytes 393224 | tf_op jit(solution)/shard_map/ppermute | solution.py:953
  271.6 16.1 %collective-permute-start.39 = (bf16[64,1024]{1,0:T(8,128)(2,1)}, bf16[64,1024]{1,0:T(8,128)(2,1)S(1)}, u32[]{:S(2)}, u32[]{:S(2)}) collective-permute-start(bf16[64,1024]{1,0:T(8,128)(2,1)} %get-tuple-element.266.refs_1_), channel_id=1, source_target_pairs={{0,3},{1,0},{2,1},{3,2},{4,7},{5,4},{6,5},{7,6},{8,11},{9,8},{10,9... | collective-permute-start | bytes 393224 | tf_op jit(solution)/shard_map/ppermute | solution.py:953
  348.6 20.4 %collective-permute-start.63 = (bf16[64,1024]{1,0:T(8,128)(2,1)}, bf16[64,1024]{1,0:T(8,128)(2,1)S(1)}, u32[]{:S(2)}, u32[]{:S(2)}) collective-permute-start(bf16[64,1024]{1,0:T(8,128)(2,1)} %get-tuple-element.303.refs_14_.refs_1_), channel_id=1, source_target_pairs={{0,1},{1,2},{2,3},{3,0},{4,5},{5,6},{6,7},{7,4},{8,9},{9,10},{10,1... | collective-permute-start | bytes 393224 | tf_op jit(solution)/shard_map/ppermute | solution.py:953
  349.4 19.5 %collective-permute-start.64 = (bf16[64,1024]{1,0:T(8,128)(2,1)}, bf16[64,1024]{1,0:T(8,128)(2,1)S(1)}, u32[]{:S(2)}, u32[]{:S(2)}) collective-permute-start(bf16[64,1024]{1,0:T(8,128)(2,1)} %get-tuple-element.303.refs_14_.refs_1_), channel_id=1, source_target_pairs={{0,2},{1,3},{2,0},{3,1},{4,6},{5,7},{6,4},{7,5},{8,10},{9,11},{10,... | collective-permute-start | bytes 393224 | tf_op jit(solution)/shard_map/ppermute | solution.py:953
  352.6 16.4 %collective-permute-start.65 = (bf16[64,1024]{1,0:T(8,128)(2,1)}, bf16[64,1024]{1,0:T(8,128)(2,1)S(1)}, u32[]{:S(2)}, u32[]{:S(2)}) collective-permute-start(bf16[64,1024]{1,0:T(8,128)(2,1)} %get-tuple-element.303.refs_14_.refs_1_), channel_id=1, source_target_pairs={{0,3},{1,0},{2,1},{3,2},{4,7},{5,4},{6,5},{7,6},{8,11},{9,8},{10,9... | collective-permute-start | bytes 393224 | tf_op jit(solution)/shard_map/ppermute | solution.py:953
  391.4 37.9 %all-to-all-start.1 = ((bf16[16,448,128]{2,1,0:T(8,128)(2,1)}), bf16[16,448,128]{2,1,0:T(8,128)(2,1)S(1)}, u32[]{:S(2)}, u32[]{:S(2)}) async-start(bf16[16,448,128]{2,1,0:T(8,128)(2,1)} %attention_weight_grads.1), calls=%async_computation.1 | async-start | bytes 3670016 | tf_op jit(solution)/shard_map/all_to_all | solution.py:1162
  (124 other events, 879.4 us)
Sparse Core Ops, SparseCore 0:
  9.8 88.8 all-gather.2
  334.9 103.5 reduce-scatter.1

commit v3 on v2

--- a/solution.py
+++ b/solution.py
@@ -1114,8 +1114,10 @@
     first_in = across(first_out, True)
     after = [first_out]
     attend(0, 1, rows_in[1])
+    after = [*after, *first_in]
+    parts = to_owner(expert(0, 1))
     late = [layer(1, 0, first_in)]
-    second_out = layer_sum(expert(0, 1), saves[0][1][5])
+    second_out = finish(parts, saves[0][1][5])
     second_in = across(second_out, True)
     expert_back(1, 0, rows_cot[0])
     late.append(layer(1, 1, second_in))

time: 457 us -> 451 us (0.987)
    unnamed x156 -> x158, local copies, waits for them, and re-layouts: 10.6 us -> 10.6 us
  transfers between devices with their start and end apart: 73 -> 73, of which waited for: 23 -> 25; matrix products, arithmetic and copies ran while one was open for 5% -> 6% of each run, Pallas kernels for 24% -> 25%
where the time goes in v3:
time: 451 us; the launch traced here: 444 us
  Pallas kernels  158 us (35%)
  waiting for transfers between devices  117 us (26%)
  starting transfers between devices  112 us (25%)
  local copies, waits for them, and re-layouts  24.7 us (5%)
  other arithmetic  16.1 us (4%)
  between operations  15.6 us (3%)
    ppermute x49, starting transfers between devices, moved(): lax.ppermute(array, 'tensor', [(i, (i + shift) % 4) for i in range(4)])  68.7 us
    ppermute x49, waiting for transfers between devices, moved(): lax.ppermute(array, 'tensor', [(i, (i + shift) % 4) for i in range(4)])  60.6 us
    ppermute x16, waiting for transfers between devices, across(): lax.ppermute(rows, ('pipe', 'tensor'), [(start + i, end + (i + s) % 4) fo...  42.9 us
    pallas_call x4, Pallas kernels, attention_backward(): pl.pallas_call(lambda *refs: attention_backward_kernel(len(after), *refs)...  38.3 us
    pallas_call x4, Pallas kernels, experts_backward(): pl.pallas_call(lambda *refs: experts_backward_kernel(len(after), *refs),...  31.7 us
    ppermute x16, starting transfers between devices, across(): lax.ppermute(rows, ('pipe', 'tensor'), [(start + i, end + (i + s) % 4) fo...  30.4 us
    pallas_call x2, Pallas kernels, attention_forward(): pl.pallas_call(lambda *refs: attention_forward_kernel(len(after), *refs),...  26.2 us
    pallas_call x2, Pallas kernels, experts_forward(): pl.pallas_call(lambda *refs: experts_forward_kernel(len(after), *refs), g...  17.4 us
  transfers between devices with their start and end apart: 73, of which 25 were waited for; matrix products, arithmetic and copies ran while one was open for 6% of the time, Pallas kernels for 25%

profile of v3, /device:TPU:0, one launch (start us, length us, event | category | flops | bytes accessed | tf_op | source)
XLA Modules:
  0.0 443.6 jit_solution(3289668895644073942)
XLA Ops:
  11.2 6.0 %all-to-all-start = ((bf16[16,400,128]{2,1,0:T(8,128)(2,1)}), bf16[16,400,128]{2,1,0:T(8,128)(2,1)S(1)}, u32[]{:S(2)}, u32[]{:S(2)}) async-start(bf16[16,400,128]{2,1,0:T(8,128)(2,1)} %broadcast_in_dim.76), calls=%async_computation | async-start | bytes 3276800 | tf_op jit(solution)/shard_map/all_to_all | solution.py:1027
  40.8 4.1 collective-permute-done.3
  44.9 6.6 %collective-permute-done.4 = bf16[2,64,1024]{2,1,0:T(8,128)(2,1)S(1)} collective-permute-done((bf16[2,64,1024]{2,1,0:T(8,128)(2,1)S(1)}, bf16[2,64,1024]{2,1,0:T(8,128)(2,1)S(1)}, u32[]{:S(2)}, u32[]{:S(2)}) %collective-permute-start.4) | collective-permute-done | bytes 262176 | tf_op jit(solution)/shard_map/ppermute | solution.py:953
  58.8 14.8 %collective-permute-done.6.refs_1_.refs_6_ = bf16[8,400,128]{2,1,0:T(8,128)(2,1)S(1)} collective-permute-done((bf16[8,400,128]{2,1,0:T(8,128)(2,1)S(1)}, bf16[8,400,128]{2,1,0:T(8,128)(2,1)S(1)}, u32[]{:S(2)}, u32[]{:S(2)}) %collective-permute-start.6) | collective-permute-done | bytes 819232 | tf_op jit(solution)/shard_map/ppermute | solution.py:953
  79.0 7.5 %collective-permute-done.8.refs_3_.refs_8_ = bf16[4,400,128]{2,1,0:T(8,128)(2,1)S(1)} collective-permute-done((bf16[4,400,128]{2,1,0:T(8,128)(2,1)S(1)}, bf16[4,400,128]{2,1,0:T(8,128)(2,1)S(1)}, u32[]{:S(2)}, u32[]{:S(2)}) %collective-permute-start.8) | collective-permute-done | bytes 409632 | tf_op jit(solution)/shard_map/ppermute | solution.py:953
  93.6 13.1 %attention_forward.2 = (bf16[256,1024]{1,0:T(8,128)(2,1)}, bf16[64,1024]{1,0:T(8,128)(2,1)}, bf16[4,256,512]{2,1,0:T(8,128)(2,1)}, bf16[256,256]{1,0:T(8,128)(2,...) custom-call(s32[3]{0:T(128)} %add_add_fusion.sref.refs_0_, ...), custom_call_target="tpu_custom_call" | custom-call | flops 1879048192 | bytes 9437184 | tf_op jit(solution)/shard_map/attention_forward/pallas_call | solution.py:272
  106.7 8.7 %experts_forward.2 = (bf16[64,1024]{1,0:T(8,128)(2,1)}, bf16[64,1024]{1,0:T(8,128)(2,1)}, bf16[64,1024]{1,0:T(8,128)(2,1)}, bf16[64,1024]{1,0:T(8,128)(2,1)}, bf16[16,256,256]{2,1,0:T(8,128)(2,1)}) custom-call(s32[3]{0:T(128)} %add_add_fusion.sref.refs_0_, bf16[256,1024]{1,0:T(8,128)(2,1)} %get-tuple-element.204.refs_1_.refs_2_.refs_9_, ...), custom_call_target="tpu_custom_call" | custom-call | flops 3221225472 | bytes 14680064 | tf_op jit(solution)/shard_map/experts_forward/pallas_call | solution.py:415
  120.4 4.4 collective-permute-done.16
  134.3 13.1 %attention_forward.3 = (bf16[256,1024]{1,0:T(8,128)(2,1)}, bf16[64,1024]{1,0:T(8,128)(2,1)}, bf16[4,256,512]{2,1,0:T(8,128)(2,1)}, bf16[256,256]{1,0:T(8,128)(2,...) custom-call(s32[3]{0:T(128)} %add_add_fusion.sref.refs_0_, ...), custom_call_target="tpu_custom_call" | custom-call | flops 1879048192 | bytes 9437184 | tf_op jit(solution)/shard_map/attention_forward/pallas_call | solution.py:272
  148.2 8.6 %experts_forward.3 = (bf16[64,1024]{1,0:T(8,128)(2,1)}, bf16[64,1024]{1,0:T(8,128)(2,1)}, bf16[64,1024]{1,0:T(8,128)(2,1)}, bf16[64,1024]{1,0:T(8,128)(2,1)}, bf16[16,256,256]{2,1,0:T(8,128)(2,1)}) custom-call(s32[3]{0:T(128)} %add_add_fusion.sref.refs_0_, bf16[256,1024]{1,0:T(8,128)(2,1)} %get-tuple-element.217.refs_1_.refs_6_.refs_3_.refs_9_, ...), custom_call_target="tpu_custom_call" | custom-call | flops 3221225472 | bytes 14680064 | tf_op jit(solution)/shard_map/experts_forward/pallas_call | solution.py:415
  158.9 4.6 %layer_forward.2 = (bf16[256,1024]{1,0:T(8,128)(2,1)}, bf16[64,1024]{1,0:T(8,128)(2,1)}, bf16[4,256,512]{2,1,0:T(8,128)(2,1)}, bf16[256,256]{1,0:T(8,128)(2,1)},...) custom-call(s32[3]{0:T(128)} %add_add_fusion.1.refs_0_, ...), custom_call_target="tpu_custom_call" | custom-call | flops 5100273664 | bytes 23068672 | tf_op jit(solution)/shard_map/layer_forward/pallas_call | solution.py:525
  166.9 7.5 %collective-permute-start.24 = (bf16[64,1024]{1,0:T(8,128)(2,1)S(1)}, bf16[64,1024]{1,0:T(8,128)(2,1)S(1)}, u32[]{:S(2)}, u32[]{:S(2)}) collective-permute-start(bf16[64,1024]{1,0:T(8,128)(2,1)S(1)} %add_convert_fusion.2), channel_id=1, source_target_pairs={{0,64},{1,65},{2,66},{3,67},{4,68},{5,69},{6,70},{7,71},{8,72},{9,... | collective-permute-start | bytes 393224 | tf_op jit(solution)/shard_map/ppermute | solution.py:971
  181.7 5.4 %experts_backward.4 = (bf16[64,1152]{1,0:T(8,128)(2,1)}, bf16[64,1152]{1,0:T(8,128)(2,1)}, bf16[64,1152]{1,0:T(8,128)(2,1)}, bf16[64,1152]{1,0:T(8,128)(2,1)}, b...) custom-call(s32[3]{0:T(128)} %add_add_fusion.1.refs_0_, ...), custom_call_target="tpu_custom_call" | custom-call | flops 3221225472 | bytes 17825792 | tf_op jit(solution)/shard_map/experts_backward/pallas_call | solution.py:629
  204.8 5.4 %experts_backward.5 = (bf16[64,1152]{1,0:T(8,128)(2,1)}, bf16[64,1152]{1,0:T(8,128)(2,1)}, bf16[64,1152]{1,0:T(8,128)(2,1)}, bf16[64,1152]{1,0:T(8,128)(2,1)}, b...) custom-call(s32[3]{0:T(128)} %add_add_fusion.1.refs_0_, ...), custom_call_target="tpu_custom_call" | custom-call | flops 3221225472 | bytes 17825792 | tf_op jit(solution)/shard_map/experts_backward/pallas_call | solution.py:629
  228.1 35.1 %collective-permute-done.40.refs_2_.refs_6_ = bf16[64,1024]{1,0:T(8,128)(2,1)S(1)} collective-permute-done((bf16[64,1024]{1,0:T(8,128)(2,1)}, bf16[64,1024]{1,0:T(8,128)(2,1)S(1)}, u32[]{:S(2)}, u32[]{:S(2)}) %collective-permute-start.40) | collective-permute-done | bytes 131104 | tf_op jit(solution)/shard_map/ppermute | solution.py:971
  267.6 10.5 %experts_backward.6 = (bf16[64,1152]{1,0:T(8,128)(2,1)}, bf16[64,1152]{1,0:T(8,128)(2,1)}, bf16[64,1152]{1,0:T(8,128)(2,1)}, bf16[64,1152]{1,0:T(8,128)(2,1)}, b...) custom-call(s32[3]{0:T(128)} %add_add_fusion.sref.refs_0_, ...), custom_call_target="tpu_custom_call" | custom-call | flops 3221225472 | bytes 17825792 | tf_op jit(solution)/shard_map/experts_backward/pallas_call | solution.py:629
  295.2 4.9 %collective-permute-done.56.refs_2_.refs_6_ = bf16[64,1024]{1,0:T(8,128)(2,1)S(1)} collective-permute-done((bf16[64,1024]{1,0:T(8,128)(2,1)}, bf16[64,1024]{1,0:T(8,128)(2,1)S(1)}, u32[]{:S(2)}, u32[]{:S(2)}) %collective-permute-start.56) | collective-permute-done | bytes 131104 | tf_op jit(solution)/shard_map/ppermute | solution.py:971
  303.7 10.4 %experts_backward.7 = (bf16[64,1152]{1,0:T(8,128)(2,1)}, bf16[64,1152]{1,0:T(8,128)(2,1)}, bf16[64,1152]{1,0:T(8,128)(2,1)}, bf16[64,1152]{1,0:T(8,128)(2,1)}, b...) custom-call(s32[3]{0:T(128)} %add_add_fusion.sref.refs_0_, ...), custom_call_target="tpu_custom_call" | custom-call | flops 3221225472 | bytes 17825792 | tf_op jit(solution)/shard_map/experts_backward/pallas_call | solution.py:629
  314.0 14.4 %expert_weight_grads.1.refs_1_ = bf16[16,3,16,64,128]{4,3,2,1,0:T(8,128)(2,1)} custom-call(s32[3]{0:T(128)} %add_add_fusion.sref.refs_0_, bf16[256,1024]{1,0:T(8,128)(2,1)} %get-tuple-element.290.refs_1_.refs_7_, bf16[256,1024]{1,0:T(8,128)(2,1)} %get-tuple-element.204.refs_1_.refs_2_.refs_9_, ...), custom_call_target="tpu_custom_call" | custom-call | flops 6442450944 | bytes 18874368 | tf_op jit(solution)/shard_map/expert_weight_grads/pallas_call | solution.py:881
  347.9 15.5 %attention_backward.6 = (f32[64,1024]{1,0:T(8,128)}, bf16[64,1024]{1,0:T(8,128)(2,1)}, f32[24,1024]{1,0:T(8,128)}, bf16[256,1024]{1,0:T(8,128)(2,1)}, bf16[256,512]{1,0:T(8,128)(2,1)}) custom-call(s32[3]{0:T(128)} %add_add_fusion.sref.refs_0_, bf16[64,1024]{1,0:T(8,128)(2,1)} %get-tuple-element.288.refs_1_, bf16[64,1024]{1,0:T(8,128)(2,1)} %copy-done.41, ...), custom_call_target="tpu_custom_call" | custom-call | flops 1207959552 | bytes 9437184 | tf_op jit(solution)/shard_map/attention_backward/pallas_call | solution.py:808
  364.1 15.6 %attention_backward.7 = (f32[64,1024]{1,0:T(8,128)}, bf16[64,1024]{1,0:T(8,128)(2,1)}, f32[24,1024]{1,0:T(8,128)}, bf16[256,1024]{1,0:T(8,128)(2,1)}, bf16[256,512]{1,0:T(8,128)(2,1)}) custom-call(s32[3]{0:T(128)} %add_add_fusion.sref.refs_0_, bf16[64,1024]{1,0:T(8,128)(2,1)} %get-tuple-element.303.refs_14_.refs_1_, bf16[64,1024]{1,0:T(8,128)(2,1)} %copy-done.40, ...), custom_call_target="tpu_custom_call" | custom-call | flops 1207959552 | bytes 9437184 | tf_op jit(solution)/shard_map/attention_backward/pallas_call | solution.py:808
  379.8 6.1 %attention_weight_grads.1 = bf16[16,448,128]{2,1,0:T(8,128)(2,1)} custom-call(s32[3]{0:T(128)} %add_add_fusion.sref.refs_0_, bf16[256,1024]{1,0:T(8,128)(2,1)} %get-tuple-element.316.refs_0_, bf16[256,1024]{1,0:T(8,128)(2,1)} %get-tuple-element.317.refs_1_, bf16[256,1024]{1,0:T(8,128)(2,1)} %get-tuple-element.318.refs_2_, ...), custom_call_target="tpu_custom_call" | custom-call | flops 805306368 | bytes 5242880 | tf_op jit(solution)/shard_map/attention_weight_grads/pallas_call | solution.py:933
  385.9 5.8 %all-to-all-start.1 = ((bf16[16,448,128]{2,1,0:T(8,128)(2,1)}), bf16[16,448,128]{2,1,0:T(8,128)(2,1)S(1)}, u32[]{:S(2)}, u32[]{:S(2)}) async-start(bf16[16,448,128]{2,1,0:T(8,128)(2,1)} %attention_weight_grads.1), calls=%async_computation.1 | async-start | bytes 3670016 | tf_op jit(solution)/shard_map/all_to_all | solution.py:1164
  410.1 13.6 %all-to-all-done.1 = bf16[16,448,128]{2,1,0:T(8,128)(2,1)S(1)} async-done(((bf16[16,448,128]{2,1,0:T(8,128)(2,1)}), bf16[16,448,128]{2,1,0:T(8,128)(2,1)S(1)}, u32[]{:S(2)}, u32[]{:S(2)}) %all-to-all-start.1) | async-done | bytes 1835040 | tf_op jit(solution)/shard_map/all_to_all | solution.py:1164
  (358 shorter events, 186.3 us)
Async XLA Ops:
  7.3 99.5 %all-gather.3.cloned.1.call-start = ((), (), s32[]{:S(2)}) async-start(), calls=%async_computation.4 | async-start | bytes 13369344 | tf_op jit(solution)/shard_map/all_gather | solution.py:1029
  11.2 40.4 %all-to-all-start = ((bf16[16,400,128]{2,1,0:T(8,128)(2,1)}), bf16[16,400,128]{2,1,0:T(8,128)(2,1)S(1)}, u32[]{:S(2)}, u32[]{:S(2)}) async-start(bf16[16,400,128]{2,1,0:T(8,128)(2,1)} %broadcast_in_dim.76), calls=%async_computation | async-start | bytes 3276800 | tf_op jit(solution)/shard_map/all_to_all | solution.py:1027
  17.3 416.7 %reduce-scatter.2.cloned.1.call-start = ((), (), s32[]{:S(2)}) async-start(), calls=%async_computation.3 | async-start | bytes 13369344 | tf_op jit(solution)/shard_map/reduce_scatter | solution.py:1142
  25.3 15.5 %collective-permute-start.1 = (bf16[2,64,1024]{2,1,0:T(8,128)(2,1)S(1)}, bf16[2,64,1024]{2,1,0:T(8,128)(2,1)S(1)}, u32[]{:S(2)}, u32[]{:S(2)}) collective-permute-start(bf16[2,64,1024]{2,1,0:T(8,128)(2,1)S(1)} %copy-done.26), channel_id=1, source_target_pairs={{0,2},{1,3},{2,0},{3,1},{4,6},{5,7},{6,4},{7,5},{8,10},{9,11},{10,... | collective-permute-start | bytes 786440 | tf_op jit(solution)/shard_map/ppermute | solution.py:953
  29.5 15.4 %collective-permute-start.3 = (bf16[2,64,1024]{2,1,0:T(8,128)(2,1)S(1)}, bf16[2,64,1024]{2,1,0:T(8,128)(2,1)S(1)}, u32[]{:S(2)}, u32[]{:S(2)}) collective-permute-start(bf16[2,64,1024]{2,1,0:T(8,128)(2,1)S(1)} %copy-done.13), channel_id=1, source_target_pairs={{0,1},{1,2},{2,3},{3,0},{4,5},{5,6},{6,7},{7,4},{8,9},{9,10},{10,1... | collective-permute-start | bytes 786440 | tf_op jit(solution)/shard_map/ppermute | solution.py:953
  30.1 21.5 %collective-permute-start.4 = (bf16[2,64,1024]{2,1,0:T(8,128)(2,1)S(1)}, bf16[2,64,1024]{2,1,0:T(8,128)(2,1)S(1)}, u32[]{:S(2)}, u32[]{:S(2)}) collective-permute-start(bf16[2,64,1024]{2,1,0:T(8,128)(2,1)S(1)} %copy-done.13), channel_id=1, source_target_pairs={{0,2},{1,3},{2,0},{3,1},{4,6},{5,7},{6,4},{7,5},{8,10},{9,11},{10,... | collective-permute-start | bytes 786440 | tf_op jit(solution)/shard_map/ppermute | solution.py:953
  34.1 17.4 %collective-permute-start.5 = (bf16[2,64,1024]{2,1,0:T(8,128)(2,1)S(1)}, bf16[2,64,1024]{2,1,0:T(8,128)(2,1)}, u32[]{:S(2)}, u32[]{:S(2)}) collective-permute-start(bf16[2,64,1024]{2,1,0:T(8,128)(2,1)S(1)} %copy-done.13), channel_id=1, source_target_pairs={{0,3},{1,0},{2,1},{3,2},{4,7},{5,4},{6,5},{7,6},{8,11},{9,8},{10,9... | collective-permute-start | bytes 786440 | tf_op jit(solution)/shard_map/ppermute | solution.py:953
  51.6 21.9 %collective-permute-start.6 = (bf16[8,400,128]{2,1,0:T(8,128)(2,1)S(1)}, bf16[8,400,128]{2,1,0:T(8,128)(2,1)S(1)}, u32[]{:S(2)}, u32[]{:S(2)}) collective-permute-start(bf16[8,400,128]{2,1,0:T(8,128)(2,1)S(1)} %constant_dynamic-slice_fusion), channel_id=1, source_target_pairs={{0,1},{1,2},{2,3},{3,0},{4,5},{5,6},{6,7},{7,4},{8,9},{9,10},{10,1... | collective-permute-start | bytes 2457608 | tf_op jit(solution)/shard_map/ppermute | solution.py:953
  53.1 20.8 %collective-permute-start.9 = (bf16[8,400,128]{2,1,0:T(8,128)(2,1)S(1)}, bf16[8,400,128]{2,1,0:T(8,128)(2,1)S(1)}, u32[]{:S(2)}, u32[]{:S(2)}) collective-permute-start(bf16[8,400,128]{2,1,0:T(8,128)(2,1)S(1)} %constant_dynamic-slice_fusion), channel_id=1, source_target_pairs={{0,3},{1,0},{2,1},{3,2},{4,7},{5,4},{6,5},{7,6},{8,11},{9,8},{10,9... | collective-permute-start | bytes 2457608 | tf_op jit(solution)/shard_map/ppermute | solution.py:953
  129.1 18.4 %collective-permute-start.17 = (bf16[64,1024]{1,0:T(8,128)(2,1)S(1)}, bf16[64,1024]{1,0:T(8,128)(2,1)S(1)}, u32[]{:S(2)}, u32[]{:S(2)}) collective-permute-start(bf16[64,1024]{1,0:T(8,128)(2,1)S(1)} %add_convert_fusion.3.refs_14_), channel_id=1, source_target_pairs={{0,64},{1,65},{2,66},{3,67},{4,68},{5,69},{6,70},{7,71},{8,72},{9,... | collective-permute-start | bytes 393224 | tf_op jit(solution)/shard_map/ppermute | solution.py:971
  130.4 17.1 %collective-permute-start.18 = (bf16[64,1024]{1,0:T(8,128)(2,1)S(1)}, bf16[64,1024]{1,0:T(8,128)(2,1)S(1)}, u32[]{:S(2)}, u32[]{:S(2)}) collective-permute-start(bf16[64,1024]{1,0:T(8,128)(2,1)S(1)} %add_convert_fusion.3.refs_14_), channel_id=1, source_target_pairs={{0,65},{1,66},{2,67},{3,64},{4,69},{5,70},{6,71},{7,68},{8,73},{9,... | collective-permute-start | bytes 393224 | tf_op jit(solution)/shard_map/ppermute | solution.py:971
  131.7 15.8 %collective-permute-start.19 = (bf16[64,1024]{1,0:T(8,128)(2,1)S(1)}, bf16[64,1024]{1,0:T(8,128)(2,1)S(1)}, u32[]{:S(2)}, u32[]{:S(2)}) collective-permute-start(bf16[64,1024]{1,0:T(8,128)(2,1)S(1)} %add_convert_fusion.3.refs_14_), channel_id=1, source_target_pairs={{0,66},{1,67},{2,64},{3,65},{4,70},{5,71},{6,68},{7,69},{8,74},{9,... | collective-permute-start | bytes 393224 | tf_op jit(solution)/shard_map/ppermute | solution.py:971
  166.9 20.2 %collective-permute-start.24 = (bf16[64,1024]{1,0:T(8,128)(2,1)S(1)}, bf16[64,1024]{1,0:T(8,128)(2,1)S(1)}, u32[]{:S(2)}, u32[]{:S(2)}) collective-permute-start(bf16[64,1024]{1,0:T(8,128)(2,1)S(1)} %add_convert_fusion.2), channel_id=1, source_target_pairs={{0,64},{1,65},{2,66},{3,67},{4,68},{5,69},{6,70},{7,71},{8,72},{9,... | collective-permute-start | bytes 393224 | tf_op jit(solution)/shard_map/ppermute | solution.py:971
  218.8 44.4 %collective-permute-start.40 = (bf16[64,1024]{1,0:T(8,128)(2,1)}, bf16[64,1024]{1,0:T(8,128)(2,1)S(1)}, u32[]{:S(2)}, u32[]{:S(2)}) collective-permute-start(bf16[64,1024]{1,0:T(8,128)(2,1)} %get-tuple-element.267), channel_id=1, source_target_pairs={{64,0},{65,1},{66,2},{67,3},{68,4},{69,5},{70,6},{71,7},{72,8},{73... | collective-permute-start | bytes 393224 | tf_op jit(solution)/shard_map/ppermute | solution.py:971
  220.1 45.3 %collective-permute-start.41 = (bf16[64,1024]{1,0:T(8,128)(2,1)}, bf16[64,1024]{1,0:T(8,128)(2,1)S(1)}, u32[]{:S(2)}, u32[]{:S(2)}) collective-permute-start(bf16[64,1024]{1,0:T(8,128)(2,1)} %get-tuple-element.267), channel_id=1, source_target_pairs={{64,1},{65,2},{66,3},{67,0},{68,5},{69,6},{70,7},{71,4},{72,9},{73... | collective-permute-start | bytes 393224 | tf_op jit(solution)/shard_map/ppermute | solution.py:971
  221.4 45.5 %collective-permute-start.42 = (bf16[64,1024]{1,0:T(8,128)(2,1)}, bf16[64,1024]{1,0:T(8,128)(2,1)S(1)}, u32[]{:S(2)}, u32[]{:S(2)}) collective-permute-start(bf16[64,1024]{1,0:T(8,128)(2,1)} %get-tuple-element.267), channel_id=1, source_target_pairs={{64,2},{65,3},{66,0},{67,1},{68,6},{69,7},{70,4},{71,5},{72,10},{7... | collective-permute-start | bytes 393224 | tf_op jit(solution)/shard_map/ppermute | solution.py:971
  222.7 44.2 %collective-permute-start.43 = (bf16[64,1024]{1,0:T(8,128)(2,1)}, bf16[64,1024]{1,0:T(8,128)(2,1)S(1)}, u32[]{:S(2)}, u32[]{:S(2)}) collective-permute-start(bf16[64,1024]{1,0:T(8,128)(2,1)} %get-tuple-element.267), channel_id=1, source_target_pairs={{64,3},{65,0},{66,1},{67,2},{68,7},{69,4},{70,5},{71,6},{72,11},{7... | collective-permute-start | bytes 393224 | tf_op jit(solution)/shard_map/ppermute | solution.py:971
  227.6 52.2 %collective-permute-start.37 = (bf16[64,1024]{1,0:T(8,128)(2,1)}, bf16[64,1024]{1,0:T(8,128)(2,1)S(1)}, u32[]{:S(2)}, u32[]{:S(2)}) collective-permute-start(bf16[64,1024]{1,0:T(8,128)(2,1)} %get-tuple-element.266.refs_1_), channel_id=1, source_target_pairs={{0,1},{1,2},{2,3},{3,0},{4,5},{5,6},{6,7},{7,4},{8,9},{9,10},{10,1... | collective-permute-start | bytes 393224 | tf_op jit(solution)/shard_map/ppermute | solution.py:953
  263.1 18.3 %collective-permute-start.38 = (bf16[64,1024]{1,0:T(8,128)(2,1)}, bf16[64,1024]{1,0:T(8,128)(2,1)S(1)}, u32[]{:S(2)}, u32[]{:S(2)}) collective-permute-start(bf16[64,1024]{1,0:T(8,128)(2,1)} %get-tuple-element.266.refs_1_), channel_id=1, source_target_pairs={{0,2},{1,3},{2,0},{3,1},{4,6},{5,7},{6,4},{7,5},{8,10},{9,11},{10,... | collective-permute-start | bytes 393224 | tf_op jit(solution)/shard_map/ppermute | solution.py:953
  265.3 16.0 %collective-permute-start.39 = (bf16[64,1024]{1,0:T(8,128)(2,1)}, bf16[64,1024]{1,0:T(8,128)(2,1)S(1)}, u32[]{:S(2)}, u32[]{:S(2)}) collective-permute-start(bf16[64,1024]{1,0:T(8,128)(2,1)} %get-tuple-element.266.refs_1_), channel_id=1, source_target_pairs={{0,3},{1,0},{2,1},{3,2},{4,7},{5,4},{6,5},{7,6},{8,11},{9,8},{10,9... | collective-permute-start | bytes 393224 | tf_op jit(solution)/shard_map/ppermute | solution.py:953
  342.5 20.8 %collective-permute-start.63 = (bf16[64,1024]{1,0:T(8,128)(2,1)}, bf16[64,1024]{1,0:T(8,128)(2,1)S(1)}, u32[]{:S(2)}, u32[]{:S(2)}) collective-permute-start(bf16[64,1024]{1,0:T(8,128)(2,1)} %get-tuple-element.303.refs_14_.refs_1_), channel_id=1, source_target_pairs={{0,1},{1,2},{2,3},{3,0},{4,5},{5,6},{6,7},{7,4},{8,9},{9,10},{10,1... | collective-permute-start | bytes 393224 | tf_op jit(solution)/shard_map/ppermute | solution.py:953
  343.8 19.5 %collective-permute-start.64 = (bf16[64,1024]{1,0:T(8,128)(2,1)}, bf16[64,1024]{1,0:T(8,128)(2,1)S(1)}, u32[]{:S(2)}, u32[]{:S(2)}) collective-permute-start(bf16[64,1024]{1,0:T(8,128)(2,1)} %get-tuple-element.303.refs_14_.refs_1_), channel_id=1, source_target_pairs={{0,2},{1,3},{2,0},{3,1},{4,6},{5,7},{6,4},{7,5},{8,10},{9,11},{10,... | collective-permute-start | bytes 393224 | tf_op jit(solution)/shard_map/ppermute | solution.py:953
  346.3 17.0 %collective-permute-start.65 = (bf16[64,1024]{1,0:T(8,128)(2,1)}, bf16[64,1024]{1,0:T(8,128)(2,1)S(1)}, u32[]{:S(2)}, u32[]{:S(2)}) collective-permute-start(bf16[64,1024]{1,0:T(8,128)(2,1)} %get-tuple-element.303.refs_14_.refs_1_), channel_id=1, source_target_pairs={{0,3},{1,0},{2,1},{3,2},{4,7},{5,4},{6,5},{7,6},{8,11},{9,8},{10,9... | collective-permute-start | bytes 393224 | tf_op jit(solution)/shard_map/ppermute | solution.py:953
  385.9 37.8 %all-to-all-start.1 = ((bf16[16,448,128]{2,1,0:T(8,128)(2,1)}), bf16[16,448,128]{2,1,0:T(8,128)(2,1)S(1)}, u32[]{:S(2)}, u32[]{:S(2)}) async-start(bf16[16,448,128]{2,1,0:T(8,128)(2,1)} %attention_weight_grads.1), calls=%async_computation.1 | async-start | bytes 3670016 | tf_op jit(solution)/shard_map/all_to_all | solution.py:1164
  (125 other events, 873.3 us)
Sparse Core Ops, SparseCore 0:
  9.8 88.8 all-gather.2
  328.7 104.1 reduce-scatter.1
